TPU v7x, 512 devices: a whole 4x8x8 slice. The times are simulated.
512 devices in a mesh: dp: 64 (over z, x, core), tensor: 8 (over y).
Axes of the slice: x: 4, y: 8, z: 8, core: 2. Of those that a mesh axis runs over, the one named last changes fastest.
Arguments:
- head_inputs: bfloat16 [64, 3, 1025, 2048], P('dp', None, None, 'tensor'), may hold values from -6 to 6
- out_weight: bfloat16 [3200, 2048], P('dp', 'tensor'), may hold values from -0.109375 to 0.109375
- sequence_gradient: bfloat16 [4, 32768, 3200], P(None, 'dp', 'tensor'), may hold values from -16 to 16
- slot_labels: int32 [64, 32], P('dp'), may hold values from -1 to 1023, as said below
Outputs:
- head_gradient: bfloat16 [64, 3, 1025, 2048], P('dp', None, None, 'tensor')
- weight_gradient: float32 [3200, 2048], P('dp', 'tensor')
Inputs may be any that keep to these rules, and one draw needn't show every extreme that they name: `slot_labels`: entry (g, s) labels slot s of shard g: -1 where the slot holds no tile's piece, else t * 16 + i for piece i of tile t. Each of the 1024 pieces appears exactly once; the 16 pieces of one tile lie in 16 different shards; a shard holds at most 32 pieces, and some shard holds exactly 32.
All inputs are finite; a program needn't handle non-finite values.
Results may differ from a plain program's by a relative error of at most 0.019.
Values may be sent and summed in bfloat16 or wider, within the bound.
No kernel may reach another device: no remote copies, remote signals or barrier semaphores. Data moves between devices by JAX's collectives and lax.ppermute only.
A program may use at most 128 MiB of HBM per device.

v0:
```python
import math

import jax
import jax.numpy as jnp
from jax import lax
from jax.sharding import PartitionSpec as P

HD = 128
GRID = 32
PIECE = 16
SHUF = 256
NPIECE = 16


def shuffle_order(patch_rows):
    half_grid = GRID // 2
    width = patch_rows.shape[-1]
    phased = patch_rows.reshape(half_grid, 2, half_grid, 2, width).transpose(1, 3, 0, 2, 4)
    return phased.reshape(4, SHUF, width)


def patch_order(shuffled):
    half_grid = GRID // 2
    width = shuffled.shape[-1]
    phased = shuffled.reshape(2, 2, half_grid, half_grid, width).transpose(2, 0, 3, 1, 4)
    return phased.reshape(GRID * GRID, width)


def first_contract(left, right):
    return lax.dot_general(
        left, right, (((0,), (0,)), ((), ())), preferred_element_type=jnp.float32
    )


def last_contract(left, right):
    return lax.dot_general(
        left, right, (((1,), (1,)), ((), ())), preferred_element_type=jnp.float32
    )


def per_device(head_inputs, out_weight, sequence_gradient, slot_labels):
    peers = lax.axis_size("dp")
    width_local = sequence_gradient.shape[2]
    slot_count = slot_labels.shape[1]
    labels = slot_labels[0]
    owners = jnp.where(labels >= 0, labels // NPIECE, -1)
    destinations = jnp.arange(peers, dtype=jnp.int32)
    chosen = owners[None, :] == destinations[:, None]
    slot_rows = sequence_gradient.reshape(4, slot_count, PIECE * width_local)
    outgoing = jnp.einsum(
        "ds,ksw->dkw", chosen.astype(jnp.bfloat16), slot_rows, preferred_element_type=jnp.float32
    ).astype(jnp.bfloat16)
    piece_sums = jnp.sum(jnp.where(chosen, (labels % NPIECE)[None, :], 0), axis=1)
    piece_ids = jnp.where(jnp.any(chosen, axis=1), piece_sums, -1)
    piece_range = jnp.arange(NPIECE, dtype=jnp.int32)
    incoming, arrived_ids = (
        lax.all_to_all(outgoing, "dp", split_axis=0, concat_axis=0, tiled=True),
        lax.all_to_all(piece_ids[:, None], "dp", split_axis=0, concat_axis=0, tiled=True),
    )
    placing = (arrived_ids[:, 0][None, :] == piece_range[:, None]).astype(jnp.bfloat16)
    local_rows = jnp.einsum(
        "np,pkw->knw", placing, incoming, preferred_element_type=jnp.float32
    ).astype(jnp.bfloat16)
    local_rows = local_rows.reshape(4, SHUF, width_local)
    weight_full = lax.all_gather(out_weight, "dp", axis=0, tiled=True)
    score_scale = HD ** (-0.5)
    head_width = head_inputs.shape[3]
    head_count = head_width // HD
    query_all = head_inputs[0, 0]
    key_all = head_inputs[0, 1]
    value_all = head_inputs[0, 2]
    stored_probs = []
    attended_parts = []
    for head_index in range(head_count):
        lower = head_index * HD
        query_rows = query_all[:, lower : lower + HD]
        key_rows = key_all[:, lower : lower + HD]
        value_rows = value_all[:, lower : lower + HD]
        scores = last_contract(query_rows, key_rows) * score_scale
        shifted = jnp.exp(scores - jnp.max(scores, axis=1, keepdims=True))
        probs = shifted / jnp.sum(shifted, axis=1, keepdims=True)
        attended = jnp.dot(
            probs.astype(jnp.bfloat16), value_rows, preferred_element_type=jnp.float32
        ).astype(jnp.bfloat16)
        stored_probs.append(probs)
        attended_parts.append(attended)
    attended_all = jnp.concatenate(attended_parts, axis=1)
    shuffled_out = shuffle_order(attended_all[1:])
    features = lax.all_gather(local_rows, "tensor", axis=2, tiled=True)
    grad_total = jnp.einsum(
        "krf,fh->krh", features, weight_full, preferred_element_type=jnp.float32
    )
    out_grad = jnp.concatenate(
        [jnp.zeros((1, head_width), jnp.bfloat16), patch_order(grad_total.astype(jnp.bfloat16))],
        axis=0,
    )
    query_parts = []
    key_parts = []
    value_parts = []
    for head_index in range(head_count):
        lower = head_index * HD
        query_rows = query_all[:, lower : lower + HD]
        key_rows = key_all[:, lower : lower + HD]
        value_rows = value_all[:, lower : lower + HD]
        grad_rows = out_grad[:, lower : lower + HD]
        probs = stored_probs[head_index]
        probs_low = probs.astype(jnp.bfloat16)
        prob_grad = last_contract(grad_rows, value_rows)
        row_delta = jnp.sum(
            grad_rows.astype(jnp.float32) * attended_parts[head_index].astype(jnp.float32),
            axis=1,
            keepdims=True,
        )
        score_grad = (probs * (prob_grad - row_delta)).astype(jnp.bfloat16)
        query_parts.append(
            (
                jnp.dot(score_grad, key_rows, preferred_element_type=jnp.float32) * score_scale
            ).astype(jnp.bfloat16)
        )
        key_parts.append(
            (first_contract(score_grad, query_rows) * score_scale).astype(jnp.bfloat16)
        )
        value_parts.append(first_contract(probs_low, grad_rows).astype(jnp.bfloat16))
    head_gradient = jnp.stack(
        [
            jnp.concatenate(query_parts, axis=1),
            jnp.concatenate(key_parts, axis=1),
            jnp.concatenate(value_parts, axis=1),
        ]
    )[None]
    summed = lax.psum_scatter(
        jnp.einsum("krf,krh->fh", features, shuffled_out, preferred_element_type=jnp.float32),
        "dp",
        scatter_dimension=0,
        tiled=True,
    )
    weight_gradient = summed * (1.0 / math.sqrt(peers * GRID * GRID))
    return (head_gradient, weight_gradient)


def solution(mesh):
    placed = (
        P("dp", None, None, "tensor"),
        P("dp", "tensor"),
        P(None, "dp", "tensor"),
        P("dp", None),
    )
    return jax.shard_map(
        per_device,
        mesh=mesh,
        in_specs=placed,
        out_specs=(P("dp", None, None, "tensor"), P("dp", "tensor")),
        check_vma=False,
    )
```

profile of v0, /device:TPU:1, one launch (start us, length us, event | category | flops | bytes accessed | tf_op | source)
XLA Modules:
  0.0 392.0 jit_solution(14757571942033922815)
XLA Ops:
  8.7 14.8 %all-to-all-start.1 = ((s32[64,1,1]{2,1,0:T(1,128)}), s32[64,1,1]{2,1,0:T(1,128)S(1)}, u32[]{:S(2)}, u32[]{:S(2)}) async-start(s32[64,1,1]{2,1,0:T(1,128)} %copy.28), calls=%async_computation.1 | async-start | bytes 65536 | tf_op jit(solution)/shard_map/all_to_all | solution.py:58
  23.6 2.7 copy.26
  26.3 3.5 reshape.47
  29.8 2.5 convolution_convert_fusion
  32.4 4.2 %copy.27 = bf16[64,4,6400]{2,1,0:T(4,128)(2,1)} copy(bf16[64,4,6400]{2,0,1:T(8,128)(2,1)S(1)} %convolution_convert_fusion) | data formatting | bytes 6553600 | tf_op jit(solution)/shard_map/convert_element_type | solution.py:52
  36.6 10.3 %all-to-all-start = ((bf16[64,4,6400]{2,1,0:T(4,128)(2,1)}), bf16[64,4,6400]{2,1,0:T(4,128)(2,1)S(1)}, u32[]{:S(2)}, u32[]{:S(2)}) async-start(bf16[64,4,6400]{2,1,0:T(4,128)(2,1)} %copy.27), calls=%async_computation | async-start | bytes 6553600 | tf_op jit(solution)/shard_map/all_to_all | solution.py:57
  49.0 74.7 %all-to-all-done = bf16[64,4,6400]{2,1,0:T(4,128)(2,1)S(1)} async-done(((bf16[64,4,6400]{2,1,0:T(4,128)(2,1)}), bf16[64,4,6400]{2,1,0:T(4,128)(2,1)S(1)}, u32[]{:S(2)}, u32[]{:S(2)}) %all-to-all-start) | async-done | bytes 3276832 | tf_op jit(solution)/shard_map/all_to_all | solution.py:57
  125.1 3.7 reshape.48
  135.3 1.7 convolution_convert_fusion.4
  140.1 2.2 fusion.16
  142.8 3.6 reshape.57
  146.5 75.5 %all-gather.4.cloned.1.call-done = bf16[4,256,3200]{1,2,0:T(8,128)(2,1)} async-done(((bf16[4,256,400]{1,2,0:T(8,128)(2,1)}), bf16[4,256,3200]{1,2,0:T(8,128)(2,1)}) %all-gather.4.cloned.1.call-update) | async-done | bytes 6553616 | tf_op jit(solution)/shard_map/all_gather | solution.py:89
  222.0 5.3 %convolution_convert_fusion.6 = bf16[4,256,256]{2,1,0:T(8,128)(2,1)S(1)} fusion(bf16[4,256,3200]{1,2,0:T(8,128)(2,1)} %all-gather.4.cloned.1.call-done, bf16[3200,256,1]{1,0,2:T(8,128)(2,1)} %reshape.57), kind=kOutput, calls=%fused_computation.34 | convolution fusion | flops 1677983744 | bytes 8716288 | tf_op jit(solution)/shard_map/krf,fh->krh/dot_general | solution.py:90
  229.9 1.6 convolution_convert_fusion.2
  234.3 6.4 %convolution_bitcast_fusion = f32[3200,256]{1,0:T(8,128)} fusion(bf16[4,256,3200]{1,2,0:T(8,128)(2,1)} %all-gather.4.cloned.1.call-done, bf16[4,256,256]{2,1,0:T(8,128)(2,1)S(1)} %bitcast.56), kind=kOutput, calls=%fused_computation.11 | convolution fusion | flops 1677721600 | bytes 10354688 | tf_op jit(solution)/shard_map/krf,krh->fh/dot_general | solution.py:132
  240.8 77.4 %fusion = f32[64,256]{1,0:T(8,128)S(1)} fusion(f32[3200,256]{1,0:T(8,128)} %convolution_bitcast_fusion), kind=kCustom, calls=%all-reduce-scatter | all-reduce-scatter fusion | flops 1048577 | bytes 3344384
  318.2 4.9 %collective-permute-start.12 = (f32[64,256]{1,0:T(8,128)S(1)}, f32[64,256]{1,0:T(8,128)S(1)}, u32[]{:S(2)}, u32[]{:S(2)}) collective-permute-start(f32[64,256]{1,0:T(8,128)S(1)} %fusion), channel_id=1, source_target_pairs={{0,104},{8,112},{16,120},{24,128},{32,136},{40,144},{48,152},{56,1... | collective-permute-start | bytes 196616
  323.1 3.1 collective-permute-start.11
  326.3 5.6 %collective-permute-start.10 = (f32[64,256]{1,0:T(8,128)S(1)}, f32[64,256]{1,0:T(8,128)S(1)}, u32[]{:S(2)}, u32[]{:S(2)}) collective-permute-start(f32[64,256]{1,0:T(8,128)S(1)} %fusion), channel_id=1, source_target_pairs={{0,88},{8,96},{16,104},{24,112},{32,120},{40,128},{48,136},{56,144... | collective-permute-start | bytes 196616
  331.8 1.8 collective-permute-start.9
  333.6 3.7 fusion.4
  342.5 4.9 %collective-permute-start.13 = (f32[50,256]{1,0:T(8,128)S(1)}, f32[50,256]{1,0:T(8,128)S(1)}, u32[]{:S(2)}, u32[]{:S(2)}) collective-permute-start(f32[50,256]{1,0:T(8,128)S(1)} %slice.60), channel_id=1, source_target_pairs={{0,112},{8,120},{16,128},{24,136},{32,144},{40,152},{48,160},{56,1... | collective-permute-start | bytes 153608
  348.6 2.2 collective-permute-start.8
  350.8 4.1 %collective-permute-start.7 = (f32[64,256]{1,0:T(8,128)S(1)}, f32[64,256]{1,0:T(8,128)S(1)}, u32[]{:S(2)}, u32[]{:S(2)}) collective-permute-start(f32[64,256]{1,0:T(8,128)S(1)} %fusion), channel_id=1, source_target_pairs={{0,64},{8,72},{16,80},{24,88},{32,96},{40,104},{48,112},{56,120},{... | collective-permute-start | bytes 196616
  355.0 3.4 collective-permute-start.6
  358.4 3.7 collective-permute-start.5
  362.2 4.2 %collective-permute-start.4 = (f32[64,256]{1,0:T(8,128)S(1)}, f32[64,256]{1,0:T(8,128)S(1)}, u32[]{:S(2)}, u32[]{:S(2)}) collective-permute-start(f32[64,256]{1,0:T(8,128)S(1)} %fusion), channel_id=1, source_target_pairs={{0,40},{8,48},{16,56},{24,64},{32,72},{40,80},{48,88},{56,96},{64,... | collective-permute-start | bytes 196616
  366.4 4.7 %collective-permute-start.3 = (f32[64,256]{1,0:T(8,128)S(1)}, f32[64,256]{1,0:T(8,128)S(1)}, u32[]{:S(2)}, u32[]{:S(2)}) collective-permute-start(f32[64,256]{1,0:T(8,128)S(1)} %fusion), channel_id=1, source_target_pairs={{0,32},{8,40},{16,48},{24,56},{32,64},{40,72},{48,80},{56,88},{64,... | collective-permute-start | bytes 196616
  371.1 1.8 collective-permute-start.2
  373.0 3.5 collective-permute-start.1
  376.5 2.2 collective-permute-start
  380.1 4.5 %concatenate.20 = f32[946,256]{1,0:T(8,128)S(1)} concatenate(f32[50,256]{1,0:T(8,128)S(1)} %collective-permute-done.13, f32[64,256]{1,0:T(8,128)S(1)} %collective-permute-done.12, f32[64,256]{1,0:T(8,128)} %copy-done.10, f32[64,256]{1,0:T(8,128)} %copy-done.11, f32[64,256]{1,0:T(8,128)} %copy-done.12, f32[64,256]{1,0:T(8,128)S(1)} %collective-permute-done.8, ...), dimensions={0} | concatenate | bytes 1937408
  (83 shorter events, 28.4 us)
Async XLA Ops:
  8.7 27.8 %all-to-all-start.1 = ((s32[64,1,1]{2,1,0:T(1,128)}), s32[64,1,1]{2,1,0:T(1,128)S(1)}, u32[]{:S(2)}, u32[]{:S(2)}) async-start(s32[64,1,1]{2,1,0:T(1,128)} %copy.28), calls=%async_computation.1 | async-start | bytes 65536 | tf_op jit(solution)/shard_map/all_to_all | solution.py:58
  36.6 87.1 %all-to-all-start = ((bf16[64,4,6400]{2,1,0:T(4,128)(2,1)}), bf16[64,4,6400]{2,1,0:T(4,128)(2,1)S(1)}, u32[]{:S(2)}, u32[]{:S(2)}) async-start(bf16[64,4,6400]{2,1,0:T(4,128)(2,1)} %copy.27), calls=%async_computation | async-start | bytes 6553600 | tf_op jit(solution)/shard_map/all_to_all | solution.py:57
  46.9 96.0 %all-gather.6.cloned.1.call-start = ((), (), s32[]{:S(2)}) async-start(), calls=%async_computation.3 | async-start | bytes 1863680 | tf_op jit(solution)/shard_map/all_gather | solution.py:65
  47.6 174.4 %all-gather.4.cloned.1.call-start = ((), (), s32[]{:S(2)}) async-start(), calls=%async_computation.2 | async-start | bytes 7372800 | tf_op jit(solution)/shard_map/all_gather | solution.py:89
  125.1 6.9 %copy-start.6 = (bf16[1,3,1025,256]{3,2,1,0:T(8,128)(2,1)S(1)}, bf16[1,3,1025,256]{3,2,1,0:T(8,128)(2,1)}, u32[]{:S(2)}) copy-start(bf16[1,3,1025,256]{3,2,1,0:T(8,128)(2,1)} %param.4) | copy-start | bytes 4723204
  132.2 3.2 copy-start.7
  132.2 4.8 %copy-start.3 = (bf16[1025,256]{1,0:T(8,128)(2,1)}, bf16[1025,256]{1,0:T(8,128)(2,1)S(1)}, u32[]{:S(2)}) copy-start(bf16[1025,256]{1,0:T(8,128)(2,1)S(1)} %get-tuple-element.6) | copy-start | bytes 1574404
  133.1 2.3 copy-start
  137.9 2.2 copy-start.1
  229.8 1.7 copy-start.2
  231.5 1.1 copy-start.9
  240.8 98.6 %slice-start = ((s8[4755456]{0:T(1024)(128)(4,1)}), s8[561152]{0:T(1024)(128)(4,1)S(1)}, s32[]{:S(2)}) async-start(s8[4755456]{0:T(1024)(128)(4,1)} %bitcast.52), calls=%async_computation.4 | async-start | bytes 1122304
  318.2 32.6 %collective-permute-start.12 = (f32[64,256]{1,0:T(8,128)S(1)}, f32[64,256]{1,0:T(8,128)S(1)}, u32[]{:S(2)}, u32[]{:S(2)}) collective-permute-start(f32[64,256]{1,0:T(8,128)S(1)} %fusion), channel_id=1, source_target_pairs={{0,104},{8,112},{16,120},{24,128},{32,136},{40,144},{48,152},{56,1... | collective-permute-start | bytes 196616
  323.1 31.8 %collective-permute-start.11 = (f32[64,256]{1,0:T(8,128)S(1)}, f32[64,256]{1,0:T(8,128)S(1)}, u32[]{:S(2)}, u32[]{:S(2)}) collective-permute-start(f32[64,256]{1,0:T(8,128)S(1)} %fusion), channel_id=1, source_target_pairs={{0,96},{8,104},{16,112},{24,120},{32,128},{40,136},{48,144},{56,15... | collective-permute-start | bytes 196616
  326.3 32.1 %collective-permute-start.10 = (f32[64,256]{1,0:T(8,128)S(1)}, f32[64,256]{1,0:T(8,128)S(1)}, u32[]{:S(2)}, u32[]{:S(2)}) collective-permute-start(f32[64,256]{1,0:T(8,128)S(1)} %fusion), channel_id=1, source_target_pairs={{0,88},{8,96},{16,104},{24,112},{32,120},{40,128},{48,136},{56,144... | collective-permute-start | bytes 196616
  331.8 30.3 %collective-permute-start.9 = (f32[64,256]{1,0:T(8,128)S(1)}, f32[64,256]{1,0:T(8,128)S(1)}, u32[]{:S(2)}, u32[]{:S(2)}) collective-permute-start(f32[64,256]{1,0:T(8,128)S(1)} %fusion), channel_id=1, source_target_pairs={{0,80},{8,88},{16,96},{24,104},{32,112},{40,120},{48,128},{56,136}... | collective-permute-start | bytes 196616
  333.6 5.8 %slice-start.1 = ((s8[4755456]{0:T(1024)(128)(4,1)}), s8[4194304]{0:T(1024)(128)(4,1)S(1)}, s32[]{:S(2)}) async-start(s8[4755456]{0:T(1024)(128)(4,1)} %bitcast.52), calls=%async_computation.5 | async-start | bytes 8388608
  337.4 1.0 copy-start.4
  341.6 20.5 %copy-start.5 = (bf16[1025,128]{1,0:T(8,128)(2,1)S(1)}, bf16[1025,128]{1,0:T(8,128)(2,1)}, u32[]{:S(2)}) copy-start(bf16[1025,128]{1,0:T(8,128)(2,1)} %convolution_convert_fusion.2) | copy-start | bytes 787204
  342.5 6.2 %collective-permute-start.13 = (f32[50,256]{1,0:T(8,128)S(1)}, f32[50,256]{1,0:T(8,128)S(1)}, u32[]{:S(2)}, u32[]{:S(2)}) collective-permute-start(f32[50,256]{1,0:T(8,128)S(1)} %slice.60), channel_id=1, source_target_pairs={{0,112},{8,120},{16,128},{24,136},{32,144},{40,152},{48,160},{56,1... | collective-permute-start | bytes 153608
  348.6 17.8 %collective-permute-start.8 = (f32[64,256]{1,0:T(8,128)S(1)}, f32[64,256]{1,0:T(8,128)S(1)}, u32[]{:S(2)}, u32[]{:S(2)}) collective-permute-start(f32[64,256]{1,0:T(8,128)S(1)} %fusion), channel_id=1, source_target_pairs={{0,72},{8,80},{16,88},{24,96},{32,104},{40,112},{48,120},{56,128},... | collective-permute-start | bytes 196616
  350.8 20.3 %collective-permute-start.7 = (f32[64,256]{1,0:T(8,128)S(1)}, f32[64,256]{1,0:T(8,128)S(1)}, u32[]{:S(2)}, u32[]{:S(2)}) collective-permute-start(f32[64,256]{1,0:T(8,128)S(1)} %fusion), channel_id=1, source_target_pairs={{0,64},{8,72},{16,80},{24,88},{32,96},{40,104},{48,112},{56,120},{... | collective-permute-start | bytes 196616
  355.0 25.1 %copy-start.10 = (f32[64,256]{1,0:T(8,128)}, f32[64,256]{1,0:T(8,128)S(1)}, u32[]{:S(2)}) copy-start(f32[64,256]{1,0:T(8,128)S(1)} %collective-permute-done.11) | copy-start | bytes 196612
  355.0 18.0 %collective-permute-start.6 = (f32[64,256]{1,0:T(8,128)S(1)}, f32[64,256]{1,0:T(8,128)S(1)}, u32[]{:S(2)}, u32[]{:S(2)}) collective-permute-start(f32[64,256]{1,0:T(8,128)S(1)} %fusion), channel_id=1, source_target_pairs={{0,56},{8,64},{16,72},{24,80},{32,88},{40,96},{48,104},{56,112},{6... | collective-permute-start | bytes 196616
  358.4 21.6 %copy-start.11 = (f32[64,256]{1,0:T(8,128)}, f32[64,256]{1,0:T(8,128)S(1)}, u32[]{:S(2)}) copy-start(f32[64,256]{1,0:T(8,128)S(1)} %collective-permute-done.10) | copy-start | bytes 196612
  358.4 18.0 %collective-permute-start.5 = (f32[64,256]{1,0:T(8,128)S(1)}, f32[64,256]{1,0:T(8,128)S(1)}, u32[]{:S(2)}, u32[]{:S(2)}) collective-permute-start(f32[64,256]{1,0:T(8,128)S(1)} %fusion), channel_id=1, source_target_pairs={{0,48},{8,56},{16,64},{24,72},{32,80},{40,88},{48,96},{56,104},{64... | collective-permute-start | bytes 196616
  362.2 17.8 %copy-start.12 = (f32[64,256]{1,0:T(8,128)}, f32[64,256]{1,0:T(8,128)S(1)}, u32[]{:S(2)}) copy-start(f32[64,256]{1,0:T(8,128)S(1)} %collective-permute-done.9) | copy-start | bytes 196612
  362.2 17.8 %collective-permute-start.4 = (f32[64,256]{1,0:T(8,128)S(1)}, f32[64,256]{1,0:T(8,128)S(1)}, u32[]{:S(2)}, u32[]{:S(2)}) collective-permute-start(f32[64,256]{1,0:T(8,128)S(1)} %fusion), channel_id=1, source_target_pairs={{0,40},{8,48},{16,56},{24,64},{32,72},{40,80},{48,88},{56,96},{64,... | collective-permute-start | bytes 196616
  366.4 13.6 %collective-permute-start.3 = (f32[64,256]{1,0:T(8,128)S(1)}, f32[64,256]{1,0:T(8,128)S(1)}, u32[]{:S(2)}, u32[]{:S(2)}) collective-permute-start(f32[64,256]{1,0:T(8,128)S(1)} %fusion), channel_id=1, source_target_pairs={{0,32},{8,40},{16,48},{24,56},{32,64},{40,72},{48,80},{56,88},{64,... | collective-permute-start | bytes 196616
  371.1 8.9 %collective-permute-start.2 = (f32[64,256]{1,0:T(8,128)S(1)}, f32[64,256]{1,0:T(8,128)S(1)}, u32[]{:S(2)}, u32[]{:S(2)}) collective-permute-start(f32[64,256]{1,0:T(8,128)S(1)} %fusion), channel_id=1, source_target_pairs={{0,24},{8,32},{16,40},{24,48},{32,56},{40,64},{48,72},{56,80},{64,... | collective-permute-start | bytes 196616
  373.0 7.0 %collective-permute-start.1 = (f32[64,256]{1,0:T(8,128)S(1)}, f32[64,256]{1,0:T(8,128)S(1)}, u32[]{:S(2)}, u32[]{:S(2)}) collective-permute-start(f32[64,256]{1,0:T(8,128)S(1)} %fusion), channel_id=1, source_target_pairs={{0,16},{8,24},{16,32},{24,40},{32,48},{40,56},{48,64},{56,72},{64,... | collective-permute-start | bytes 196616
  376.5 3.6 collective-permute-start
  (1 other events, 1.0 us)
Sparse Core Ops, SparseCore 0:
  51.0 91.8 all-gather.5
  145.5 76.4 all-gather.3
where the time goes:
time: 394 us; the launch traced here: 392 us
  waiting for transfers between devices  153 us (39%)
  blocking collectives  77.4 us (20%)
  starting transfers between devices  75.4 us (19%)
  matrix products  31.5 us (8%)
  local copies, waits for them, and re-layouts  31.1 us (8%)
  between operations  15.2 us (4%)
  other arithmetic  8.82 us (2%)
    unnamed x1, blocking collectives  77.4 us
    all_gather x1, waiting for transfers between devices, per_device(): features = lax.all_gather(local_rows, 'tensor', axis=2, tiled=True)  75.5 us
    all_to_all x1, waiting for transfers between devices, per_device(): lax.all_to_all(outgoing, 'dp', split_axis=0, concat_axis=0, tiled=True)  74.7 us
    unnamed x14, starting transfers between devices  50 us
    all_to_all x1, starting transfers between devices, per_device(): lax.all_to_all(piece_ids[:, None], 'dp', split_axis=0, concat_axis=0, til...  14.8 us
    unnamed x35, local copies, waits for them, and re-layouts  14.8 us
    all_to_all x1, starting transfers between devices, per_device(): lax.all_to_all(outgoing, 'dp', split_axis=0, concat_axis=0, tiled=True)  10.3 us
  transfers between devices with their start and end apart: 18, of which 4 were waited for; matrix products, arithmetic and copies ran while one was open for 11% of the time, Pallas kernels for 0%

commit v1 on v0

v1 whole, which is shorter than its diff:
```python
import functools
import math

import jax
import jax.numpy as jnp
from jax import lax
from jax.experimental import pallas as pl
from jax.experimental.pallas import tpu as pltpu
from jax.sharding import Mesh, PartitionSpec as P

HD = 128
TT = 1025
PATCHES = 1024
KPAD = 1040
QPAD = 1152
QBLK = 384
PIECE = 16
NPIECE = 16
MAIN = 384
GROUP = 50
GPAD = 64
BF = jnp.bfloat16
F32 = jnp.float32
SHARDS = ("z", "x", "c")
SCALE = HD ** (-0.5)


def dot(left, right):
    return jnp.dot(left, right, preferred_element_type=F32)


def dot_last(left, right):
    return lax.dot_general(left, right, (((1,), (1,)), ((), ())), preferred_element_type=F32)


def dot_first(left, right):
    return lax.dot_general(left, right, (((0,), (0,)), ((), ())), preferred_element_type=F32)


def iota(shape, axis):
    return lax.broadcasted_iota(jnp.int32, shape, axis)


def params():
    return pltpu.CompilerParams(vmem_limit_bytes=50 * 1024 * 1024)


def pack_kernel(label_ref, rows_ref, out0_ref, out1_ref, rest_ref):
    slots = label_ref.shape[1]
    rest = jnp.zeros(rest_ref.shape, F32)
    for k in range(4):
        place = (iota((16, 128), 1) == iota((16, 128), 0) + 16 * k).astype(F32).astype(BF)
        rest = rest + dot(rows_ref[k, :, MAIN : MAIN + 16], place)
    rest_ref[...] = rest
    lane = iota((PIECE, 128), 1)
    nothing = jnp.where(lane == 64, -1.0, 0.0).astype(BF)

    def clear(d, carry):
        out0_ref[d, :, 2 * MAIN :] = nothing
        return carry

    lax.fori_loop(0, out0_ref.shape[0], clear, 0)

    def place_slot(s, carry):
        label = label_ref[0, s]

        @pl.when(label >= 0)
        def _():
            owner = label >> 4
            piece = label & 15
            rows = pl.ds(pl.multiple_of(s * PIECE, PIECE), PIECE)
            out0_ref[owner, :, 0:MAIN] = rows_ref[0, rows, 0:MAIN]
            out0_ref[owner, :, MAIN : 2 * MAIN] = rows_ref[1, rows, 0:MAIN]
            out1_ref[owner, :, 0:MAIN] = rows_ref[2, rows, 0:MAIN]
            out1_ref[owner, :, MAIN : 2 * MAIN] = rows_ref[3, rows, 0:MAIN]
            number = piece.astype(F32)
            out0_ref[owner, :, 2 * MAIN :] = jnp.where(lane == 64, number, rest_ref[rows, :]).astype(BF)

        return carry

    lax.fori_loop(0, slots, place_slot, 0)


def pack(labels, rows, peers):
    return pl.pallas_call(
        pack_kernel,
        out_shape=(
            jax.ShapeDtypeStruct((peers, PIECE, 2 * MAIN + 128), BF),
            jax.ShapeDtypeStruct((peers, PIECE, 2 * MAIN), BF),
        ),
        in_specs=[
            pl.BlockSpec(memory_space=pltpu.SMEM),
            pl.BlockSpec(memory_space=pltpu.VMEM),
        ],
        out_specs=(
            pl.BlockSpec(memory_space=pltpu.VMEM),
            pl.BlockSpec(memory_space=pltpu.VMEM),
        ),
        scratch_shapes=[pltpu.VMEM((rows.shape[1], 128), F32)],
        compiler_params=params(),
        name="pack_pieces",
    )(labels, rows)


def receive_kernel(chunk, source_ref, in_ref, rest_in_ref, weight_ref, rows_ref, part_ref, rest_ref, left_scr, stack_scr):
    if chunk == 0:
        for i in range(NPIECE):
            rest_ref[16 * i : 16 * i + 16, :] = in_ref[source_ref[i], :, 2 * MAIN :]
        rest = rest_ref[...]
    else:
        rest = rest_in_ref[...]
    column = iota((MAIN, 8 * GPAD), 1)
    inside = (column & 63) < GROUP
    feature = (column >> 6) * GROUP + (column & 63)
    spread = jnp.where((feature == iota((MAIN, 8 * GPAD), 0)) & inside, 1.0, 0.0).astype(BF)
    for u in range(2):
        for i in range(NPIECE):
            left_scr[16 * i : 16 * i + 16, :] = in_ref[source_ref[i], :, u * MAIN : (u + 1) * MAIN]
        k = 2 * chunk + u
        lane = iota((128, 8 * GPAD), 0)
        spread_rest = jnp.where(
            (feature[0:128] == lane + (MAIN - 16 * k)) & inside[0:128] & (lane >= 16 * k) & (lane < 16 * k + 16),
            1.0,
            0.0,
        ).astype(BF)
        wide = (dot(left_scr[...], spread) + dot(rest, spread_rest)).astype(BF)
        stack_scr[0, u * 128 : (u + 1) * 128, :] = wide[0:128]
        stack_scr[1, u * 128 : (u + 1) * 128, :] = wide[128:256]
    row = iota((256, 256), 0)
    wanted = (row & 1) * 128 + (row >> 5) * 16 + ((row >> 1) & 15)
    order = jnp.where(iota((256, 256), 1) == wanted, 1.0, 0.0).astype(BF)
    for half in range(2):
        rows_ref[half * 256 : (half + 1) * 256, :] = dot(order, stack_scr[half]).astype(BF)
    rows = rows_ref[...]
    for a in range(8):
        part_ref[a] = dot(rows, weight_ref[:, a * 256 : (a + 1) * 256]).astype(BF)


def receive(chunk, source, arrived, rest, weight):
    vmem = pl.BlockSpec(memory_space=pltpu.VMEM)
    return pl.pallas_call(
        functools.partial(receive_kernel, chunk),
        out_shape=(
            jax.ShapeDtypeStruct((512, 512), BF),
            jax.ShapeDtypeStruct((8, 512, 256), BF),
            jax.ShapeDtypeStruct((256, 128), BF),
        ),
        in_specs=[pl.BlockSpec(memory_space=pltpu.SMEM), vmem, vmem, vmem],
        out_specs=(vmem, vmem, vmem),
        scratch_shapes=[pltpu.VMEM((256, MAIN), BF), pltpu.VMEM((2, 256, 512), BF)],
        compiler_params=params(),
        name=f"receive_{chunk}",
    )(source, arrived, rest, weight)


def forward_kernel(x_ref, p_ref, att_ref, a_ref, q_scr, vt_scr, a_scr):
    tail_row = iota((16, 128), 0) == 0
    q_scr[0:1024, :] = x_ref[0, 0, 0:1024, :]
    q_scr[1024:QPAD, :] = jnp.zeros((128, 128), BF)
    q_scr[1024:1040, :] = jnp.where(tail_row, x_ref[0, 0, 1024:1025, :].astype(F32), 0.0).astype(BF)
    key = x_ref[0, 1, 0:1024, :]
    key_tail = jnp.where(tail_row, x_ref[0, 1, 1024:1025, :].astype(F32), 0.0).astype(BF)
    vt_scr[...] = x_ref[0, 2, 0:1024, :].astype(F32).T.astype(BF)
    value_tail = jnp.where(tail_row, x_ref[0, 2, 1024:1025, :].astype(F32), 0.0).astype(BF)
    first = iota((16, QBLK), 0) == 0
    for j in range(QPAD // QBLK):
        span = slice(j * QBLK, (j + 1) * QBLK)
        query = q_scr[span, :]
        score = dot_last(key, query) * SCALE
        score_tail = (dot_last(key_tail, query) * SCALE)[0:1]
        top = jnp.maximum(jnp.max(score, axis=0, keepdims=True), score_tail)
        shifted = jnp.exp(score - top)
        shifted_tail = jnp.exp(score_tail - top)
        inverse = 1.0 / (jnp.sum(shifted, axis=0, keepdims=True) + shifted_tail)
        low = (shifted * inverse).astype(BF)
        low_tail = jnp.where(first, shifted_tail * inverse, 0.0).astype(BF)
        p_ref[0, 0:1024, span] = low
        p_ref[0, 1024:KPAD, span] = low_tail
        att = (dot(vt_scr[...], low) + dot_first(value_tail, low_tail)).T.astype(BF)
        att_ref[span, :] = att
        a_scr[span, :] = att.astype(F32)
    moved = a_scr[pl.ds(1, 1024), :].astype(BF)
    for i in range(NPIECE):
        for e in range(2):
            a_ref[e, 32 * i : 32 * i + 32, :] = moved[64 * i + 32 * e : 64 * i + 32 * e + 32]


def forward(head_inputs):
    return pl.pallas_call(
        forward_kernel,
        grid=(2,),
        out_shape=(
            jax.ShapeDtypeStruct((2, KPAD, QPAD), BF),
            jax.ShapeDtypeStruct((QPAD, 256), BF),
            jax.ShapeDtypeStruct((2, 512, 256), BF),
        ),
        in_specs=[pl.BlockSpec((1, 3, TT, HD), lambda h: (0, 0, 0, h))],
        out_specs=(
            pl.BlockSpec((1, KPAD, QPAD), lambda h: (h, 0, 0)),
            pl.BlockSpec((QPAD, HD), lambda h: (0, h)),
            pl.BlockSpec((2, 512, HD), lambda h: (0, 0, h)),
        ),
        scratch_shapes=[
            pltpu.VMEM((QPAD, HD), BF),
            pltpu.VMEM((HD, 1024), BF),
            pltpu.VMEM((QPAD, HD), F32),
        ],
        compiler_params=params(),
        cost_estimate=pl.CostEstimate(flops=12 * 10**9, bytes_accessed=8 * 10**6, transcendentals=2 * 10**6),
        name="attend",
    )(head_inputs)


def backward_kernel(x_ref, p_ref, att_ref, o0_ref, o1_ref, out_ref, q_scr, kt_scr, g_scr, dq_scr, dk_scr, dv_scr, dkt_scr, dvt_scr):
    tail_row = iota((16, 128), 0) == 0
    q_scr[0:1024, :] = x_ref[0, 0, 0:1024, :]
    q_scr[1024:QPAD, :] = jnp.zeros((128, 128), BF)
    q_scr[1024:1040, :] = jnp.where(tail_row, x_ref[0, 0, 1024:1025, :].astype(F32), 0.0).astype(BF)
    kt_scr[...] = x_ref[0, 1, 0:1024, :].astype(F32).T.astype(BF)
    key_tail = jnp.where(tail_row, x_ref[0, 1, 1024:1025, :].astype(F32), 0.0).astype(BF)
    value = x_ref[0, 2, 0:1024, :]
    value_tail = jnp.where(tail_row, x_ref[0, 2, 1024:1025, :].astype(F32), 0.0).astype(BF)
    g_scr[0:8, :] = jnp.zeros((8, HD), F32)
    g_scr[1024 : QPAD, :] = jnp.zeros((QPAD - 1024, HD), F32)
    for i in range(NPIECE):
        g_scr[pl.ds(1 + 64 * i, 32), :] = o0_ref[32 * i : 32 * i + 32, :].astype(F32)
        g_scr[pl.ds(33 + 64 * i, 32), :] = o1_ref[32 * i : 32 * i + 32, :].astype(F32)
    for j in range(QPAD // QBLK):
        span = slice(j * QBLK, (j + 1) * QBLK)
        query = q_scr[span, :]
        grad_wide = g_scr[span, :]
        grad = grad_wide.astype(BF)
        delta = jnp.sum((grad_wide * att_ref[span, :].astype(F32)).T, axis=0, keepdims=True)
        low = p_ref[0, 0:1024, span]
        low_tail = p_ref[0, 1024:KPAD, span]
        inner = (low.astype(F32) * (dot_last(value, grad) - delta)).astype(BF)
        inner_tail = (low_tail.astype(F32) * (dot_last(value_tail, grad) - delta)).astype(BF)
        dq = (dot(kt_scr[...], inner) + dot_first(key_tail, inner_tail)) * SCALE
        dq_scr[span, :] = dq.T.astype(BF)
        dk, dkt = dot(inner, query), dot(inner_tail, query)
        dv, dvt = dot(low, grad), dot(low_tail, grad)
        if j == 0:
            dk_scr[...], dkt_scr[...], dv_scr[...], dvt_scr[...] = dk, dkt, dv, dvt
        else:
            dk_scr[...] += dk
            dkt_scr[...] += dkt
            dv_scr[...] += dv
            dvt_scr[...] += dvt
    out_ref[0, 0, 0:1024, :] = dq_scr[0:1024, :]
    out_ref[0, 0, 1024:1025, :] = dq_scr[1024:1040, :][0:1]
    out_ref[0, 1, 0:1024, :] = (dk_scr[...] * SCALE).astype(BF)
    out_ref[0, 1, 1024:1025, :] = (dkt_scr[...] * SCALE).astype(BF)[0:1]
    out_ref[0, 2, 0:1024, :] = dv_scr[...].astype(BF)
    out_ref[0, 2, 1024:1025, :] = dvt_scr[...].astype(BF)[0:1]


def backward(head_inputs, probs, att, o0, o1):
    return pl.pallas_call(
        backward_kernel,
        grid=(2,),
        out_shape=jax.ShapeDtypeStruct((1, 3, TT, 256), BF),
        in_specs=[
            pl.BlockSpec((1, 3, TT, HD), lambda h: (0, 0, 0, h)),
            pl.BlockSpec((1, KPAD, QPAD), lambda h: (h, 0, 0)),
            pl.BlockSpec((QPAD, HD), lambda h: (0, h)),
            pl.BlockSpec((512, HD), lambda h: (0, h)),
            pl.BlockSpec((512, HD), lambda h: (0, h)),
        ],
        out_specs=pl.BlockSpec((1, 3, TT, HD), lambda h: (0, 0, 0, h)),
        scratch_shapes=[
            pltpu.VMEM((QPAD, HD), BF),
            pltpu.VMEM((HD, 1024), BF),
            pltpu.VMEM((QPAD, HD), F32),
            pltpu.VMEM((QPAD, HD), BF),
            pltpu.VMEM((1024, HD), F32),
            pltpu.VMEM((1024, HD), F32),
            pltpu.VMEM((16, HD), F32),
            pltpu.VMEM((16, HD), F32),
        ],
        compiler_params=params(),
        name="attend_backward",
    )(head_inputs, probs, att, o0, o1)


def weight_kernel(core_ref, r0_ref, r1_ref, a_ref, keep_ref, send_ref, t0_scr, t1_scr, sum_scr):
    @pl.when(pl.program_id(0) == 0)
    def _():
        t0_scr[...] = r0_ref[...].astype(F32).T.astype(BF)
        t1_scr[...] = r1_ref[...].astype(F32).T.astype(BF)

    sum_scr[...] = dot(t0_scr[...], a_ref[0, 0]) + dot(t1_scr[...], a_ref[0, 1])
    core = core_ref[0]
    for x in range(4):
        mine = pl.multiple_of((2 * x + core) * GPAD, GPAD)
        other = pl.multiple_of((2 * x + 1 - core) * GPAD, GPAD)
        keep_ref[0, x] = sum_scr[pl.ds(mine, GPAD), :][0:GROUP]
        send_ref[0, x] = sum_scr[pl.ds(other, GPAD), :][0:GROUP].astype(BF)


def weight_parts(core, r0, r1, gathered):
    return pl.pallas_call(
        weight_kernel,
        grid=(8,),
        out_shape=(
            jax.ShapeDtypeStruct((8, 4, GROUP, 256), F32),
            jax.ShapeDtypeStruct((8, 4, GROUP, 256), BF),
        ),
        in_specs=[
            pl.BlockSpec(memory_space=pltpu.SMEM),
            pl.BlockSpec((512, 512), lambda a: (0, 0)),
            pl.BlockSpec((512, 512), lambda a: (0, 0)),
            pl.BlockSpec((1, 2, 512, 256), lambda a: (a, 0, 0, 0)),
        ],
        out_specs=(
            pl.BlockSpec((1, 4, GROUP, 256), lambda a: (a, 0, 0, 0)),
            pl.BlockSpec((1, 4, GROUP, 256), lambda a: (a, 0, 0, 0)),
        ),
        scratch_shapes=[
            pltpu.VMEM((512, 512), BF),
            pltpu.VMEM((512, 512), BF),
            pltpu.VMEM((512, 256), F32),
        ],
        compiler_params=params(),
        name="weight_parts",
    )(core, r0, r1, gathered)


def per_device(head_inputs, out_weight, sequence_gradient, slot_labels):
    peers = 64
    swap = [(z * 8 + y, y * 8 + z) for z in range(8) for y in range(8)]
    out0, out1 = pack(slot_labels, sequence_gradient, peers)
    in0 = lax.all_to_all(out0, SHARDS, 0, 0, tiled=True)
    in1 = lax.all_to_all(out1, SHARDS, 0, 0, tiled=True)

    weight = lax.ppermute(out_weight, ("z", "y"), swap)
    weight = lax.all_gather(weight, "z", axis=0)
    weight = lax.all_gather(weight, "x", axis=0)
    weight = lax.all_gather(weight, "c", axis=0)
    weight = jnp.pad(weight, ((0, 0), (0, 0), (0, 0), (0, GPAD - GROUP), (0, 0)))
    weight = weight.transpose(1, 0, 3, 2, 4).reshape(8 * GPAD, 2048)

    probs, att, parts = forward(head_inputs)
    gathered = lax.all_gather(parts, "y", axis=0)

    ids = in0[:, 0, 2 * MAIN + 64].astype(jnp.int32)
    wanted = jnp.arange(NPIECE, dtype=jnp.int32)
    source = jnp.sum(
        jnp.where(ids[None, :] == wanted[:, None], jnp.arange(peers, dtype=jnp.int32)[None, :], 0), axis=1
    )
    r0, part0, rest = receive(0, source, in0, jnp.zeros((256, 128), BF), weight)
    o0 = lax.psum_scatter(part0, "y", scatter_dimension=0, tiled=True)[0]
    r1, part1, _ = receive(1, source, in1, rest, weight)
    o1 = lax.psum_scatter(part1, "y", scatter_dimension=0, tiled=True)[0]

    core = lax.axis_index("c").astype(jnp.int32)[None]
    keep, send = weight_parts(core, r0, r1, gathered)
    got = lax.ppermute(send, "c", [(0, 1), (1, 0)])
    both = (keep + got.astype(F32)).astype(BF).reshape(32, GROUP, 256)
    spread = lax.all_to_all(both, ("z", "x"), 0, 0, tiled=True)
    summed = jnp.sum(spread.astype(F32), axis=0) * (1.0 / math.sqrt(65536))
    weight_gradient = lax.ppermute(summed, ("z", "y"), swap)

    head_gradient = backward(head_inputs, probs, att, o0, o1)
    return head_gradient, weight_gradient


def solution(mesh):
    fine = Mesh(mesh.devices.reshape(8, 4, 2, 8), ("z", "x", "c", "y"))
    return jax.shard_map(
        per_device,
        mesh=fine,
        in_specs=(
            P(SHARDS, None, None, "y"),
            P(SHARDS, "y"),
            P(None, SHARDS, "y"),
            P(SHARDS, None),
        ),
        out_specs=(P(SHARDS, None, None, "y"), P(SHARDS, "y")),
        check_vma=False,
    )
```

time: 394 us -> 289 us (0.73)
  waiting for transfers between devices: 153 us -> 69 us
  starting transfers between devices: 75.4 us -> 12.8 us
  blocking collectives: 77.4 us -> 139 us
  Pallas kernels: 0 us -> 36.8 us
  matrix products: 31.5 us -> 0 us
  local copies, waits for them, and re-layouts: 31.1 us -> 11.2 us
  other arithmetic: 8.82 us -> 1.92 us
    all_to_all x0 -> x2, blocking collectives: none -> 90.8 us  [the longest x1 62.5 us: per_device(): in0 = lax.all_to_all(out0, SHARDS, 0, 0, tiled=True)]
    unnamed x1 -> x0, blocking collectives: 77.4 us -> none
    all_gather x2, waiting for transfers between devices: 76.1 us -> 0.04 us  [the longest x1 0.02 us: per_device(): weight = lax.all_gather(weight, 'c', axis=0)]
    unnamed x14 -> x0, starting transfers between devices: 50 us -> none
    all_gather x0 -> x2, blocking collectives: none -> 48.2 us  [the longest x1 36.5 us: per_device(): weight = lax.all_gather(weight, 'z', axis=0)]
    all_to_all x2 -> x1, waiting for transfers between devices: 74.7 us -> 28 us  [per_device(): in1 = lax.all_to_all(out1, SHARDS, 0, 0, tiled=True)]
    reduce_scatter x0 -> x2, waiting for transfers between devices: none -> 38.6 us  [the longest x1 38.6 us: per_device(): o0 = lax.psum_scatter(part0, 'y', scatter_dimension=0, tiled=True)[0]]
    pallas_call x0 -> x6, Pallas kernels: none -> 36.8 us  [the longest x2 9.8 us: receive(): pl.pallas_call(functools.partial(receive_kernel, chunk), out_shape=(jax.S...]
  transfers between devices with their start and end apart: 18 -> 8, of which waited for: 4 -> 3; matrix products, arithmetic and copies ran while one was open for 11% -> 3% of each run, Pallas kernels for 0% -> 13%
where the time goes in v1:
time: 289 us; the launch traced here: 285 us
  blocking collectives  139 us (48%)
  waiting for transfers between devices  69 us (24%)
  Pallas kernels  36.8 us (13%)
  between operations  14 us (5%)
  starting transfers between devices  12.8 us (4%)
  local copies, waits for them, and re-layouts  11.2 us (4%)
    all_to_all x1, blocking collectives, per_device(): in0 = lax.all_to_all(out0, SHARDS, 0, 0, tiled=True)  62.5 us
    reduce_scatter x1, waiting for transfers between devices, per_device(): o0 = lax.psum_scatter(part0, 'y', scatter_dimension=0, tiled=True)[0]  38.6 us
    all_gather x1, blocking collectives, per_device(): weight = lax.all_gather(weight, 'z', axis=0)  36.5 us
    all_to_all x1, blocking collectives, per_device(): spread = lax.all_to_all(both, ('z', 'x'), 0, 0, tiled=True)  28.3 us
    all_to_all x1, waiting for transfers between devices, per_device(): in1 = lax.all_to_all(out1, SHARDS, 0, 0, tiled=True)  28 us
    all_gather x1, blocking collectives, per_device(): weight = lax.all_gather(weight, 'x', axis=0)  11.7 us
    pallas_call x2, Pallas kernels, receive(): pl.pallas_call(functools.partial(receive_kernel, chunk), out_shape=(jax.S...  9.8 us
    pallas_call x1, Pallas kernels, backward(): pl.pallas_call(backward_kernel, grid=(2,), out_shape=jax.ShapeDtypeStruct...  9.33 us
  transfers between devices with their start and end apart: 8, of which 3 were waited for; matrix products, arithmetic and copies ran while one was open for 3% of the time, Pallas kernels for 13%

profile of v1, /device:TPU:1, one launch (start us, length us, event | category | flops | bytes accessed | tf_op | source)
XLA Modules:
  0.0 284.8 jit_solution(10664452409012888800)
XLA Ops:
  7.2 1.5 collective-permute-start
  8.8 36.5 %all-gather.4 = bf16[8,50,256]{2,1,0:T(8,128)(2,1)S(1)} all-gather(bf16[1,50,256]{2,1,0:T(8,128)(2,1)S(1)} %bitcast.22), channel_id=2, replica_groups=mesh['z'=8,'x'=4,'c'=2,'y'=8] {'z'}, dimensions={0}, use_global_device_ids=true | all-gather | bytes 230400 | tf_op jit(solution)/shard_map/all_gather | solution.py:336
  45.3 11.7 %all-gather.1 = bf16[32,50,256]{2,0,1:T(8,128)(2,1)} all-gather(bf16[8,50,256]{2,0,1:T(8,128)(2,1)S(1)} %copy.23), channel_id=3, replica_groups=mesh['z'=8,'x'=4,'c'=2,'y'=8] {'x'}, dimensions={0}, use_global_device_ids=true | all-gather | bytes 1024000 | tf_op jit(solution)/shard_map/all_gather | solution.py:337
  57.1 7.9 %attend.1 = (bf16[2,1040,1152]{2,1,0:T(8,128)(2,1)}, bf16[1152,256]{1,0:T(8,128)(2,1)S(1)}, bf16[2,512,256]{2,1,0:T(8,128)(2,1)}) custom-call(bf16[1,3,1025,256]{3,2,1,0:T(8,128)(2,1)S(1)} %copy-done), custom_call_target="tpu_custom_call" | custom-call | flops 12000000000 | bytes 8000000 | tf_op jit(solution)/shard_map/attend/pallas_call | solution.py:189
  65.0 0.8 copy-done.3
  65.9 2.3 copy.22.rows_ref
  68.2 2.8 pack_pieces.1
  71.0 62.5 %all_to_all.15.in_ref = bf16[64,16,896]{2,1,0:T(8,128)(2,1)S(1)} all-to-all(bf16[64,16,896]{2,1,0:T(8,128)(2,1)S(1)} %get-tuple-element.16), channel_id=1, replica_groups=mesh['z'=8,'x'=4,'c'=2,'y'=8] {'z','x','c'}, dimensions={0} | all-to-all | bytes 3670016 | tf_op jit(solution)/shard_map/all_to_all | solution.py:332
  133.5 6.8 %all-to-all-start.1 = ((bf16[64,16,768]{2,1,0:T(8,128)(2,1)}), bf16[64,16,768]{2,1,0:T(8,128)(2,1)S(1)}, u32[]{:S(2)}, u32[]{:S(2)}) async-start(bf16[64,16,768]{2,1,0:T(8,128)(2,1)} %copy-done.2), calls=%async_computation.2 | async-start | bytes 3145728 | tf_op jit(solution)/shard_map/all_to_all | solution.py:333
  140.4 1.5 copy.24
  142.2 2.0 copy.28
  144.2 1.3 fusion
  145.7 4.9 %receive_0.1 = (bf16[512,512]{1,0:T(8,128)(2,1)S(1)}, bf16[8,512,256]{2,1,0:T(8,128)(2,1)}, bf16[256,128]{1,0:T(8,128)(2,1)S(1)}) custom-call(s32[16]{0:T(128)S(1)} %select_reduce_fusion.source_ref, bf16[64,16,896]{2,1,0:T(8,128)(2,1)S(1)} %all_to_all.15.in_ref, bf16[256,128]{1,0:T(8,128)(2,1)S(1)} %broadcast_in_dim.23.rest_in_ref, bf16[512,2048]{1,0:T(8,128)(2,1)} %bitcast.15), custom_call_target="tpu_custom_call" | custom-call | tf_op jit(solution)/shard_map/receive_0/pallas_call | solution.py:141
  150.5 0.8 copy-done.5
  151.3 28.0 %all-to-all-done.1.in_ref = bf16[64,16,768]{2,1,0:T(8,128)(2,1)S(1)} async-done(((bf16[64,16,768]{2,1,0:T(8,128)(2,1)}), bf16[64,16,768]{2,1,0:T(8,128)(2,1)S(1)}, u32[]{:S(2)}, u32[]{:S(2)}) %all-to-all-start.1) | async-done | bytes 1572896 | tf_op jit(solution)/shard_map/all_to_all | solution.py:333
  179.3 4.9 %receive_1.1 = (bf16[512,512]{1,0:T(8,128)(2,1)S(1)}, bf16[8,512,256]{2,1,0:T(8,128)(2,1)}, bf16[256,128]{1,0:T(8,128)(2,1)}) custom-call(s32[16]{0:T(128)S(1)} %select_reduce_fusion.source_ref, bf16[64,16,768]{2,1,0:T(8,128)(2,1)S(1)} %all-to-all-done.1.in_ref, bf16[256,128]{1,0:T(8,128)(2,1)S(1)} %get-tuple-element.19.rest_in_ref, bf16[512,2048]{1,0:T(8,128)(2,1)} %bitcast.16), custom_call_target="tpu_custom_call" | custom-call | tf_op jit(solution)/shard_map/receive_1/pallas_call | solution.py:141
  184.3 0.2 reduce-scatter.3.cloned.1.call-start
  184.5 0.3 reduce-scatter.3.cloned.1.call-update
  184.9 0.4 copy-done.6
  185.3 7.0 %weight_parts.1 = (f32[8,4,50,256]{3,2,1,0:T(8,128)S(1)}, bf16[8,4,50,256]{3,2,1,0:T(8,128)(2,1)S(1)}) custom-call(s32[1]{0:T(128)} %bitcast.6.core_ref, bf16[512,512]{1,0:T(8,128)(2,1)S(1)} %copy-done.6, bf16[512,512]{1,0:T(8,128)(2,1)S(1)} %get-tuple-element.22.r1_ref, bf16[8,2,512,256]{3,2,1,0:T(8,128)(2,1)} %bitcast.19), custom_call_target="tpu_custom_call" | custom-call | tf_op jit(solution)/shard_map/weight_parts/pallas_call | solution.py:301
  192.3 0.5 copy.26
  192.8 3.5 %collective-permute-start.1 = (bf16[8,4,50,256]{3,0,2,1:T(8,128)(2,1)S(1)}, bf16[8,4,50,256]{3,0,2,1:T(8,128)(2,1)S(1)}, u32[]{:S(2)}, u32[]{:S(2)}) collective-permute-start(bf16[8,4,50,256]{3,0,2,1:T(8,128)(2,1)S(1)} %copy.26), channel_id=1, source_target_pairs={{0,8},{8,0},{1,9},{9,1},{2,10},{10,2},{3,11},{11,3},{4,12},{12,4},... | collective-permute-start | bytes 2457608 | tf_op jit(solution)/shard_map/ppermute | solution.py:357
  196.3 1.9 collective-permute-done.1
  198.2 0.3 add_convert_fusion
  198.6 28.3 %all_to_all.16 = bf16[32,50,256]{2,1,0:T(8,128)(2,1)S(1)} all-to-all(bf16[32,50,256]{2,1,0:T(8,128)(2,1)S(1)} %bitcast.20), channel_id=1, replica_groups=mesh['z'=8,'x'=4,'c'=2,'y'=8] {'z','x'}, dimensions={0} | all-to-all | bytes 1638400 | tf_op jit(solution)/shard_map/all_to_all | solution.py:359
  226.9 0.1 convert_reduce_fusion
  227.1 0.7 collective-permute-start.2
  227.8 38.6 %reduce-scatter.3.cloned.1.call-done = bf16[1,512,256]{2,1,0:T(8,128)(2,1)} async-done(((bf16[8,512,256]{2,1,0:T(8,128)(2,1)}), bf16[1,512,256]{2,1,0:T(8,128)(2,1)}) %reduce-scatter.3.cloned.1.call-update) | async-done | bytes 262160 | tf_op jit(solution)/shard_map/reduce_scatter | solution.py:351
  266.4 0.9 copy-done.7
  267.3 0.9 copy-done.8
  268.3 9.3 %attend_backward.1 = bf16[1,3,1025,256]{3,2,1,0:T(8,128)(2,1)} custom-call(bf16[1,3,1025,256]{3,2,1,0:T(8,128)(2,1)S(1)} %copy-done.1, bf16[2,1040,1152]{2,1,0:T(8,128)(2,1)} %get-tuple-element.14.p_ref, bf16[1152,256]{1,0:T(8,128)(2,1)S(1)} %copy-done.4, bf16[512,256]{1,0:T(8,128)(2,1)S(1)} %bitcast.14, bf16[512,256]{1,0:T(8,128)(2,1)S(1)} %bitcast.13), custom_call_target="tpu_custom_call" | custom-call | tf_op jit(solution)/shard_map/attend_backward/pallas_call | solution.py:258
  277.6 0.6 copy.31
  (34 shorter events, 0.7 us)
Async XLA Ops:
  7.2 50.0 %copy-start = (bf16[1,3,1025,256]{3,2,1,0:T(8,128)(2,1)S(1)}, bf16[1,3,1025,256]{3,2,1,0:T(8,128)(2,1)}, u32[]{:S(2)}) copy-start(bf16[1,3,1025,256]{3,2,1,0:T(8,128)(2,1)} %x_ref.3) | copy-start | bytes 4723204
  7.2 133.2 %all-gather.8.cloned.1.call-start = ((), (), s32[]{:S(2)}) async-start(), calls=%async_computation.7 | async-start | bytes 2457600 | tf_op jit(solution)/shard_map/all_gather | solution.py:338
  7.2 1.5 collective-permute-start
  57.1 8.8 %copy-start.10 = (bf16[4,512,400]{1,2,0:T(8,128)(2,1)S(1)}, bf16[4,512,400]{1,2,0:T(8,128)(2,1)}, u32[]{:S(2)}) copy-start(bf16[4,512,400]{1,2,0:T(8,128)(2,1)} %param.6) | copy-start | bytes 4915204
  57.1 127.8 %all-gather.10.cloned.1.call-start = ((), (), s32[]{:S(2)}) async-start(), calls=%async_computation.8 | async-start | bytes 4718592 | tf_op jit(solution)/shard_map/all_gather | solution.py:343
  65.0 0.8 copy-start.3
  65.9 2.4 copy-start.9
  71.0 62.5 %copy-start.2 = (bf16[64,16,768]{2,1,0:T(8,128)(2,1)}, bf16[64,16,768]{2,1,0:T(8,128)(2,1)S(1)}, u32[]{:S(2)}) copy-start(bf16[64,16,768]{2,1,0:T(8,128)(2,1)S(1)} %get-tuple-element.18) | copy-start | bytes 4718596
  133.5 45.8 %all-to-all-start.1 = ((bf16[64,16,768]{2,1,0:T(8,128)(2,1)}), bf16[64,16,768]{2,1,0:T(8,128)(2,1)S(1)}, u32[]{:S(2)}, u32[]{:S(2)}) async-start(bf16[64,16,768]{2,1,0:T(8,128)(2,1)} %copy-done.2), calls=%async_computation.2 | async-start | bytes 3145728 | tf_op jit(solution)/shard_map/all_to_all | solution.py:333
  140.3 87.4 %reduce-scatter.5.cloned.1.call-start = ((), (), s32[]{:S(2)}) async-start(), calls=%async_computation.6 | async-start | bytes 2359296 | tf_op jit(solution)/shard_map/reduce_scatter | solution.py:353
  150.5 0.8 copy-start.5
  184.3 1.0 copy-start.6
  184.3 82.1 %reduce-scatter.3.cloned.1.call-start = ((), (), s32[]{:S(2)}) async-start(), calls=%async_computation.5 | async-start | bytes 2359296 | tf_op jit(solution)/shard_map/reduce_scatter | solution.py:351
  192.8 5.4 %collective-permute-start.1 = (bf16[8,4,50,256]{3,0,2,1:T(8,128)(2,1)S(1)}, bf16[8,4,50,256]{3,0,2,1:T(8,128)(2,1)S(1)}, u32[]{:S(2)}, u32[]{:S(2)}) collective-permute-start(bf16[8,4,50,256]{3,0,2,1:T(8,128)(2,1)S(1)} %copy.26), channel_id=1, source_target_pairs={{0,8},{8,0},{1,9},{9,1},{2,10},{10,2},{3,11},{11,3},{4,12},{12,4},... | collective-permute-start | bytes 2457608 | tf_op jit(solution)/shard_map/ppermute | solution.py:357
  198.6 67.8 %copy-start.1 = (bf16[1,3,1025,256]{3,2,1,0:T(8,128)(2,1)S(1)}, bf16[1,3,1025,256]{3,2,1,0:T(8,128)(2,1)}, u32[]{:S(2)}) copy-start(bf16[1,3,1025,256]{3,2,1,0:T(8,128)(2,1)} %x_ref.3) | copy-start | bytes 4723204
  198.6 67.8 %copy-start.4 = (bf16[1152,256]{1,0:T(8,128)(2,1)S(1)}, bf16[1152,256]{1,0:T(8,128)(2,1)}, u32[]{:S(2)}) copy-start(bf16[1152,256]{1,0:T(8,128)(2,1)} %copy-done.3) | copy-start | bytes 1769476
  227.1 50.5 %collective-permute-start.2 = (f32[50,256]{1,0:T(8,128)S(1)}, f32[50,256]{1,0:T(8,128)S(1)}, u32[]{:S(2)}, u32[]{:S(2)}) collective-permute-start(f32[50,256]{1,0:T(8,128)S(1)} %broadcast_multiply_fusion), channel_id=1, source_target_pairs={{0,0},{1,64},{2,128},{3,192},{4,256},{5,320},{6,384},{7,448},{64,1... | collective-permute-start | bytes 153608 | tf_op jit(solution)/shard_map/ppermute | solution.py:361
  266.4 1.0 copy-start.7
  267.3 0.9 copy-start.8
Sparse Core Ops, SparseCore 0:
  57.2 26.3 all-gather.7
  85.7 56.9 all-gather.9
  184.4 35.5 reduce-scatter.4
  222.7 43.6 reduce-scatter.2

commit v2 on v1

v2 whole, which is shorter than its diff:
```python
import functools
import math

import jax
import jax.numpy as jnp
from jax import lax
from jax.experimental import pallas as pl
from jax.experimental.pallas import tpu as pltpu
from jax.sharding import Mesh, PartitionSpec as P

HD = 128
TT = 1025
PATCHES = 1024
KPAD = 1040
QPAD = 1152
QBLK = 384
PIECE = 16
NPIECE = 16
MAIN = 384
GROUP = 50
GPAD = 64
BF = jnp.bfloat16
F32 = jnp.float32
SHARDS = ("z", "x", "c")
SCALE = HD ** (-0.5)


def dot(left, right):
    return jnp.dot(left, right, preferred_element_type=F32)


def dot_last(left, right):
    return lax.dot_general(left, right, (((1,), (1,)), ((), ())), preferred_element_type=F32)


def dot_first(left, right):
    return lax.dot_general(left, right, (((0,), (0,)), ((), ())), preferred_element_type=F32)


def iota(shape, axis):
    return lax.broadcasted_iota(jnp.int32, shape, axis)


def params():
    return pltpu.CompilerParams(vmem_limit_bytes=50 * 1024 * 1024)


def pack_kernel(label_ref, x_ref, out_ref, rest_scr):
    slots = label_ref.shape[1]
    positions = x_ref.shape[2]
    lane = iota((16, positions), 1)
    slot = lane >> 4
    goal = jnp.full((16, positions), -1, jnp.int32)
    number = jnp.zeros((16, positions), jnp.int32)
    for s in range(slots):
        label = label_ref[0, s]
        goal = jnp.where(slot == s, label, goal)
    number = jnp.where(goal >= 0, (goal & 15) + 1, 0)
    goal = jnp.where(goal >= 0, (goal >> 4) * 16 + (lane & 15), -1)[0:1]
    rest_scr[...] = jnp.zeros(rest_scr.shape, BF)
    for k in range(4):
        rest_scr[16 * k : 16 * k + 16, :] = x_ref[k, MAIN : MAIN + 16, :]
    rest_scr[64:80, :] = jnp.where(iota((16, positions), 0) == 0, number, 0).astype(F32).astype(BF)
    step = 256
    for r in range(0, out_ref.shape[0] * PIECE, step):
        pick = jnp.where(iota((step, positions), 0) + r == goal, 1.0, 0.0).astype(BF)
        first = slice(r // PIECE, (r + step) // PIECE)
        for k in range(4):
            left = k * MAIN
            moved = dot_last(pick, x_ref[k, 0:MAIN, :]).astype(BF)
            out_ref[first, :, left : left + MAIN] = moved.reshape(step // PIECE, PIECE, MAIN)
        moved = dot_last(pick, rest_scr[...]).astype(BF)
        out_ref[first, :, 4 * MAIN :] = moved.reshape(step // PIECE, PIECE, 128)


def pack(labels, columns, peers):
    return pl.pallas_call(
        pack_kernel,
        out_shape=jax.ShapeDtypeStruct((peers, PIECE, 4 * MAIN + 128), BF),
        in_specs=[
            pl.BlockSpec(memory_space=pltpu.SMEM),
            pl.BlockSpec(memory_space=pltpu.VMEM),
        ],
        out_specs=pl.BlockSpec(memory_space=pltpu.VMEM),
        scratch_shapes=[pltpu.VMEM((128, columns.shape[2]), BF)],
        compiler_params=params(),
        name="pack_pieces",
    )(labels, columns)


def receive_kernel(source_ref, in_ref, weight_ref, rows_ref, part_ref, rest_scr, left_scr, stack_scr, weight_scr):
    @pl.when(pl.program_id(0) == 0)
    def _():
        for i in range(NPIECE):
            rest_scr[16 * i : 16 * i + 16, :] = in_ref[source_ref[i], :, 4 * MAIN :]
        rest = rest_scr[...]
        column = iota((MAIN, 8 * GPAD), 1)
        inside = (column & 63) < GROUP
        feature = (column >> 6) * GROUP + (column & 63)
        spread = jnp.where((feature == iota((MAIN, 8 * GPAD), 0)) & inside, 1.0, 0.0).astype(BF)
        row = iota((256, 256), 0)
        wanted = (row & 1) * 128 + (row >> 5) * 16 + ((row >> 1) & 15)
        order = jnp.where(iota((256, 256), 1) == wanted, 1.0, 0.0).astype(BF)
        lane = iota((128, 8 * GPAD), 0)
        for e in range(2):
            for u in range(2):
                k = 2 * e + u
                for i in range(NPIECE):
                    left_scr[16 * i : 16 * i + 16, :] = in_ref[source_ref[i], :, k * MAIN : (k + 1) * MAIN]
                spread_rest = jnp.where(
                    (feature[0:128] == lane + (MAIN - 16 * k)) & inside[0:128] & (lane >= 16 * k) & (lane < 16 * k + 16),
                    1.0,
                    0.0,
                ).astype(BF)
                wide = (dot(left_scr[...], spread) + dot(rest, spread_rest)).astype(BF)
                stack_scr[0, u * 128 : (u + 1) * 128, :] = wide[0:128]
                stack_scr[1, u * 128 : (u + 1) * 128, :] = wide[128:256]
            for half in range(2):
                lower = e * 512 + half * 256
                rows_ref[lower : lower + 256, :] = dot(order, stack_scr[half]).astype(BF)
        weight_scr[...] = jnp.zeros(weight_scr.shape, BF)

    for c in range(2):
        for x in range(4):
            lower = (2 * x + c) * GPAD
            weight_scr[lower : lower + GROUP, :] = weight_ref[c, x, 0]
    part_ref[0] = dot(rows_ref[...], weight_scr[...]).astype(BF)


def receive(source, arrived, weight):
    return pl.pallas_call(
        receive_kernel,
        grid=(8,),
        out_shape=(
            jax.ShapeDtypeStruct((1024, 512), BF),
            jax.ShapeDtypeStruct((8, 1024, 256), BF),
        ),
        in_specs=[
            pl.BlockSpec(memory_space=pltpu.SMEM),
            pl.BlockSpec(memory_space=pltpu.VMEM),
            pl.BlockSpec((2, 4, 1, GROUP, 256), lambda a: (0, 0, a, 0, 0)),
        ],
        out_specs=(
            pl.BlockSpec((1024, 512), lambda a: (0, 0)),
            pl.BlockSpec((1, 1024, 256), lambda a: (a, 0, 0)),
        ),
        scratch_shapes=[
            pltpu.VMEM((256, 128), BF),
            pltpu.VMEM((256, MAIN), BF),
            pltpu.VMEM((2, 256, 512), BF),
            pltpu.VMEM((8 * GPAD, 256), BF),
        ],
        compiler_params=params(),
        name="receive_pieces",
    )(source, arrived, weight)


def forward_kernel(x_ref, p_ref, att_ref, a_ref, q_scr, vt_scr, a_scr):
    tail_row = iota((16, 128), 0) == 0
    q_scr[0:1024, :] = x_ref[0, 0, 0:1024, :]
    q_scr[1024:QPAD, :] = jnp.zeros((128, 128), BF)
    q_scr[1024:1040, :] = jnp.where(tail_row, x_ref[0, 0, 1024:1025, :].astype(F32), 0.0).astype(BF)
    key = x_ref[0, 1, 0:1024, :]
    key_tail = jnp.where(tail_row, x_ref[0, 1, 1024:1025, :].astype(F32), 0.0).astype(BF)
    vt_scr[...] = x_ref[0, 2, 0:1024, :].astype(F32).T.astype(BF)
    value_tail = jnp.where(tail_row, x_ref[0, 2, 1024:1025, :].astype(F32), 0.0).astype(BF)
    first = iota((16, QBLK), 0) == 0
    for j in range(QPAD // QBLK):
        span = slice(j * QBLK, (j + 1) * QBLK)
        query = q_scr[span, :]
        score = dot_last(key, query) * SCALE
        score_tail = (dot_last(key_tail, query) * SCALE)[0:1]
        top = jnp.maximum(jnp.max(score, axis=0, keepdims=True), score_tail)
        shifted = jnp.exp(score - top)
        shifted_tail = jnp.exp(score_tail - top)
        inverse = 1.0 / (jnp.sum(shifted, axis=0, keepdims=True) + shifted_tail)
        low = (shifted * inverse).astype(BF)
        low_tail = jnp.where(first, shifted_tail * inverse, 0.0).astype(BF)
        p_ref[0, 0:1024, span] = low
        p_ref[0, 1024:KPAD, span] = low_tail
        att = (dot(vt_scr[...], low) + dot_first(value_tail, low_tail)).T.astype(BF)
        att_ref[span, :] = att
        a_scr[span, :] = att.astype(F32)
    moved = a_scr[pl.ds(1, 1024), :].astype(BF)
    for i in range(NPIECE):
        for e in range(2):
            a_ref[512 * e + 32 * i : 512 * e + 32 * i + 32, :] = moved[64 * i + 32 * e : 64 * i + 32 * e + 32]


def forward(head_inputs):
    return pl.pallas_call(
        forward_kernel,
        grid=(2,),
        out_shape=(
            jax.ShapeDtypeStruct((2, KPAD, QPAD), BF),
            jax.ShapeDtypeStruct((QPAD, 256), BF),
            jax.ShapeDtypeStruct((PATCHES, 256), BF),
        ),
        in_specs=[pl.BlockSpec((1, 3, TT, HD), lambda h: (0, 0, 0, h))],
        out_specs=(
            pl.BlockSpec((1, KPAD, QPAD), lambda h: (h, 0, 0)),
            pl.BlockSpec((QPAD, HD), lambda h: (0, h)),
            pl.BlockSpec((PATCHES, HD), lambda h: (0, h)),
        ),
        scratch_shapes=[
            pltpu.VMEM((QPAD, HD), BF),
            pltpu.VMEM((HD, 1024), BF),
            pltpu.VMEM((QPAD, HD), F32),
        ],
        compiler_params=params(),
        cost_estimate=pl.CostEstimate(flops=12 * 10**9, bytes_accessed=8 * 10**6, transcendentals=2 * 10**6),
        name="attend",
    )(head_inputs)


def backward_kernel(x_ref, p_ref, att_ref, o_ref, out_ref, q_scr, kt_scr, g_scr, dq_scr, dk_scr, dv_scr, dkt_scr, dvt_scr):
    tail_row = iota((16, 128), 0) == 0
    q_scr[0:1024, :] = x_ref[0, 0, 0:1024, :]
    q_scr[1024:QPAD, :] = jnp.zeros((128, 128), BF)
    q_scr[1024:1040, :] = jnp.where(tail_row, x_ref[0, 0, 1024:1025, :].astype(F32), 0.0).astype(BF)
    kt_scr[...] = x_ref[0, 1, 0:1024, :].astype(F32).T.astype(BF)
    key_tail = jnp.where(tail_row, x_ref[0, 1, 1024:1025, :].astype(F32), 0.0).astype(BF)
    value = x_ref[0, 2, 0:1024, :]
    value_tail = jnp.where(tail_row, x_ref[0, 2, 1024:1025, :].astype(F32), 0.0).astype(BF)
    g_scr[0:8, :] = jnp.zeros((8, HD), F32)
    g_scr[1024 : QPAD, :] = jnp.zeros((QPAD - 1024, HD), F32)
    for i in range(NPIECE):
        g_scr[pl.ds(1 + 64 * i, 32), :] = o_ref[32 * i : 32 * i + 32, :].astype(F32)
        g_scr[pl.ds(33 + 64 * i, 32), :] = o_ref[512 + 32 * i : 544 + 32 * i, :].astype(F32)
    for j in range(QPAD // QBLK):
        span = slice(j * QBLK, (j + 1) * QBLK)
        query = q_scr[span, :]
        grad_wide = g_scr[span, :]
        grad = grad_wide.astype(BF)
        delta = jnp.sum((grad_wide * att_ref[span, :].astype(F32)).T, axis=0, keepdims=True)
        low = p_ref[0, 0:1024, span]
        low_tail = p_ref[0, 1024:KPAD, span]
        inner = (low.astype(F32) * (dot_last(value, grad) - delta)).astype(BF)
        inner_tail = (low_tail.astype(F32) * (dot_last(value_tail, grad) - delta)).astype(BF)
        dq = (dot(kt_scr[...], inner) + dot_first(key_tail, inner_tail)) * SCALE
        dq_scr[span, :] = dq.T.astype(BF)
        dk, dkt = dot(inner, query), dot(inner_tail, query)
        dv, dvt = dot(low, grad), dot(low_tail, grad)
        if j == 0:
            dk_scr[...], dkt_scr[...], dv_scr[...], dvt_scr[...] = dk, dkt, dv, dvt
        else:
            dk_scr[...] += dk
            dkt_scr[...] += dkt
            dv_scr[...] += dv
            dvt_scr[...] += dvt
    out_ref[0, 0, 0:1024, :] = dq_scr[0:1024, :]
    out_ref[0, 0, 1024:1025, :] = dq_scr[1024:1040, :][0:1]
    out_ref[0, 1, 0:1024, :] = (dk_scr[...] * SCALE).astype(BF)
    out_ref[0, 1, 1024:1025, :] = (dkt_scr[...] * SCALE).astype(BF)[0:1]
    out_ref[0, 2, 0:1024, :] = dv_scr[...].astype(BF)
    out_ref[0, 2, 1024:1025, :] = dvt_scr[...].astype(BF)[0:1]


def backward(head_inputs, probs, att, out_grad):
    return pl.pallas_call(
        backward_kernel,
        grid=(2,),
        out_shape=jax.ShapeDtypeStruct((1, 3, TT, 256), BF),
        in_specs=[
            pl.BlockSpec((1, 3, TT, HD), lambda h: (0, 0, 0, h)),
            pl.BlockSpec((1, KPAD, QPAD), lambda h: (h, 0, 0)),
            pl.BlockSpec((QPAD, HD), lambda h: (0, h)),
            pl.BlockSpec((PATCHES, HD), lambda h: (0, h)),
        ],
        out_specs=pl.BlockSpec((1, 3, TT, HD), lambda h: (0, 0, 0, h)),
        scratch_shapes=[
            pltpu.VMEM((QPAD, HD), BF),
            pltpu.VMEM((HD, 1024), BF),
            pltpu.VMEM((QPAD, HD), F32),
            pltpu.VMEM((QPAD, HD), BF),
            pltpu.VMEM((1024, HD), F32),
            pltpu.VMEM((1024, HD), F32),
            pltpu.VMEM((16, HD), F32),
            pltpu.VMEM((16, HD), F32),
        ],
        compiler_params=params(),
        name="attend_backward",
    )(head_inputs, probs, att, out_grad)


def weight_kernel(core_ref, r_ref, a_ref, keep_ref, send_ref, t_scr, sum_scr):
    @pl.when(pl.program_id(0) == 0)
    def _():
        t_scr[...] = r_ref[...].astype(F32).T.astype(BF)

    sum_scr[...] = dot(t_scr[...], a_ref[0])
    core = core_ref[0]
    for x in range(4):
        mine = pl.multiple_of((2 * x + core) * GPAD, GPAD)
        other = pl.multiple_of((2 * x + 1 - core) * GPAD, GPAD)
        keep_ref[0, x] = sum_scr[pl.ds(mine, GPAD), :][0:GROUP]
        send_ref[0, x] = sum_scr[pl.ds(other, GPAD), :][0:GROUP].astype(BF)


def weight_parts(core, rows, gathered):
    return pl.pallas_call(
        weight_kernel,
        grid=(8,),
        out_shape=(
            jax.ShapeDtypeStruct((8, 4, GROUP, 256), F32),
            jax.ShapeDtypeStruct((8, 4, GROUP, 256), BF),
        ),
        in_specs=[
            pl.BlockSpec(memory_space=pltpu.SMEM),
            pl.BlockSpec((1024, 512), lambda a: (0, 0)),
            pl.BlockSpec((1, PATCHES, 256), lambda a: (a, 0, 0)),
        ],
        out_specs=(
            pl.BlockSpec((1, 4, GROUP, 256), lambda a: (a, 0, 0, 0)),
            pl.BlockSpec((1, 4, GROUP, 256), lambda a: (a, 0, 0, 0)),
        ),
        scratch_shapes=[
            pltpu.VMEM((512, 1024), BF),
            pltpu.VMEM((512, 256), F32),
        ],
        compiler_params=params(),
        name="weight_parts",
    )(core, rows, gathered)


def per_device(head_inputs, out_weight, sequence_gradient, slot_labels):
    peers = 64
    swap = [(z * 8 + y, y * 8 + z) for z in range(8) for y in range(8)]
    weight = lax.ppermute(out_weight, ("z", "y"), swap)
    outgoing = pack(slot_labels, sequence_gradient.transpose(0, 2, 1), peers)
    outgoing, weight = lax.optimization_barrier((outgoing, weight))
    weight = lax.all_to_all(jnp.broadcast_to(weight[None], (8, GROUP, 256)), "z", 0, 0, tiled=True)
    probs, att, parts = forward(head_inputs)
    outgoing, weight, parts = lax.optimization_barrier((outgoing, weight, parts))

    arrived = lax.all_to_all(outgoing, SHARDS, 0, 0, tiled=True)
    weight = lax.all_gather(weight, ("c", "x"), axis=0)
    weight = weight.reshape(2, 4, 8, GROUP, 256)
    gathered = lax.all_gather(parts, "y", axis=0)

    ids = arrived[:, 0, 4 * MAIN + 64].astype(jnp.int32) - 1
    wanted = jnp.arange(NPIECE, dtype=jnp.int32)
    source = jnp.sum(
        jnp.where(ids[None, :] == wanted[:, None], jnp.arange(peers, dtype=jnp.int32)[None, :], 0), axis=1
    )
    rows, part = receive(source, arrived, weight)
    out_grad = lax.psum_scatter(part, "y", scatter_dimension=0, tiled=True)[0]

    core = lax.axis_index("c").astype(jnp.int32)[None]
    keep, send = weight_parts(core, rows, gathered)
    got = lax.ppermute(send, "c", [(0, 1), (1, 0)])
    both = (keep + got.astype(F32)).astype(BF).reshape(32, GROUP, 256)
    spread = lax.all_to_all(both, ("z", "x"), 0, 0, tiled=True)
    summed = jnp.sum(spread.astype(F32), axis=0) * (1.0 / math.sqrt(65536))
    weight_gradient = lax.ppermute(summed, ("z", "y"), swap)

    head_gradient = backward(head_inputs, probs, att, out_grad)
    return head_gradient, weight_gradient


def solution(mesh):
    fine = Mesh(mesh.devices.reshape(8, 4, 2, 8), ("z", "x", "c", "y"))
    return jax.shard_map(
        per_device,
        mesh=fine,
        in_specs=(
            P(SHARDS, None, None, "y"),
            P(SHARDS, "y"),
            P(None, SHARDS, "y"),
            P(SHARDS, None),
        ),
        out_specs=(P(SHARDS, None, None, "y"), P(SHARDS, "y")),
        check_vma=False,
    )
```

time: 289 us -> 226 us (0.78); the launches traced: 285 us -> 225 us
  blocking collectives: 139 us -> 29 us
  waiting for transfers between devices: 69 us -> 96 us
  starting transfers between devices: 12.8 us -> 34.2 us
    all_to_all x1 -> x0, blocking collectives: 62.5 us -> none  [per_device(): in0 = lax.all_to_all(out0, SHARDS, 0, 0, tiled=True)]
    all_gather x2 -> x0, blocking collectives: 48.2 us -> none  [the longest x1 36.5 us: per_device(): weight = lax.all_gather(weight, 'z', axis=0)]
    all_gather x1, waiting for transfers between devices: 0.02 us -> 30.3 us  [per_device(): weight = lax.all_gather(weight, ('c', 'x'), axis=0)]
    all_to_all x1 -> x2, starting transfers between devices: 6.8 us -> 28.1 us  [the longest x1 16 us: per_device(): lax.all_to_all(jnp.broadcast_to(weight[None], (8, GROUP, 256)), 'z', 0, 0...]
    reduce_scatter x2 -> x1, waiting for transfers between devices: 38.6 us -> 17.5 us  [per_device(): out_grad = lax.psum_scatter(part, 'y', scatter_dimension=0, tiled=True)[0]]
    all_to_all x1 -> x2, waiting for transfers between devices: 28 us -> 45.7 us  [the longest x1 45.4 us: per_device(): arrived = lax.all_to_all(outgoing, SHARDS, 0, 0, tiled=True)]
    unnamed x25 -> x17, local copies, waits for them, and re-layouts: 8.91 us -> 6.72 us
    pallas_call x3 -> x2, Pallas kernels: 12.6 us -> 14 us  [the longest x1 9.13 us: receive(): pl.pallas_call(receive_kernel, grid=(8,), out_shape=(jax.ShapeDtypeStruct...]
  transfers between devices with their start and end apart: 8 -> 8, of which waited for: 3 -> 5; matrix products, arithmetic and copies ran while one was open for 3% -> 3% of each run, Pallas kernels for 13% -> 13%
where the time goes in v2:
time: 226 us; the launch traced here: 225 us
  waiting for transfers between devices  96 us (42%)
  Pallas kernels  38.2 us (17%)
  starting transfers between devices  34.2 us (15%)
  blocking collectives  29 us (13%)
  between operations  13.8 us (6%)
  local copies, waits for them, and re-layouts  10.9 us (5%)
  other arithmetic  2.87 us (1%)
    all_to_all x1, waiting for transfers between devices, per_device(): arrived = lax.all_to_all(outgoing, SHARDS, 0, 0, tiled=True)  45.4 us
    all_gather x1, waiting for transfers between devices, per_device(): weight = lax.all_gather(weight, ('c', 'x'), axis=0)  30.3 us
    all_to_all x1, blocking collectives, per_device(): spread = lax.all_to_all(both, ('z', 'x'), 0, 0, tiled=True)  29 us
    reduce_scatter x1, waiting for transfers between devices, per_device(): out_grad = lax.psum_scatter(part, 'y', scatter_dimension=0, tiled=True)[0]  17.5 us
    all_to_all x1, starting transfers between devices, per_device(): lax.all_to_all(jnp.broadcast_to(weight[None], (8, GROUP, 256)), 'z', 0, 0...  16 us
    all_to_all x1, starting transfers between devices, per_device(): arrived = lax.all_to_all(outgoing, SHARDS, 0, 0, tiled=True)  12.1 us
    pallas_call x1, Pallas kernels, backward(): pl.pallas_call(backward_kernel, grid=(2,), out_shape=jax.ShapeDtypeStruct...  9.33 us
    pallas_call x1, Pallas kernels, receive(): pl.pallas_call(receive_kernel, grid=(8,), out_shape=(jax.ShapeDtypeStruct...  9.13 us
  transfers between devices with their start and end apart: 8, of which 5 were waited for; matrix products, arithmetic and copies ran while one was open for 3% of the time, Pallas kernels for 13%

profile of v2, /device:TPU:1, one launch (start us, length us, event | category | flops | bytes accessed | tf_op | source)
XLA Modules:
  0.0 225.2 jit_solution(2742538132423918268)
XLA Ops:
  7.2 1.4 collective-permute-start
  8.6 1.4 copy-done
  10.0 0.7 copy-done.7
  10.7 4.9 %pack_pieces.1 = bf16[64,16,1664]{2,1,0:T(8,128)(2,1)} custom-call(s32[1,32]{1,0:T(1,128)S(1)} %copy-done.7, bf16[4,400,512]{2,1,0:T(8,128)(2,1)S(1)} %bitcast.7), custom_call_target="tpu_custom_call" | custom-call | tf_op jit(solution)/shard_map/pack_pieces/pallas_call | solution.py:77
  15.6 0.7 broadcast_in_dim.24
  16.3 16.0 %all-to-all-start = ((bf16[8,50,256]{2,1,0:T(8,128)(2,1)}), bf16[8,50,256]{2,1,0:T(8,128)(2,1)S(1)}, u32[]{:S(2)}, u32[]{:S(2)}) async-start(bf16[8,50,256]{2,1,0:T(8,128)(2,1)} %broadcast_in_dim.24), calls=%async_computation | async-start | bytes 458752 | tf_op jit(solution)/shard_map/all_to_all | solution.py:332
  32.3 7.9 %attend.1 = (bf16[2,1040,1152]{2,1,0:T(8,128)(2,1)}, bf16[1152,256]{1,0:T(8,128)(2,1)S(1)}, bf16[1024,256]{1,0:T(8,128)(2,1)}) custom-call(bf16[1,3,1025,256]{3,2,1,0:T(8,128)(2,1)S(1)} %copy-done.1), custom_call_target="tpu_custom_call" | custom-call | flops 12000000000 | bytes 8000000 | tf_op jit(solution)/shard_map/attend/pallas_call | solution.py:191
  40.2 0.8 copy-done.4
  41.0 0.3 all-to-all-done
  41.3 0.7 copy.13
  42.1 0.7 all-gather.7.cloned.1.call-update
  42.8 12.1 %all-to-all-start.1 = ((bf16[64,16,1664]{2,1,0:T(8,128)(2,1)}), bf16[64,16,1664]{2,1,0:T(8,128)(2,1)}, u32[]{:S(2)}, u32[]{:S(2)}) async-start(bf16[64,16,1664]{2,1,0:T(8,128)(2,1)} %pack_pieces.1), calls=%async_computation.1 | async-start | bytes 6815744 | tf_op jit(solution)/shard_map/all_to_all | solution.py:336
  55.0 30.3 %all-gather.5.cloned.1.call-done = bf16[64,50,256]{2,0,1:T(8,128)(2,1)} async-done(((bf16[8,50,256]{2,0,1:T(8,128)(2,1)}), bf16[64,50,256]{2,0,1:T(8,128)(2,1)}) %all-gather.5.cloned.1.call-update) | async-done | bytes 1638416 | tf_op jit(solution)/shard_map/all_gather | solution.py:337
  85.3 2.4 %copy.14 = bf16[64,50,256]{2,1,0:T(8,128)(2,1)S(1)} copy(bf16[64,50,256]{2,0,1:T(8,128)(2,1)} %all-gather.5.cloned.1.call-done) | data formatting | bytes 3276800 | tf_op jit(solution)/shard_map/all_gather | solution.py:337
  87.7 45.4 %all-to-all-done.1.in_ref = bf16[64,16,1664]{2,1,0:T(8,128)(2,1)} async-done(((bf16[64,16,1664]{2,1,0:T(8,128)(2,1)}), bf16[64,16,1664]{2,1,0:T(8,128)(2,1)}, u32[]{:S(2)}, u32[]{:S(2)}) %all-to-all-start.1) | async-done | bytes 3407904 | tf_op jit(solution)/shard_map/all_to_all | solution.py:336
  133.1 2.2 fusion.1
  135.3 0.1 select_reduce_fusion.source_ref
  135.4 9.1 %receive_pieces.1 = (bf16[1024,512]{1,0:T(8,128)(2,1)S(1)}, bf16[8,1024,256]{2,1,0:T(8,128)(2,1)}) custom-call(s32[16]{0:T(128)S(1)} %select_reduce_fusion.source_ref, bf16[64,16,1664]{2,1,0:T(8,128)(2,1)} %all-to-all-done.1.in_ref, bf16[2,4,8,50,256]{4,3,2,1,0:T(8,128)(2,1)S(1)} %bitcast.6), custom_call_target="tpu_custom_call" | custom-call | tf_op jit(solution)/shard_map/receive_pieces/pallas_call | solution.py:131
  144.5 1.0 copy-done.2
  145.6 1.2 copy-done.3
  146.7 7.0 %weight_parts.1 = (f32[8,4,50,256]{3,2,1,0:T(8,128)S(1)}, bf16[8,4,50,256]{3,2,1,0:T(8,128)(2,1)S(1)}) custom-call(s32[1]{0:T(128)} %bitcast.3.core_ref, bf16[1024,512]{1,0:T(8,128)(2,1)S(1)} %copy-done.3, bf16[8,1024,256]{2,1,0:T(8,128)(2,1)} %bitcast.9), custom_call_target="tpu_custom_call" | custom-call | tf_op jit(solution)/shard_map/weight_parts/pallas_call | solution.py:301
  153.8 0.5 copy.15
  154.2 3.9 %collective-permute-start.1 = (bf16[8,4,50,256]{3,0,2,1:T(8,128)(2,1)S(1)}, bf16[8,4,50,256]{3,0,2,1:T(8,128)(2,1)S(1)}, u32[]{:S(2)}, u32[]{:S(2)}) collective-permute-start(bf16[8,4,50,256]{3,0,2,1:T(8,128)(2,1)S(1)} %copy.15), channel_id=1, source_target_pairs={{0,8},{8,0},{1,9},{9,1},{2,10},{10,2},{3,11},{11,3},{4,12},{12,4},... | collective-permute-start | bytes 2457608 | tf_op jit(solution)/shard_map/ppermute | solution.py:351
  158.1 1.8 collective-permute-done.1
  159.9 0.4 add_convert_fusion
  160.3 29.0 %all_to_all.15 = bf16[32,50,256]{2,1,0:T(8,128)(2,1)S(1)} all-to-all(bf16[32,50,256]{2,1,0:T(8,128)(2,1)S(1)} %bitcast.10), channel_id=1, replica_groups=mesh['z'=8,'x'=4,'c'=2,'y'=8] {'z','x'}, dimensions={0} | all-to-all | bytes 1638400 | tf_op jit(solution)/shard_map/all_to_all | solution.py:353
  189.3 0.1 convert_reduce_fusion
  189.5 0.7 collective-permute-start.2
  190.2 17.5 %reduce-scatter.2.cloned.1.call-done = bf16[1,1024,256]{2,1,0:T(8,128)(2,1)} async-done(((bf16[8,1024,256]{2,1,0:T(8,128)(2,1)}), bf16[1,1024,256]{2,1,0:T(8,128)(2,1)}) %reduce-scatter.2.cloned.1.call-update) | async-done | bytes 524304 | tf_op jit(solution)/shard_map/reduce_scatter | solution.py:347
  207.6 1.0 copy-done.6
  208.7 9.3 %attend_backward.1 = bf16[1,3,1025,256]{3,2,1,0:T(8,128)(2,1)} custom-call(bf16[1,3,1025,256]{3,2,1,0:T(8,128)(2,1)S(1)} %copy-done.1, bf16[2,1040,1152]{2,1,0:T(8,128)(2,1)} %get-tuple-element.14.p_ref, bf16[1152,256]{1,0:T(8,128)(2,1)S(1)} %copy-done.5, bf16[1024,256]{1,0:T(8,128)(2,1)S(1)} %bitcast.8), custom_call_target="tpu_custom_call" | custom-call | tf_op jit(solution)/shard_map/attend_backward/pallas_call | solution.py:260
  218.0 0.6 copy.19
  (19 shorter events, 0.2 us)
Async XLA Ops:
  7.2 8.4 %collective-permute-start = (bf16[50,256]{1,0:T(8,128)(2,1)}, bf16[50,256]{1,0:T(8,128)(2,1)S(1)}, u32[]{:S(2)}, u32[]{:S(2)}) collective-permute-start(bf16[50,256]{1,0:T(8,128)(2,1)} %param.5), channel_id=1, source_target_pairs={{0,0},{1,64},{2,128},{3,192},{4,256},{5,320},{6,384},{7,448},{64,1... | collective-permute-start | bytes 76808 | tf_op jit(solution)/shard_map/ppermute | solution.py:329
  8.6 1.4 copy-start
  10.0 0.7 copy-start.7
  10.7 21.6 %copy-start.1 = (bf16[1,3,1025,256]{3,2,1,0:T(8,128)(2,1)S(1)}, bf16[1,3,1025,256]{3,2,1,0:T(8,128)(2,1)}, u32[]{:S(2)}) copy-start(bf16[1,3,1025,256]{3,2,1,0:T(8,128)(2,1)} %x_ref.3) | copy-start | bytes 4723204
  16.3 25.1 %all-to-all-start = ((bf16[8,50,256]{2,1,0:T(8,128)(2,1)}), bf16[8,50,256]{2,1,0:T(8,128)(2,1)S(1)}, u32[]{:S(2)}, u32[]{:S(2)}) async-start(bf16[8,50,256]{2,1,0:T(8,128)(2,1)} %broadcast_in_dim.24), calls=%async_computation | async-start | bytes 458752 | tf_op jit(solution)/shard_map/all_to_all | solution.py:332
  32.2 53.1 %all-gather.5.cloned.1.call-start = ((), (), s32[]{:S(2)}) async-start(), calls=%async_computation.5 | async-start | bytes 1843200 | tf_op jit(solution)/shard_map/all_gather | solution.py:337
  40.2 0.8 copy-start.4
  42.1 103.5 %all-gather.7.cloned.1.call-start = ((), (), s32[]{:S(2)}) async-start(), calls=%async_computation.6 | async-start | bytes 4718592 | tf_op jit(solution)/shard_map/all_gather | solution.py:339
  42.8 90.3 %all-to-all-start.1 = ((bf16[64,16,1664]{2,1,0:T(8,128)(2,1)}), bf16[64,16,1664]{2,1,0:T(8,128)(2,1)}, u32[]{:S(2)}, u32[]{:S(2)}) async-start(bf16[64,16,1664]{2,1,0:T(8,128)(2,1)} %pack_pieces.1), calls=%async_computation.1 | async-start | bytes 6815744 | tf_op jit(solution)/shard_map/all_to_all | solution.py:336
  55.0 152.7 %reduce-scatter.2.cloned.1.call-start = ((), (), s32[]{:S(2)}) async-start(), calls=%async_computation.4 | async-start | bytes 4718592 | tf_op jit(solution)/shard_map/reduce_scatter | solution.py:347
  144.5 1.0 copy-start.2
  145.5 1.2 copy-start.3
  154.2 5.7 %collective-permute-start.1 = (bf16[8,4,50,256]{3,0,2,1:T(8,128)(2,1)S(1)}, bf16[8,4,50,256]{3,0,2,1:T(8,128)(2,1)S(1)}, u32[]{:S(2)}, u32[]{:S(2)}) collective-permute-start(bf16[8,4,50,256]{3,0,2,1:T(8,128)(2,1)S(1)} %copy.15), channel_id=1, source_target_pairs={{0,8},{8,0},{1,9},{9,1},{2,10},{10,2},{3,11},{11,3},{4,12},{12,4},... | collective-permute-start | bytes 2457608 | tf_op jit(solution)/shard_map/ppermute | solution.py:351
  160.3 47.4 %copy-start.5 = (bf16[1152,256]{1,0:T(8,128)(2,1)S(1)}, bf16[1152,256]{1,0:T(8,128)(2,1)}, u32[]{:S(2)}) copy-start(bf16[1152,256]{1,0:T(8,128)(2,1)} %copy-done.4) | copy-start | bytes 1769476
  189.5 0.7 collective-permute-start.2
  207.6 1.0 copy-start.6
Sparse Core Ops, SparseCore 0:
  42.2 43.0 all-gather.4
  87.4 55.6 all-gather.6
  146.0 61.6 reduce-scatter.1

commit v3 on v2

v3 whole, which is shorter than its diff:
```python
import functools
import math

import jax
import jax.numpy as jnp
from jax import lax
from jax.experimental import pallas as pl
from jax.experimental.pallas import tpu as pltpu
from jax.sharding import Mesh, PartitionSpec as P

HD = 128
TT = 1025
PATCHES = 1024
KPAD = 1040
QPAD = 1152
QBLK = 384
PIECE = 16
NPIECE = 16
MAIN = 384
GROUP = 50
GPAD = 64
GSEND = 56
BF = jnp.bfloat16
F32 = jnp.float32
SHARDS = ("z", "x", "c")
SCALE = HD ** (-0.5)


def dot(left, right):
    return jnp.dot(left, right, preferred_element_type=F32)


def dot_last(left, right):
    return lax.dot_general(left, right, (((1,), (1,)), ((), ())), preferred_element_type=F32)


def dot_first(left, right):
    return lax.dot_general(left, right, (((0,), (0,)), ((), ())), preferred_element_type=F32)


def iota(shape, axis):
    return lax.broadcasted_iota(jnp.int32, shape, axis)


def params(mebibytes):
    return pltpu.CompilerParams(vmem_limit_bytes=mebibytes * 1024 * 1024)


def pack_kernel(label_ref, x_ref, out_ref, rest_scr, goal_scr):
    positions = x_ref.shape[2]

    @pl.when(pl.program_id(0) == 0)
    def _():
        lane = iota((16, positions), 1)
        slot = lane >> 4
        goal = jnp.full((16, positions), -1, jnp.int32)
        for s in range(label_ref.shape[1]):
            goal = jnp.where(slot == s, label_ref[0, s], goal)
        number = jnp.where(goal >= 0, (goal & 15) + 1, 0)
        goal_scr[...] = jnp.where(goal >= 0, (goal >> 4) * 16 + (lane & 15), -1)
        rest_scr[...] = jnp.zeros(rest_scr.shape, BF)
        for k in range(4):
            rest_scr[16 * k : 16 * k + 16, :] = x_ref[k, MAIN : MAIN + 16, :]
        rest_scr[64:80, :] = jnp.where(iota((16, positions), 0) == 0, number, 0).astype(F32).astype(BF)

    step = out_ref.shape[0] * PIECE
    row = iota((step, positions), 0) + pl.program_id(0) * step
    pick = jnp.where(row == goal_scr[0:1, :], 1.0, 0.0).astype(BF)
    for k in range(4):
        moved = dot_last(pick, x_ref[k, 0:MAIN, :]).astype(BF)
        out_ref[:, :, k * MAIN : (k + 1) * MAIN] = moved.reshape(step // PIECE, PIECE, MAIN)
    moved = dot_last(pick, rest_scr[...]).astype(BF)
    out_ref[:, :, 4 * MAIN :] = moved.reshape(step // PIECE, PIECE, 128)


def pack(labels, columns, peers):
    features, positions = columns.shape[1:]
    return pl.pallas_call(
        pack_kernel,
        grid=(4,),
        out_shape=jax.ShapeDtypeStruct((peers, PIECE, 4 * MAIN + 128), BF),
        in_specs=[
            pl.BlockSpec(memory_space=pltpu.SMEM),
            pl.BlockSpec((4, features, positions), lambda r: (0, 0, 0)),
        ],
        out_specs=pl.BlockSpec((peers // 4, PIECE, 4 * MAIN + 128), lambda r: (r, 0, 0)),
        scratch_shapes=[pltpu.VMEM((128, positions), BF), pltpu.VMEM((16, positions), jnp.int32)],
        compiler_params=params(60),
        name="pack_pieces",
    )(labels, columns)


def assemble_kernel(in_ref, out_ref):
    out_ref[...] = jnp.zeros(out_ref.shape, BF)
    for a in range(8):
        for g in range(8):
            out_ref[a, g * GPAD : g * GPAD + GROUP, :] = in_ref[8 * a + g]


def assemble(arrived):
    vmem = pl.BlockSpec(memory_space=pltpu.VMEM)
    return pl.pallas_call(
        assemble_kernel,
        out_shape=jax.ShapeDtypeStruct((8, 8 * GPAD, 256), BF),
        in_specs=[vmem],
        out_specs=vmem,
        compiler_params=params(24),
        cost_estimate=pl.CostEstimate(flops=48 * 10**9, bytes_accessed=4 * 10**6, transcendentals=0),
        name="assemble_weight",
    )(arrived)


def receive_kernel(in_ref, weight_ref, rows_ref, part_ref, placed_scr, stack_scr):
    @pl.when(pl.program_id(0) == 0)
    def _():
        slots = in_ref.shape[0]
        numbers = in_ref[:, 4 * MAIN :].astype(F32).T[64:65]
        row = iota((256, slots), 0)
        wanted = (numbers == ((row >> 4) + 1).astype(F32)) & ((iota((256, slots), 1) & 15) == (row & 15))
        pick = jnp.where(wanted, 1.0, 0.0).astype(BF)
        for left in range(0, 4 * MAIN, MAIN):
            placed_scr[:, left : left + MAIN] = dot(pick, in_ref[:, left : left + MAIN]).astype(BF)
        rest = dot(pick, in_ref[:, 4 * MAIN :]).astype(BF)
        column = iota((MAIN, 8 * GPAD), 1)
        inside = (column & 63) < GROUP
        feature = (column >> 6) * GROUP + (column & 63)
        spread = jnp.where((feature == iota((MAIN, 8 * GPAD), 0)) & inside, 1.0, 0.0).astype(BF)
        row = iota((256, 256), 0)
        source = (row & 1) * 128 + (row >> 5) * 16 + ((row >> 1) & 15)
        order = jnp.where(iota((256, 256), 1) == source, 1.0, 0.0).astype(BF)
        lane = iota((128, 8 * GPAD), 0)
        for e in range(2):
            for u in range(2):
                k = 2 * e + u
                spread_rest = jnp.where(
                    (feature[0:128] == lane + (MAIN - 16 * k)) & inside[0:128] & (lane >= 16 * k) & (lane < 16 * k + 16),
                    1.0,
                    0.0,
                ).astype(BF)
                wide = (dot(placed_scr[:, k * MAIN : (k + 1) * MAIN], spread) + dot(rest, spread_rest)).astype(BF)
                stack_scr[0, u * 128 : (u + 1) * 128, :] = wide[0:128]
                stack_scr[1, u * 128 : (u + 1) * 128, :] = wide[128:256]
            for half in range(2):
                lower = e * 512 + half * 256
                rows_ref[lower : lower + 256, :] = dot(order, stack_scr[half]).astype(BF)

    for a in range(2):
        part_ref[a] = dot(rows_ref[...], weight_ref[a]).astype(BF)


def receive(arrived, weight):
    slots = arrived.shape[0]
    return pl.pallas_call(
        receive_kernel,
        grid=(4,),
        out_shape=(
            jax.ShapeDtypeStruct((1024, 512), BF),
            jax.ShapeDtypeStruct((8, 1024, 256), BF),
        ),
        in_specs=[
            pl.BlockSpec(memory_space=pltpu.VMEM),
            pl.BlockSpec((2, 8 * GPAD, 256), lambda a: (a, 0, 0)),
        ],
        out_specs=(
            pl.BlockSpec((1024, 512), lambda a: (0, 0)),
            pl.BlockSpec((2, 1024, 256), lambda a: (a, 0, 0)),
        ),
        scratch_shapes=[
            pltpu.VMEM((256, 4 * MAIN), BF),
            pltpu.VMEM((2, 256, 512), BF),
        ],
        compiler_params=params(60),
        name="receive_pieces",
    )(arrived, weight)


def forward_kernel(x_ref, p_ref, att_ref, a_ref, q_scr, vt_scr, a_scr):
    tail_row = iota((16, 128), 0) == 0
    q_scr[0:1024, :] = x_ref[0, 0, 0:1024, :]
    q_scr[1024:QPAD, :] = jnp.zeros((128, 128), BF)
    q_scr[1024:1040, :] = jnp.where(tail_row, x_ref[0, 0, 1024:1025, :].astype(F32), 0.0).astype(BF)
    key = x_ref[0, 1, 0:1024, :]
    key_tail = jnp.where(tail_row, x_ref[0, 1, 1024:1025, :].astype(F32), 0.0).astype(BF)
    vt_scr[...] = x_ref[0, 2, 0:1024, :].astype(F32).T.astype(BF)
    value_tail = jnp.where(tail_row, x_ref[0, 2, 1024:1025, :].astype(F32), 0.0).astype(BF)
    first = iota((16, QBLK), 0) == 0
    for j in range(QPAD // QBLK):
        span = slice(j * QBLK, (j + 1) * QBLK)
        query = q_scr[span, :]
        score = dot_last(key, query) * SCALE
        score_tail = (dot_last(key_tail, query) * SCALE)[0:1]
        top = jnp.maximum(jnp.max(score, axis=0, keepdims=True), score_tail)
        shifted = jnp.exp(score - top)
        shifted_tail = jnp.exp(score_tail - top)
        inverse = 1.0 / (jnp.sum(shifted, axis=0, keepdims=True) + shifted_tail)
        low = (shifted * inverse).astype(BF)
        low_tail = jnp.where(first, shifted_tail * inverse, 0.0).astype(BF)
        p_ref[0, 0:1024, span] = low
        p_ref[0, 1024:KPAD, span] = low_tail
        att = (dot(vt_scr[...], low) + dot_first(value_tail, low_tail)).T.astype(BF)
        att_ref[span, :] = att
        a_scr[span, :] = att.astype(F32)
    moved = a_scr[pl.ds(1, 1024), :].astype(BF)
    for i in range(NPIECE):
        for e in range(2):
            a_ref[512 * e + 32 * i : 512 * e + 32 * i + 32, :] = moved[64 * i + 32 * e : 64 * i + 32 * e + 32]


def forward(head_inputs):
    return pl.pallas_call(
        forward_kernel,
        grid=(2,),
        out_shape=(
            jax.ShapeDtypeStruct((2, KPAD, QPAD), BF),
            jax.ShapeDtypeStruct((QPAD, 256), BF),
            jax.ShapeDtypeStruct((PATCHES, 256), BF),
        ),
        in_specs=[pl.BlockSpec((1, 3, TT, HD), lambda h: (0, 0, 0, h))],
        out_specs=(
            pl.BlockSpec((1, KPAD, QPAD), lambda h: (h, 0, 0)),
            pl.BlockSpec((QPAD, HD), lambda h: (0, h)),
            pl.BlockSpec((PATCHES, HD), lambda h: (0, h)),
        ),
        scratch_shapes=[
            pltpu.VMEM((QPAD, HD), BF),
            pltpu.VMEM((HD, 1024), BF),
            pltpu.VMEM((QPAD, HD), F32),
        ],
        compiler_params=params(50),
        cost_estimate=pl.CostEstimate(flops=2 * 10**9, bytes_accessed=8 * 10**6, transcendentals=2 * 10**6),
        name="attend",
    )(head_inputs)


def backward_kernel(x_ref, p_ref, att_ref, o_ref, out_ref, q_scr, kt_scr, g_scr):
    tail_row = iota((16, 128), 0) == 0
    q_scr[0:1024, :] = x_ref[0, 0, 0:1024, :]
    q_scr[1024:QPAD, :] = jnp.zeros((128, 128), BF)
    q_scr[1024:1040, :] = jnp.where(tail_row, x_ref[0, 0, 1024:1025, :].astype(F32), 0.0).astype(BF)
    kt_scr[...] = x_ref[0, 1, 0:1024, :].astype(F32).T.astype(BF)
    key_tail = jnp.where(tail_row, x_ref[0, 1, 1024:1025, :].astype(F32), 0.0).astype(BF)
    value = x_ref[0, 2, 0:1024, :]
    value_tail = jnp.where(tail_row, x_ref[0, 2, 1024:1025, :].astype(F32), 0.0).astype(BF)
    g_scr[0:8, :] = jnp.zeros((8, HD), F32)
    g_scr[1024 : QPAD, :] = jnp.zeros((QPAD - 1024, HD), F32)
    for i in range(NPIECE):
        g_scr[pl.ds(1 + 64 * i, 32), :] = o_ref[32 * i : 32 * i + 32, :].astype(F32)
        g_scr[pl.ds(33 + 64 * i, 32), :] = o_ref[512 + 32 * i : 544 + 32 * i, :].astype(F32)
    query = q_scr[...]
    grad_wide = g_scr[...]
    grad = grad_wide.astype(BF)
    delta = jnp.sum((grad_wide * att_ref[...].astype(F32)).T, axis=0, keepdims=True)
    low_tail = p_ref[0, 1024:KPAD, :]
    inner_tail = (low_tail.astype(F32) * (dot_last(value_tail, grad) - delta)).astype(BF)
    dq = dot_first(key_tail, inner_tail)
    out_ref[0, 1, 1024:1025, :] = (dot(inner_tail, query) * SCALE).astype(BF)[0:1]
    out_ref[0, 2, 1024:1025, :] = dot(low_tail, grad).astype(BF)[0:1]
    low = p_ref[0, 0:1024, :]
    out_ref[0, 2, 0:1024, :] = dot(low, grad).astype(BF)
    inner = (low.astype(F32) * (dot_last(value, grad) - delta)).astype(BF)
    out_ref[0, 1, 0:1024, :] = (dot(inner, query) * SCALE).astype(BF)
    dq = dq + dot(kt_scr[...], inner)
    dq = (dq * SCALE).T.astype(BF)
    out_ref[0, 0, 0:1024, :] = dq[0:1024]
    out_ref[0, 0, 1024:1025, :] = dq[1024:1040][0:1]


def backward(head_inputs, probs, att, out_grad):
    return pl.pallas_call(
        backward_kernel,
        grid=(2,),
        out_shape=jax.ShapeDtypeStruct((1, 3, TT, 256), BF),
        in_specs=[
            pl.BlockSpec((1, 3, TT, HD), lambda h: (0, 0, 0, h)),
            pl.BlockSpec((1, KPAD, QPAD), lambda h: (h, 0, 0)),
            pl.BlockSpec((QPAD, HD), lambda h: (0, h)),
            pl.BlockSpec((PATCHES, HD), lambda h: (0, h)),
        ],
        out_specs=pl.BlockSpec((1, 3, TT, HD), lambda h: (0, 0, 0, h)),
        scratch_shapes=[
            pltpu.VMEM((QPAD, HD), BF),
            pltpu.VMEM((HD, 1024), BF),
            pltpu.VMEM((QPAD, HD), F32),
        ],
        compiler_params=params(60),
        name="attend_backward",
    )(head_inputs, probs, att, out_grad)


def weight_kernel(place_ref, r_ref, *refs):
    parts = refs[:8]
    keep_ref, send_ref, t_scr, sum_scr, part_scr, sems = refs[8:]
    copies = [pltpu.make_async_copy(parts[n], part_scr.at[n], sems.at[n]) for n in range(8)]
    for copy in copies:
        copy.start()
    t_scr[...] = r_ref[...].astype(F32).T.astype(BF)
    core = place_ref[0]
    for n in range(8):
        block = (place_ref[1] - n) & 7
        copies[n].wait()
        sum_scr[...] = dot(t_scr[...], part_scr[n])
        for x in range(4):
            mine = pl.multiple_of((2 * x + core) * GPAD, GPAD)
            other = pl.multiple_of((2 * x + 1 - core) * GPAD, GPAD)
            keep_ref[4 * block + x] = sum_scr[pl.ds(mine, GSEND), :]
            send_ref[4 * block + x] = sum_scr[pl.ds(other, GSEND), :].astype(BF)


def weight_parts(place, rows, gathered):
    vmem = pl.BlockSpec(memory_space=pltpu.VMEM)
    return pl.pallas_call(
        weight_kernel,
        out_shape=(
            jax.ShapeDtypeStruct((32, GSEND, 256), F32),
            jax.ShapeDtypeStruct((32, GSEND, 256), BF),
        ),
        in_specs=[pl.BlockSpec(memory_space=pltpu.SMEM), vmem] + [pl.BlockSpec(memory_space=pl.ANY)] * 8,
        out_specs=(vmem, vmem),
        scratch_shapes=[
            pltpu.VMEM((512, 1024), BF),
            pltpu.VMEM((512, 256), F32),
            pltpu.VMEM((8, PATCHES, 256), BF),
            pltpu.SemaphoreType.DMA((8,)),
        ],
        compiler_params=params(60),
        name="weight_parts",
    )(place, rows, *gathered)


def ring(count, step):
    return [(i, (i + step) % count) for i in range(count)]


def per_device(head_inputs, out_weight, sequence_gradient, slot_labels):
    peers = 64
    swap = [(z * 8 + y, y * 8 + z) for z in range(8) for y in range(8)]
    weight = lax.ppermute(out_weight, ("z", "y"), swap)
    place = jnp.stack([lax.axis_index(name).astype(jnp.int32) for name in ("c", "y")])
    outgoing = pack(slot_labels, sequence_gradient.transpose(0, 2, 1), peers)
    outgoing, head_inputs, weight = lax.optimization_barrier((outgoing, head_inputs, weight))
    weight = assemble(lax.all_gather(weight, SHARDS, axis=0))
    arrived = lax.all_to_all(outgoing, SHARDS, 0, 0, tiled=True)

    probs, att, parts = forward(head_inputs)
    back = [parts]
    for _ in range(4):
        back.append(lax.ppermute(back[-1], "y", ring(8, 1)))
    ahead = [parts]
    for _ in range(3):
        ahead.append(lax.ppermute(ahead[-1], "y", ring(8, -1)))
    arrived, *gathered = lax.optimization_barrier((arrived, *back, *ahead[:0:-1]))

    rows, part = receive(arrived.reshape(peers * PIECE, 4 * MAIN + 128), weight)
    out_grad = lax.psum_scatter(part, "y", scatter_dimension=0, tiled=True)[0]

    keep, send = weight_parts(place, rows, gathered)
    got = lax.ppermute(send, "c", [(0, 1), (1, 0)])
    both = (keep + got.astype(F32)).astype(BF)
    spread = lax.all_to_all(both, ("z", "x"), 0, 0, tiled=True)
    summed = jnp.sum(spread.astype(F32), axis=0)[:GROUP] * (1.0 / math.sqrt(65536))
    weight_gradient = lax.ppermute(summed, ("z", "y"), swap)

    head_gradient = backward(head_inputs, probs, att, out_grad)
    return head_gradient, weight_gradient


def solution(mesh):
    fine = Mesh(mesh.devices.reshape(8, 4, 2, 8), ("z", "x", "c", "y"))
    return jax.shard_map(
        per_device,
        mesh=fine,
        in_specs=(
            P(SHARDS, None, None, "y"),
            P(SHARDS, "y"),
            P(None, SHARDS, "y"),
            P(SHARDS, None),
        ),
        out_specs=(P(SHARDS, None, None, "y"), P(SHARDS, "y")),
        check_vma=False,
    )
```

time: 226 us -> 212 us (0.938)
  the two profiles are of different devices: /device:TPU:1 before, /device:TPU:34 now
where the time goes in v3:
time: 212 us
  waiting for transfers between devices  65.5 us (31%)
  starting transfers between devices  50.2 us (24%)
  Pallas kernels  41.5 us (20%)
  blocking collectives  32.8 us (15%)
  between operations  14.3 us (7%)
  local copies, waits for them, and re-layouts  4.9 us (2%)
  other arithmetic  2.53 us (1%)
    all_to_all x1, blocking collectives, per_device(): spread = lax.all_to_all(both, ('z', 'x'), 0, 0, tiled=True)  32.8 us
    ppermute x4, waiting for transfers between devices, per_device(): back.append(lax.ppermute(back[-1], 'y', ring(8, 1)))  28.6 us
    all_gather x1, waiting for transfers between devices, per_device(): weight = assemble(lax.all_gather(weight, SHARDS, axis=0))  24.1 us
    ppermute x3, starting transfers between devices, per_device(): ahead.append(lax.ppermute(ahead[-1], 'y', ring(8, -1)))  16.7 us
    ppermute x1, starting transfers between devices, per_device(): weight = lax.ppermute(out_weight, ('z', 'y'), swap)  10.5 us
    ppermute x1, waiting for transfers between devices, per_device(): weight_gradient = lax.ppermute(summed, ('z', 'y'), swap)  10.3 us
    pallas_call x1, Pallas kernels, receive(): pl.pallas_call(receive_kernel, grid=(4,), out_shape=(jax.ShapeDtypeStruct...  9.7 us
    pallas_call x1, Pallas kernels, weight_parts(): pl.pallas_call(weight_kernel, out_shape=(jax.ShapeDtypeStruct((32, GSEND,...  9.57 us
  transfers between devices with their start and end apart: 13, of which 6 were waited for; matrix products, arithmetic and copies ran while one was open for 1% of the time, Pallas kernels for 11%

profile of v3, /device:TPU:34, one launch (start us, length us, event | category | flops | bytes accessed | tf_op | source)
XLA Modules:
  0.0 211.7 jit_solution(14838695145526051157)
XLA Ops:
  7.2 10.5 %collective-permute-start = (bf16[50,256]{1,0:T(8,128)(2,1)}, bf16[50,256]{1,0:T(8,128)(2,1)S(1)}, u32[]{:S(2)}, u32[]{:S(2)}) collective-permute-start(bf16[50,256]{1,0:T(8,128)(2,1)} %param.5), channel_id=1, source_target_pairs={{0,0},{1,64},{2,128},{3,192},{4,256},{5,320},{6,384},{7,448},{64,1... | collective-permute-start | bytes 76808 | tf_op jit(solution)/shard_map/ppermute | solution.py:337
  17.7 5.8 %pack_pieces.1 = bf16[64,16,1664]{2,1,0:T(8,128)(2,1)} custom-call(s32[1,32]{1,0:T(1,128)} %label_ref.1, bf16[4,400,512]{2,1,0:T(8,128)(2,1)} %bitcast.6), custom_call_target="tpu_custom_call" | custom-call | tf_op jit(solution)/shard_map/pack_pieces/pallas_call | solution.py:78
  23.5 0.6 copy-done.10
  24.1 8.4 %all-to-all-start = ((bf16[64,16,1664]{2,1,0:T(8,128)(2,1)}), bf16[64,16,1664]{2,1,0:T(8,128)(2,1)}, u32[]{:S(2)}, u32[]{:S(2)}) async-start(bf16[64,16,1664]{2,1,0:T(8,128)(2,1)} %pack_pieces.1), calls=%async_computation | async-start | bytes 6815744 | tf_op jit(solution)/shard_map/all_to_all | solution.py:342
  32.6 7.8 %attend.1 = (bf16[2,1040,1152]{2,1,0:T(8,128)(2,1)}, bf16[1152,256]{1,0:T(8,128)(2,1)S(1)}, bf16[1024,256]{1,0:T(8,128)(2,1)S(1)}) custom-call(bf16[1,3,1025,256]{3,2,1,0:T(8,128)(2,1)S(1)} %copy-done.1), custom_call_target="tpu_custom_call" | custom-call | flops 2000000000 | bytes 8000000 | tf_op jit(solution)/shard_map/attend/pallas_call | solution.py:210
  40.4 0.8 copy-done.2
  41.2 2.1 collective-permute-start.1
  43.3 6.4 %collective-permute-start.5 = (bf16[1024,256]{1,0:T(8,128)(2,1)S(1)}, bf16[1024,256]{1,0:T(8,128)(2,1)S(1)}, u32[]{:S(2)}, u32[]{:S(2)}) collective-permute-start(bf16[1024,256]{1,0:T(8,128)(2,1)S(1)} %get-tuple-element.30.refs_0_), channel_id=1, source_target_pairs={{0,7},{1,0},{2,1},{3,2},{4,3},{5,4},{6,5},{7,6},{8,15},{9,8},{10,9... | collective-permute-start | bytes 1572872 | tf_op jit(solution)/shard_map/ppermute | solution.py:350
  49.7 10.3 %collective-permute-done.1.refs_1_ = bf16[1024,256]{1,0:T(8,128)(2,1)S(1)} collective-permute-done((bf16[1024,256]{1,0:T(8,128)(2,1)S(1)}, bf16[1024,256]{1,0:T(8,128)(2,1)S(1)}, u32[]{:S(2)}, u32[]{:S(2)}) %collective-permute-start.1) | collective-permute-done | bytes 524320 | tf_op jit(solution)/shard_map/ppermute | solution.py:347
  60.0 1.9 collective-permute-start.2
  62.0 5.1 %collective-permute-start.6 = (bf16[1024,256]{1,0:T(8,128)(2,1)S(1)}, bf16[1024,256]{1,0:T(8,128)(2,1)S(1)}, u32[]{:S(2)}, u32[]{:S(2)}) collective-permute-start(bf16[1024,256]{1,0:T(8,128)(2,1)S(1)} %collective-permute-done.5.refs_7_), channel_id=1, source_target_pairs={{0,7},{1,0},{2,1},{3,2},{4,3},{5,4},{6,5},{7,6},{8,15},{9,8},{10,9... | collective-permute-start | bytes 1572872 | tf_op jit(solution)/shard_map/ppermute | solution.py:350
  67.1 9.6 %collective-permute-done.2.refs_2_ = bf16[1024,256]{1,0:T(8,128)(2,1)S(1)} collective-permute-done((bf16[1024,256]{1,0:T(8,128)(2,1)S(1)}, bf16[1024,256]{1,0:T(8,128)(2,1)S(1)}, u32[]{:S(2)}, u32[]{:S(2)}) %collective-permute-start.2) | collective-permute-done | bytes 524320 | tf_op jit(solution)/shard_map/ppermute | solution.py:347
  76.7 1.9 collective-permute-start.3
  78.6 5.1 %collective-permute-start.7 = (bf16[1024,256]{1,0:T(8,128)(2,1)S(1)}, bf16[1024,256]{1,0:T(8,128)(2,1)}, u32[]{:S(2)}, u32[]{:S(2)}) collective-permute-start(bf16[1024,256]{1,0:T(8,128)(2,1)S(1)} %collective-permute-done.6.refs_6_), channel_id=1, source_target_pairs={{0,7},{1,0},{2,1},{3,2},{4,3},{5,4},{6,5},{7,6},{8,15},{9,8},{10,9... | collective-permute-start | bytes 1572872 | tf_op jit(solution)/shard_map/ppermute | solution.py:350
  83.8 8.7 %collective-permute-done.3.refs_3_ = bf16[1024,256]{1,0:T(8,128)(2,1)S(1)} collective-permute-done((bf16[1024,256]{1,0:T(8,128)(2,1)S(1)}, bf16[1024,256]{1,0:T(8,128)(2,1)S(1)}, u32[]{:S(2)}, u32[]{:S(2)}) %collective-permute-start.3) | collective-permute-done | bytes 524320 | tf_op jit(solution)/shard_map/ppermute | solution.py:347
  92.5 2.1 collective-permute-start.4
  94.6 24.1 %all-gather.4.cloned.1.call-done.in_ref = bf16[64,50,256]{2,1,0:T(8,128)(2,1)} async-done(((bf16[1,50,256]{2,1,0:T(8,128)(2,1)}), bf16[64,50,256]{2,1,0:T(8,128)(2,1)}) %all-gather.4.cloned.1.call-update) | async-done | bytes 1638416 | tf_op jit(solution)/shard_map/all_gather | solution.py:341
  118.7 1.5 copy-done.4
  120.2 0.2 assemble_weight.1.weight_ref
  120.4 1.3 copy-done
  121.8 9.7 %receive_pieces.1 = (bf16[1024,512]{1,0:T(8,128)(2,1)}, bf16[8,1024,256]{2,1,0:T(8,128)(2,1)}) custom-call(bf16[1024,1664]{1,0:T(8,128)(2,1)} %bitcast.1.in_ref, bf16[8,512,256]{2,1,0:T(8,128)(2,1)} %copy-done), custom_call_target="tpu_custom_call" | custom-call | tf_op jit(solution)/shard_map/receive_pieces/pallas_call | solution.py:153
  131.5 0.6 pad_add_fusion.place_ref
  132.1 9.6 %weight_parts.1 = (f32[32,56,256]{2,1,0:T(8,128)}, bf16[32,56,256]{2,1,0:T(8,128)(2,1)}) custom-call(s32[2]{0:T(128)} %pad_add_fusion.place_ref, bf16[1024,512]{1,0:T(8,128)(2,1)} %get-tuple-element.29.r_ref, bf16[1024,256]{1,0:T(8,128)(2,1)} %copy-done.3, bf16[1024,256]{1,0:T(8,128)(2,1)} %copy-done.5, bf16[1024,256]{1,0:T(8,128)(2,1)} %copy-done.7, ...), custom_call_target="tpu_custom_call" | custom-call | tf_op jit(solution)/shard_map/weight_parts/pallas_call | solution.py:311
  141.7 2.2 %collective-permute-start.8 = (bf16[32,56,256]{2,1,0:T(8,128)(2,1)}, bf16[32,56,256]{2,1,0:T(8,128)(2,1)S(1)}, u32[]{:S(2)}, u32[]{:S(2)}) collective-permute-start(bf16[32,56,256]{2,1,0:T(8,128)(2,1)} %get-tuple-element.39), channel_id=1, source_target_pairs={{0,8},{8,0},{1,9},{9,1},{2,10},{10,2},{3,11},{11,3},{4,12},{12,4},... | collective-permute-start | bytes 2752520 | tf_op jit(solution)/shard_map/ppermute | solution.py:357
  143.8 2.4 %collective-permute-done.8 = bf16[32,56,256]{2,1,0:T(8,128)(2,1)S(1)} collective-permute-done((bf16[32,56,256]{2,1,0:T(8,128)(2,1)}, bf16[32,56,256]{2,1,0:T(8,128)(2,1)S(1)}, u32[]{:S(2)}, u32[]{:S(2)}) %collective-permute-start.8) | collective-permute-done | bytes 917536 | tf_op jit(solution)/shard_map/ppermute | solution.py:357
  146.3 1.8 add_convert_fusion
  148.0 32.8 %all_to_all.10 = bf16[32,56,256]{2,1,0:T(8,128)(2,1)S(1)} all-to-all(bf16[32,56,256]{2,1,0:T(8,128)(2,1)S(1)} %add_convert_fusion), channel_id=1, replica_groups=mesh['z'=8,'x'=4,'c'=2,'y'=8] {'z','x'}, dimensions={0} | all-to-all | bytes 1835008 | tf_op jit(solution)/shard_map/all_to_all | solution.py:359
  180.9 0.1 convert_reduce_fusion
  181.0 4.5 %collective-permute-start.9 = (f32[50,256]{1,0:T(8,128)S(1)}, f32[50,256]{1,0:T(8,128)S(1)}, u32[]{:S(2)}, u32[]{:S(2)}) collective-permute-start(f32[50,256]{1,0:T(8,128)S(1)} %slice_multiply_fusion), channel_id=1, source_target_pairs={{0,0},{1,64},{2,128},{3,192},{4,256},{5,320},{6,384},{7,448},{64,1... | collective-permute-start | bytes 153608 | tf_op jit(solution)/shard_map/ppermute | solution.py:361
  185.5 10.3 %collective-permute-done.9 = f32[50,256]{1,0:T(8,128)S(1)} collective-permute-done((f32[50,256]{1,0:T(8,128)S(1)}, f32[50,256]{1,0:T(8,128)S(1)}, u32[]{:S(2)}, u32[]{:S(2)}) %collective-permute-start.9) | collective-permute-done | bytes 51232 | tf_op jit(solution)/shard_map/ppermute | solution.py:361
  195.8 8.4 %attend_backward.1 = bf16[1,3,1025,256]{3,2,1,0:T(8,128)(2,1)} custom-call(bf16[1,3,1025,256]{3,2,1,0:T(8,128)(2,1)} %x_ref.1, bf16[2,1040,1152]{2,1,0:T(8,128)(2,1)} %get-tuple-element.22.p_ref, bf16[1152,256]{1,0:T(8,128)(2,1)} %copy-done.2, bf16[1024,256]{1,0:T(8,128)(2,1)} %bitcast.7), custom_call_target="tpu_custom_call" | custom-call | tf_op jit(solution)/shard_map/attend_backward/pallas_call | solution.py:269
  204.2 0.6 copy.7
  (30 shorter events, 0.2 us)
Async XLA Ops:
  7.2 111.5 %all-gather.4.cloned.1.call-start = ((), (), s32[]{:S(2)}) async-start(), calls=%async_computation.4 | async-start | bytes 1863680 | tf_op jit(solution)/shard_map/all_gather | solution.py:341
  7.2 16.3 %collective-permute-start = (bf16[50,256]{1,0:T(8,128)(2,1)}, bf16[50,256]{1,0:T(8,128)(2,1)S(1)}, u32[]{:S(2)}, u32[]{:S(2)}) collective-permute-start(bf16[50,256]{1,0:T(8,128)(2,1)} %param.5), channel_id=1, source_target_pairs={{0,0},{1,64},{2,128},{3,192},{4,256},{5,320},{6,384},{7,448},{64,1... | collective-permute-start | bytes 76808 | tf_op jit(solution)/shard_map/ppermute | solution.py:337
  23.5 0.6 copy-start.10
  24.1 8.4 %copy-start.1 = (bf16[1,3,1025,256]{3,2,1,0:T(8,128)(2,1)S(1)}, bf16[1,3,1025,256]{3,2,1,0:T(8,128)(2,1)}, u32[]{:S(2)}) copy-start(bf16[1,3,1025,256]{3,2,1,0:T(8,128)(2,1)} %x_ref.1) | copy-start | bytes 4723204
  24.1 97.6 %all-to-all-start = ((bf16[64,16,1664]{2,1,0:T(8,128)(2,1)}), bf16[64,16,1664]{2,1,0:T(8,128)(2,1)}, u32[]{:S(2)}, u32[]{:S(2)}) async-start(bf16[64,16,1664]{2,1,0:T(8,128)(2,1)} %pack_pieces.1), calls=%async_computation | async-start | bytes 6815744 | tf_op jit(solution)/shard_map/all_to_all | solution.py:342
  32.5 163.3 %reduce-scatter.2.cloned.1.call-start = ((), (), s32[]{:S(2)}) async-start(), calls=%async_computation.3 | async-start | bytes 4718592 | tf_op jit(solution)/shard_map/reduce_scatter | solution.py:354
  40.4 0.8 copy-start.2
  41.2 79.1 %copy-start.3 = (bf16[1024,256]{1,0:T(8,128)(2,1)}, bf16[1024,256]{1,0:T(8,128)(2,1)S(1)}, u32[]{:S(2)}) copy-start(bf16[1024,256]{1,0:T(8,128)(2,1)S(1)} %get-tuple-element.30.refs_0_) | copy-start | bytes 1572868
  41.2 18.8 %collective-permute-start.1 = (bf16[1024,256]{1,0:T(8,128)(2,1)S(1)}, bf16[1024,256]{1,0:T(8,128)(2,1)S(1)}, u32[]{:S(2)}, u32[]{:S(2)}) collective-permute-start(bf16[1024,256]{1,0:T(8,128)(2,1)S(1)} %get-tuple-element.30.refs_0_), channel_id=1, source_target_pairs={{0,1},{1,2},{2,3},{3,4},{4,5},{5,6},{6,7},{7,0},{8,9},{9,10},{10,1... | collective-permute-start | bytes 1572872 | tf_op jit(solution)/shard_map/ppermute | solution.py:347
  43.3 18.7 %collective-permute-start.5 = (bf16[1024,256]{1,0:T(8,128)(2,1)S(1)}, bf16[1024,256]{1,0:T(8,128)(2,1)S(1)}, u32[]{:S(2)}, u32[]{:S(2)}) collective-permute-start(bf16[1024,256]{1,0:T(8,128)(2,1)S(1)} %get-tuple-element.30.refs_0_), channel_id=1, source_target_pairs={{0,7},{1,0},{2,1},{3,2},{4,3},{5,4},{6,5},{7,6},{8,15},{9,8},{10,9... | collective-permute-start | bytes 1572872 | tf_op jit(solution)/shard_map/ppermute | solution.py:350
  60.0 60.3 %copy-start.5 = (bf16[1024,256]{1,0:T(8,128)(2,1)}, bf16[1024,256]{1,0:T(8,128)(2,1)S(1)}, u32[]{:S(2)}) copy-start(bf16[1024,256]{1,0:T(8,128)(2,1)S(1)} %collective-permute-done.1.refs_1_) | copy-start | bytes 1572868
  60.0 16.7 %collective-permute-start.2 = (bf16[1024,256]{1,0:T(8,128)(2,1)S(1)}, bf16[1024,256]{1,0:T(8,128)(2,1)S(1)}, u32[]{:S(2)}, u32[]{:S(2)}) collective-permute-start(bf16[1024,256]{1,0:T(8,128)(2,1)S(1)} %collective-permute-done.1.refs_1_), channel_id=1, source_target_pairs={{0,1},{1,2},{2,3},{3,4},{4,5},{5,6},{6,7},{7,0},{8,9},{9,10},{10,1... | collective-permute-start | bytes 1572872 | tf_op jit(solution)/shard_map/ppermute | solution.py:347
  61.9 58.4 %copy-start.6 = (bf16[1024,256]{1,0:T(8,128)(2,1)}, bf16[1024,256]{1,0:T(8,128)(2,1)S(1)}, u32[]{:S(2)}) copy-start(bf16[1024,256]{1,0:T(8,128)(2,1)S(1)} %collective-permute-done.5.refs_7_) | copy-start | bytes 1572868
  62.0 16.6 %collective-permute-start.6 = (bf16[1024,256]{1,0:T(8,128)(2,1)S(1)}, bf16[1024,256]{1,0:T(8,128)(2,1)S(1)}, u32[]{:S(2)}, u32[]{:S(2)}) collective-permute-start(bf16[1024,256]{1,0:T(8,128)(2,1)S(1)} %collective-permute-done.5.refs_7_), channel_id=1, source_target_pairs={{0,7},{1,0},{2,1},{3,2},{4,3},{5,4},{6,5},{7,6},{8,15},{9,8},{10,9... | collective-permute-start | bytes 1572872 | tf_op jit(solution)/shard_map/ppermute | solution.py:350
  76.7 43.7 %copy-start.7 = (bf16[1024,256]{1,0:T(8,128)(2,1)}, bf16[1024,256]{1,0:T(8,128)(2,1)S(1)}, u32[]{:S(2)}) copy-start(bf16[1024,256]{1,0:T(8,128)(2,1)S(1)} %collective-permute-done.2.refs_2_) | copy-start | bytes 1572868
  76.7 15.8 %collective-permute-start.3 = (bf16[1024,256]{1,0:T(8,128)(2,1)S(1)}, bf16[1024,256]{1,0:T(8,128)(2,1)S(1)}, u32[]{:S(2)}, u32[]{:S(2)}) collective-permute-start(bf16[1024,256]{1,0:T(8,128)(2,1)S(1)} %collective-permute-done.2.refs_2_), channel_id=1, source_target_pairs={{0,1},{1,2},{2,3},{3,4},{4,5},{5,6},{6,7},{7,0},{8,9},{9,10},{10,1... | collective-permute-start | bytes 1572872 | tf_op jit(solution)/shard_map/ppermute | solution.py:347
  78.6 41.8 %copy-start.8 = (bf16[1024,256]{1,0:T(8,128)(2,1)}, bf16[1024,256]{1,0:T(8,128)(2,1)S(1)}, u32[]{:S(2)}) copy-start(bf16[1024,256]{1,0:T(8,128)(2,1)S(1)} %collective-permute-done.6.refs_6_) | copy-start | bytes 1572868
  78.6 43.1 %collective-permute-start.7 = (bf16[1024,256]{1,0:T(8,128)(2,1)S(1)}, bf16[1024,256]{1,0:T(8,128)(2,1)}, u32[]{:S(2)}, u32[]{:S(2)}) collective-permute-start(bf16[1024,256]{1,0:T(8,128)(2,1)S(1)} %collective-permute-done.6.refs_6_), channel_id=1, source_target_pairs={{0,7},{1,0},{2,1},{3,2},{4,3},{5,4},{6,5},{7,6},{8,15},{9,8},{10,9... | collective-permute-start | bytes 1572872 | tf_op jit(solution)/shard_map/ppermute | solution.py:350
  92.5 27.9 %copy-start.9 = (bf16[1024,256]{1,0:T(8,128)(2,1)}, bf16[1024,256]{1,0:T(8,128)(2,1)S(1)}, u32[]{:S(2)}) copy-start(bf16[1024,256]{1,0:T(8,128)(2,1)S(1)} %collective-permute-done.3.refs_3_) | copy-start | bytes 1572868
  92.5 29.3 %collective-permute-start.4 = (bf16[1024,256]{1,0:T(8,128)(2,1)S(1)}, bf16[1024,256]{1,0:T(8,128)(2,1)}, u32[]{:S(2)}, u32[]{:S(2)}) collective-permute-start(bf16[1024,256]{1,0:T(8,128)(2,1)S(1)} %collective-permute-done.3.refs_3_), channel_id=1, source_target_pairs={{0,1},{1,2},{2,3},{3,4},{4,5},{5,6},{6,7},{7,0},{8,9},{9,10},{10,1... | collective-permute-start | bytes 1572872 | tf_op jit(solution)/shard_map/ppermute | solution.py:347
  118.7 1.5 copy-start.4
  120.4 1.3 copy-start
  141.7 4.6 %collective-permute-start.8 = (bf16[32,56,256]{2,1,0:T(8,128)(2,1)}, bf16[32,56,256]{2,1,0:T(8,128)(2,1)S(1)}, u32[]{:S(2)}, u32[]{:S(2)}) collective-permute-start(bf16[32,56,256]{2,1,0:T(8,128)(2,1)} %get-tuple-element.39), channel_id=1, source_target_pairs={{0,8},{8,0},{1,9},{9,1},{2,10},{10,2},{3,11},{11,3},{4,12},{12,4},... | collective-permute-start | bytes 2752520 | tf_op jit(solution)/shard_map/ppermute | solution.py:357
  181.0 14.8 %collective-permute-start.9 = (f32[50,256]{1,0:T(8,128)S(1)}, f32[50,256]{1,0:T(8,128)S(1)}, u32[]{:S(2)}, u32[]{:S(2)}) collective-permute-start(f32[50,256]{1,0:T(8,128)S(1)} %slice_multiply_fusion), channel_id=1, source_target_pairs={{0,0},{1,64},{2,128},{3,192},{4,256},{5,320},{6,384},{7,448},{64,1... | collective-permute-start | bytes 153608 | tf_op jit(solution)/shard_map/ppermute | solution.py:361
Sparse Core Ops, SparseCore 0:
  24.3 94.3 all-gather.3
  131.6 53.2 reduce-scatter.1

commit v4 on v3

--- a/solution.py
+++ b/solution.py
@@ -66,9 +66,9 @@
     step = out_ref.shape[0] * PIECE
     row = iota((step, positions), 0) + pl.program_id(0) * step
     pick = jnp.where(row == goal_scr[0:1, :], 1.0, 0.0).astype(BF)
-    for k in range(4):
-        moved = dot_last(pick, x_ref[k, 0:MAIN, :]).astype(BF)
-        out_ref[:, :, k * MAIN : (k + 1) * MAIN] = moved.reshape(step // PIECE, PIECE, MAIN)
+    for k in range(0, 4, 2):
+        moved = dot_last(pick, x_ref[k : k + 2, 0:MAIN, :].reshape(2 * MAIN, positions)).astype(BF)
+        out_ref[:, :, k * MAIN : (k + 2) * MAIN] = moved.reshape(step // PIECE, PIECE, 2 * MAIN)
     moved = dot_last(pick, rest_scr[...]).astype(BF)
     out_ref[:, :, 4 * MAIN :] = moved.reshape(step // PIECE, PIECE, 128)
 
@@ -77,13 +77,13 @@
     features, positions = columns.shape[1:]
     return pl.pallas_call(
         pack_kernel,
-        grid=(4,),
+        grid=(2,),
         out_shape=jax.ShapeDtypeStruct((peers, PIECE, 4 * MAIN + 128), BF),
         in_specs=[
             pl.BlockSpec(memory_space=pltpu.SMEM),
             pl.BlockSpec((4, features, positions), lambda r: (0, 0, 0)),
         ],
-        out_specs=pl.BlockSpec((peers // 4, PIECE, 4 * MAIN + 128), lambda r: (r, 0, 0)),
+        out_specs=pl.BlockSpec((peers // 2, PIECE, 4 * MAIN + 128), lambda r: (r, 0, 0)),
         scratch_shapes=[pltpu.VMEM((128, positions), BF), pltpu.VMEM((16, positions), jnp.int32)],
         compiler_params=params(60),
         name="pack_pieces",
@@ -144,7 +144,7 @@
                 lower = e * 512 + half * 256
                 rows_ref[lower : lower + 256, :] = dot(order, stack_scr[half]).astype(BF)
 
-    for a in range(2):
+    for a in range(4):
         part_ref[a] = dot(rows_ref[...], weight_ref[a]).astype(BF)
 
 
@@ -152,18 +152,18 @@
     slots = arrived.shape[0]
     return pl.pallas_call(
         receive_kernel,
-        grid=(4,),
+        grid=(2,),
         out_shape=(
             jax.ShapeDtypeStruct((1024, 512), BF),
             jax.ShapeDtypeStruct((8, 1024, 256), BF),
         ),
         in_specs=[
             pl.BlockSpec(memory_space=pltpu.VMEM),
-            pl.BlockSpec((2, 8 * GPAD, 256), lambda a: (a, 0, 0)),
+            pl.BlockSpec((4, 8 * GPAD, 256), lambda a: (a, 0, 0)),
         ],
         out_specs=(
             pl.BlockSpec((1024, 512), lambda a: (0, 0)),
-            pl.BlockSpec((2, 1024, 256), lambda a: (a, 0, 0)),
+            pl.BlockSpec((4, 1024, 256), lambda a: (a, 0, 0)),
         ),
         scratch_shapes=[
             pltpu.VMEM((256, 4 * MAIN), BF),

time: 212 us -> 213 us (level)
  no operation moved by 1% of the time
where the time goes in v4:
time: 213 us; the launch traced here: 212 us
  waiting for transfers between devices  66.1 us (31%)
  starting transfers between devices  51.2 us (24%)
  Pallas kernels  40.1 us (19%)
  blocking collectives  32.8 us (15%)
  between operations  14.3 us (7%)
  local copies, waits for them, and re-layouts  4.9 us (2%)
  other arithmetic  2.53 us (1%)
    all_to_all x1, blocking collectives, per_device(): spread = lax.all_to_all(both, ('z', 'x'), 0, 0, tiled=True)  32.8 us
    ppermute x4, waiting for transfers between devices, per_device(): back.append(lax.ppermute(back[-1], 'y', ring(8, 1)))  28.6 us
    all_gather x1, waiting for transfers between devices, per_device(): weight = assemble(lax.all_gather(weight, SHARDS, axis=0))  25 us
    ppermute x3, starting transfers between devices, per_device(): ahead.append(lax.ppermute(ahead[-1], 'y', ring(8, -1)))  16.8 us
    ppermute x1, starting transfers between devices, per_device(): weight = lax.ppermute(out_weight, ('z', 'y'), swap)  10.5 us
    ppermute x1, waiting for transfers between devices, per_device(): weight_gradient = lax.ppermute(summed, ('z', 'y'), swap)  10 us
    pallas_call x1, Pallas kernels, weight_parts(): pl.pallas_call(weight_kernel, out_shape=(jax.ShapeDtypeStruct((32, GSEND,...  9.57 us
    pallas_call x1, Pallas kernels, receive(): pl.pallas_call(receive_kernel, grid=(2,), out_shape=(jax.ShapeDtypeStruct...  9.09 us
  transfers between devices with their start and end apart: 13, of which 6 were waited for; matrix products, arithmetic and copies ran while one was open for 1% of the time, Pallas kernels for 11%

profile of v4, /device:TPU:34, one launch (start us, length us, event | category | flops | bytes accessed | tf_op | source)
XLA Modules:
  0.0 211.9 jit_solution(9688905752969141866)
XLA Ops:
  7.2 10.5 %collective-permute-start = (bf16[50,256]{1,0:T(8,128)(2,1)}, bf16[50,256]{1,0:T(8,128)(2,1)S(1)}, u32[]{:S(2)}, u32[]{:S(2)}) collective-permute-start(bf16[50,256]{1,0:T(8,128)(2,1)} %param.5), channel_id=1, source_target_pairs={{0,0},{1,64},{2,128},{3,192},{4,256},{5,320},{6,384},{7,448},{64,1... | collective-permute-start | bytes 76808 | tf_op jit(solution)/shard_map/ppermute | solution.py:337
  17.7 5.1 %pack_pieces.1 = bf16[64,16,1664]{2,1,0:T(8,128)(2,1)} custom-call(s32[1,32]{1,0:T(1,128)} %label_ref.1, bf16[4,400,512]{2,1,0:T(8,128)(2,1)} %bitcast.6), custom_call_target="tpu_custom_call" | custom-call | tf_op jit(solution)/shard_map/pack_pieces/pallas_call | solution.py:78
  22.8 0.6 copy-done.10
  23.4 9.1 %all-to-all-start = ((bf16[64,16,1664]{2,1,0:T(8,128)(2,1)}), bf16[64,16,1664]{2,1,0:T(8,128)(2,1)}, u32[]{:S(2)}, u32[]{:S(2)}) async-start(bf16[64,16,1664]{2,1,0:T(8,128)(2,1)} %pack_pieces.1), calls=%async_computation | async-start | bytes 6815744 | tf_op jit(solution)/shard_map/all_to_all | solution.py:342
  32.6 7.8 %attend.1 = (bf16[2,1040,1152]{2,1,0:T(8,128)(2,1)}, bf16[1152,256]{1,0:T(8,128)(2,1)S(1)}, bf16[1024,256]{1,0:T(8,128)(2,1)S(1)}) custom-call(bf16[1,3,1025,256]{3,2,1,0:T(8,128)(2,1)S(1)} %copy-done.1), custom_call_target="tpu_custom_call" | custom-call | flops 2000000000 | bytes 8000000 | tf_op jit(solution)/shard_map/attend/pallas_call | solution.py:210
  40.4 0.8 copy-done.2
  41.2 1.9 collective-permute-start.1
  43.1 6.6 %collective-permute-start.5 = (bf16[1024,256]{1,0:T(8,128)(2,1)S(1)}, bf16[1024,256]{1,0:T(8,128)(2,1)S(1)}, u32[]{:S(2)}, u32[]{:S(2)}) collective-permute-start(bf16[1024,256]{1,0:T(8,128)(2,1)S(1)} %get-tuple-element.30.refs_0_), channel_id=1, source_target_pairs={{0,7},{1,0},{2,1},{3,2},{4,3},{5,4},{6,5},{7,6},{8,15},{9,8},{10,9... | collective-permute-start | bytes 1572872 | tf_op jit(solution)/shard_map/ppermute | solution.py:350
  49.7 10.3 %collective-permute-done.1.refs_1_ = bf16[1024,256]{1,0:T(8,128)(2,1)S(1)} collective-permute-done((bf16[1024,256]{1,0:T(8,128)(2,1)S(1)}, bf16[1024,256]{1,0:T(8,128)(2,1)S(1)}, u32[]{:S(2)}, u32[]{:S(2)}) %collective-permute-start.1) | collective-permute-done | bytes 524320 | tf_op jit(solution)/shard_map/ppermute | solution.py:347
  60.0 1.9 collective-permute-start.2
  62.0 5.1 %collective-permute-start.6 = (bf16[1024,256]{1,0:T(8,128)(2,1)S(1)}, bf16[1024,256]{1,0:T(8,128)(2,1)S(1)}, u32[]{:S(2)}, u32[]{:S(2)}) collective-permute-start(bf16[1024,256]{1,0:T(8,128)(2,1)S(1)} %collective-permute-done.5.refs_7_), channel_id=1, source_target_pairs={{0,7},{1,0},{2,1},{3,2},{4,3},{5,4},{6,5},{7,6},{8,15},{9,8},{10,9... | collective-permute-start | bytes 1572872 | tf_op jit(solution)/shard_map/ppermute | solution.py:350
  67.1 9.6 %collective-permute-done.2.refs_2_ = bf16[1024,256]{1,0:T(8,128)(2,1)S(1)} collective-permute-done((bf16[1024,256]{1,0:T(8,128)(2,1)S(1)}, bf16[1024,256]{1,0:T(8,128)(2,1)S(1)}, u32[]{:S(2)}, u32[]{:S(2)}) %collective-permute-start.2) | collective-permute-done | bytes 524320 | tf_op jit(solution)/shard_map/ppermute | solution.py:347
  76.7 1.9 collective-permute-start.3
  78.6 5.1 %collective-permute-start.7 = (bf16[1024,256]{1,0:T(8,128)(2,1)S(1)}, bf16[1024,256]{1,0:T(8,128)(2,1)}, u32[]{:S(2)}, u32[]{:S(2)}) collective-permute-start(bf16[1024,256]{1,0:T(8,128)(2,1)S(1)} %collective-permute-done.6.refs_6_), channel_id=1, source_target_pairs={{0,7},{1,0},{2,1},{3,2},{4,3},{5,4},{6,5},{7,6},{8,15},{9,8},{10,9... | collective-permute-start | bytes 1572872 | tf_op jit(solution)/shard_map/ppermute | solution.py:350
  83.8 8.7 %collective-permute-done.3.refs_3_ = bf16[1024,256]{1,0:T(8,128)(2,1)S(1)} collective-permute-done((bf16[1024,256]{1,0:T(8,128)(2,1)S(1)}, bf16[1024,256]{1,0:T(8,128)(2,1)S(1)}, u32[]{:S(2)}, u32[]{:S(2)}) %collective-permute-start.3) | collective-permute-done | bytes 524320 | tf_op jit(solution)/shard_map/ppermute | solution.py:347
  92.5 2.1 collective-permute-start.4
  94.6 25.0 %all-gather.4.cloned.1.call-done.in_ref = bf16[64,50,256]{2,1,0:T(8,128)(2,1)} async-done(((bf16[1,50,256]{2,1,0:T(8,128)(2,1)}), bf16[64,50,256]{2,1,0:T(8,128)(2,1)}) %all-gather.4.cloned.1.call-update) | async-done | bytes 1638416 | tf_op jit(solution)/shard_map/all_gather | solution.py:341
  119.6 1.5 copy-done.4
  121.1 0.2 assemble_weight.1.weight_ref
  121.3 1.3 copy-done
  122.7 9.1 %receive_pieces.1 = (bf16[1024,512]{1,0:T(8,128)(2,1)}, bf16[8,1024,256]{2,1,0:T(8,128)(2,1)}) custom-call(bf16[1024,1664]{1,0:T(8,128)(2,1)} %bitcast.1.in_ref, bf16[8,512,256]{2,1,0:T(8,128)(2,1)} %copy-done), custom_call_target="tpu_custom_call" | custom-call | tf_op jit(solution)/shard_map/receive_pieces/pallas_call | solution.py:153
  131.8 0.6 pad_add_fusion.place_ref
  132.4 9.6 %weight_parts.1 = (f32[32,56,256]{2,1,0:T(8,128)}, bf16[32,56,256]{2,1,0:T(8,128)(2,1)}) custom-call(s32[2]{0:T(128)} %pad_add_fusion.place_ref, bf16[1024,512]{1,0:T(8,128)(2,1)} %get-tuple-element.29.r_ref, bf16[1024,256]{1,0:T(8,128)(2,1)} %copy-done.3, bf16[1024,256]{1,0:T(8,128)(2,1)} %copy-done.5, bf16[1024,256]{1,0:T(8,128)(2,1)} %copy-done.7, ...), custom_call_target="tpu_custom_call" | custom-call | tf_op jit(solution)/shard_map/weight_parts/pallas_call | solution.py:311
  142.0 2.2 %collective-permute-start.8 = (bf16[32,56,256]{2,1,0:T(8,128)(2,1)}, bf16[32,56,256]{2,1,0:T(8,128)(2,1)S(1)}, u32[]{:S(2)}, u32[]{:S(2)}) collective-permute-start(bf16[32,56,256]{2,1,0:T(8,128)(2,1)} %get-tuple-element.39), channel_id=1, source_target_pairs={{0,8},{8,0},{1,9},{9,1},{2,10},{10,2},{3,11},{11,3},{4,12},{12,4},... | collective-permute-start | bytes 2752520 | tf_op jit(solution)/shard_map/ppermute | solution.py:357
  144.2 2.4 %collective-permute-done.8 = bf16[32,56,256]{2,1,0:T(8,128)(2,1)S(1)} collective-permute-done((bf16[32,56,256]{2,1,0:T(8,128)(2,1)}, bf16[32,56,256]{2,1,0:T(8,128)(2,1)S(1)}, u32[]{:S(2)}, u32[]{:S(2)}) %collective-permute-start.8) | collective-permute-done | bytes 917536 | tf_op jit(solution)/shard_map/ppermute | solution.py:357
  146.6 1.8 add_convert_fusion
  148.3 32.8 %all_to_all.10 = bf16[32,56,256]{2,1,0:T(8,128)(2,1)S(1)} all-to-all(bf16[32,56,256]{2,1,0:T(8,128)(2,1)S(1)} %add_convert_fusion), channel_id=1, replica_groups=mesh['z'=8,'x'=4,'c'=2,'y'=8] {'z','x'}, dimensions={0} | all-to-all | bytes 1835008 | tf_op jit(solution)/shard_map/all_to_all | solution.py:359
  181.1 0.1 convert_reduce_fusion
  181.2 4.8 %collective-permute-start.9 = (f32[50,256]{1,0:T(8,128)S(1)}, f32[50,256]{1,0:T(8,128)S(1)}, u32[]{:S(2)}, u32[]{:S(2)}) collective-permute-start(f32[50,256]{1,0:T(8,128)S(1)} %slice_multiply_fusion), channel_id=1, source_target_pairs={{0,0},{1,64},{2,128},{3,192},{4,256},{5,320},{6,384},{7,448},{64,1... | collective-permute-start | bytes 153608 | tf_op jit(solution)/shard_map/ppermute | solution.py:361
  186.0 10.0 %collective-permute-done.9 = f32[50,256]{1,0:T(8,128)S(1)} collective-permute-done((f32[50,256]{1,0:T(8,128)S(1)}, f32[50,256]{1,0:T(8,128)S(1)}, u32[]{:S(2)}, u32[]{:S(2)}) %collective-permute-start.9) | collective-permute-done | bytes 51232 | tf_op jit(solution)/shard_map/ppermute | solution.py:361
  196.0 8.4 %attend_backward.1 = bf16[1,3,1025,256]{3,2,1,0:T(8,128)(2,1)} custom-call(bf16[1,3,1025,256]{3,2,1,0:T(8,128)(2,1)} %x_ref.1, bf16[2,1040,1152]{2,1,0:T(8,128)(2,1)} %get-tuple-element.22.p_ref, bf16[1152,256]{1,0:T(8,128)(2,1)} %copy-done.2, bf16[1024,256]{1,0:T(8,128)(2,1)} %bitcast.7), custom_call_target="tpu_custom_call" | custom-call | tf_op jit(solution)/shard_map/attend_backward/pallas_call | solution.py:269
  204.4 0.6 copy.7
  (30 shorter events, 0.2 us)
Async XLA Ops:
  7.2 112.4 %all-gather.4.cloned.1.call-start = ((), (), s32[]{:S(2)}) async-start(), calls=%async_computation.4 | async-start | bytes 1863680 | tf_op jit(solution)/shard_map/all_gather | solution.py:341
  7.2 15.6 %collective-permute-start = (bf16[50,256]{1,0:T(8,128)(2,1)}, bf16[50,256]{1,0:T(8,128)(2,1)S(1)}, u32[]{:S(2)}, u32[]{:S(2)}) collective-permute-start(bf16[50,256]{1,0:T(8,128)(2,1)} %param.5), channel_id=1, source_target_pairs={{0,0},{1,64},{2,128},{3,192},{4,256},{5,320},{6,384},{7,448},{64,1... | collective-permute-start | bytes 76808 | tf_op jit(solution)/shard_map/ppermute | solution.py:337
  22.8 0.6 copy-start.10
  23.4 9.2 %copy-start.1 = (bf16[1,3,1025,256]{3,2,1,0:T(8,128)(2,1)S(1)}, bf16[1,3,1025,256]{3,2,1,0:T(8,128)(2,1)}, u32[]{:S(2)}) copy-start(bf16[1,3,1025,256]{3,2,1,0:T(8,128)(2,1)} %x_ref.1) | copy-start | bytes 4723204
  23.4 99.2 %all-to-all-start = ((bf16[64,16,1664]{2,1,0:T(8,128)(2,1)}), bf16[64,16,1664]{2,1,0:T(8,128)(2,1)}, u32[]{:S(2)}, u32[]{:S(2)}) async-start(bf16[64,16,1664]{2,1,0:T(8,128)(2,1)} %pack_pieces.1), calls=%async_computation | async-start | bytes 6815744 | tf_op jit(solution)/shard_map/all_to_all | solution.py:342
  32.5 163.5 %reduce-scatter.2.cloned.1.call-start = ((), (), s32[]{:S(2)}) async-start(), calls=%async_computation.3 | async-start | bytes 4718592 | tf_op jit(solution)/shard_map/reduce_scatter | solution.py:354
  40.4 0.8 copy-start.2
  41.2 80.0 %copy-start.3 = (bf16[1024,256]{1,0:T(8,128)(2,1)}, bf16[1024,256]{1,0:T(8,128)(2,1)S(1)}, u32[]{:S(2)}) copy-start(bf16[1024,256]{1,0:T(8,128)(2,1)S(1)} %get-tuple-element.30.refs_0_) | copy-start | bytes 1572868
  41.2 18.8 %collective-permute-start.1 = (bf16[1024,256]{1,0:T(8,128)(2,1)S(1)}, bf16[1024,256]{1,0:T(8,128)(2,1)S(1)}, u32[]{:S(2)}, u32[]{:S(2)}) collective-permute-start(bf16[1024,256]{1,0:T(8,128)(2,1)S(1)} %get-tuple-element.30.refs_0_), channel_id=1, source_target_pairs={{0,1},{1,2},{2,3},{3,4},{4,5},{5,6},{6,7},{7,0},{8,9},{9,10},{10,1... | collective-permute-start | bytes 1572872 | tf_op jit(solution)/shard_map/ppermute | solution.py:347
  43.1 18.8 %collective-permute-start.5 = (bf16[1024,256]{1,0:T(8,128)(2,1)S(1)}, bf16[1024,256]{1,0:T(8,128)(2,1)S(1)}, u32[]{:S(2)}, u32[]{:S(2)}) collective-permute-start(bf16[1024,256]{1,0:T(8,128)(2,1)S(1)} %get-tuple-element.30.refs_0_), channel_id=1, source_target_pairs={{0,7},{1,0},{2,1},{3,2},{4,3},{5,4},{6,5},{7,6},{8,15},{9,8},{10,9... | collective-permute-start | bytes 1572872 | tf_op jit(solution)/shard_map/ppermute | solution.py:350
  60.0 61.3 %copy-start.5 = (bf16[1024,256]{1,0:T(8,128)(2,1)}, bf16[1024,256]{1,0:T(8,128)(2,1)S(1)}, u32[]{:S(2)}) copy-start(bf16[1024,256]{1,0:T(8,128)(2,1)S(1)} %collective-permute-done.1.refs_1_) | copy-start | bytes 1572868
  60.0 16.7 %collective-permute-start.2 = (bf16[1024,256]{1,0:T(8,128)(2,1)S(1)}, bf16[1024,256]{1,0:T(8,128)(2,1)S(1)}, u32[]{:S(2)}, u32[]{:S(2)}) collective-permute-start(bf16[1024,256]{1,0:T(8,128)(2,1)S(1)} %collective-permute-done.1.refs_1_), channel_id=1, source_target_pairs={{0,1},{1,2},{2,3},{3,4},{4,5},{5,6},{6,7},{7,0},{8,9},{9,10},{10,1... | collective-permute-start | bytes 1572872 | tf_op jit(solution)/shard_map/ppermute | solution.py:347
  61.9 59.3 %copy-start.6 = (bf16[1024,256]{1,0:T(8,128)(2,1)}, bf16[1024,256]{1,0:T(8,128)(2,1)S(1)}, u32[]{:S(2)}) copy-start(bf16[1024,256]{1,0:T(8,128)(2,1)S(1)} %collective-permute-done.5.refs_7_) | copy-start | bytes 1572868
  62.0 16.6 %collective-permute-start.6 = (bf16[1024,256]{1,0:T(8,128)(2,1)S(1)}, bf16[1024,256]{1,0:T(8,128)(2,1)S(1)}, u32[]{:S(2)}, u32[]{:S(2)}) collective-permute-start(bf16[1024,256]{1,0:T(8,128)(2,1)S(1)} %collective-permute-done.5.refs_7_), channel_id=1, source_target_pairs={{0,7},{1,0},{2,1},{3,2},{4,3},{5,4},{6,5},{7,6},{8,15},{9,8},{10,9... | collective-permute-start | bytes 1572872 | tf_op jit(solution)/shard_map/ppermute | solution.py:350
  76.7 44.6 %copy-start.7 = (bf16[1024,256]{1,0:T(8,128)(2,1)}, bf16[1024,256]{1,0:T(8,128)(2,1)S(1)}, u32[]{:S(2)}) copy-start(bf16[1024,256]{1,0:T(8,128)(2,1)S(1)} %collective-permute-done.2.refs_2_) | copy-start | bytes 1572868
  76.7 15.8 %collective-permute-start.3 = (bf16[1024,256]{1,0:T(8,128)(2,1)S(1)}, bf16[1024,256]{1,0:T(8,128)(2,1)S(1)}, u32[]{:S(2)}, u32[]{:S(2)}) collective-permute-start(bf16[1024,256]{1,0:T(8,128)(2,1)S(1)} %collective-permute-done.2.refs_2_), channel_id=1, source_target_pairs={{0,1},{1,2},{2,3},{3,4},{4,5},{5,6},{6,7},{7,0},{8,9},{9,10},{10,1... | collective-permute-start | bytes 1572872 | tf_op jit(solution)/shard_map/ppermute | solution.py:347
  78.6 42.7 %copy-start.8 = (bf16[1024,256]{1,0:T(8,128)(2,1)}, bf16[1024,256]{1,0:T(8,128)(2,1)S(1)}, u32[]{:S(2)}) copy-start(bf16[1024,256]{1,0:T(8,128)(2,1)S(1)} %collective-permute-done.6.refs_6_) | copy-start | bytes 1572868
  78.6 44.0 %collective-permute-start.7 = (bf16[1024,256]{1,0:T(8,128)(2,1)S(1)}, bf16[1024,256]{1,0:T(8,128)(2,1)}, u32[]{:S(2)}, u32[]{:S(2)}) collective-permute-start(bf16[1024,256]{1,0:T(8,128)(2,1)S(1)} %collective-permute-done.6.refs_6_), channel_id=1, source_target_pairs={{0,7},{1,0},{2,1},{3,2},{4,3},{5,4},{6,5},{7,6},{8,15},{9,8},{10,9... | collective-permute-start | bytes 1572872 | tf_op jit(solution)/shard_map/ppermute | solution.py:350
  92.5 28.8 %copy-start.9 = (bf16[1024,256]{1,0:T(8,128)(2,1)}, bf16[1024,256]{1,0:T(8,128)(2,1)S(1)}, u32[]{:S(2)}) copy-start(bf16[1024,256]{1,0:T(8,128)(2,1)S(1)} %collective-permute-done.3.refs_3_) | copy-start | bytes 1572868
  92.5 30.2 %collective-permute-start.4 = (bf16[1024,256]{1,0:T(8,128)(2,1)S(1)}, bf16[1024,256]{1,0:T(8,128)(2,1)}, u32[]{:S(2)}, u32[]{:S(2)}) collective-permute-start(bf16[1024,256]{1,0:T(8,128)(2,1)S(1)} %collective-permute-done.3.refs_3_), channel_id=1, source_target_pairs={{0,1},{1,2},{2,3},{3,4},{4,5},{5,6},{6,7},{7,0},{8,9},{9,10},{10,1... | collective-permute-start | bytes 1572872 | tf_op jit(solution)/shard_map/ppermute | solution.py:347
  119.6 1.5 copy-start.4
  121.3 1.3 copy-start
  142.0 4.6 %collective-permute-start.8 = (bf16[32,56,256]{2,1,0:T(8,128)(2,1)}, bf16[32,56,256]{2,1,0:T(8,128)(2,1)S(1)}, u32[]{:S(2)}, u32[]{:S(2)}) collective-permute-start(bf16[32,56,256]{2,1,0:T(8,128)(2,1)} %get-tuple-element.39), channel_id=1, source_target_pairs={{0,8},{8,0},{1,9},{9,1},{2,10},{10,2},{3,11},{11,3},{4,12},{12,4},... | collective-permute-start | bytes 2752520 | tf_op jit(solution)/shard_map/ppermute | solution.py:357
  181.2 14.8 %collective-permute-start.9 = (f32[50,256]{1,0:T(8,128)S(1)}, f32[50,256]{1,0:T(8,128)S(1)}, u32[]{:S(2)}, u32[]{:S(2)}) collective-permute-start(f32[50,256]{1,0:T(8,128)S(1)} %slice_multiply_fusion), channel_id=1, source_target_pairs={{0,0},{1,64},{2,128},{3,192},{4,256},{5,320},{6,384},{7,448},{64,1... | collective-permute-start | bytes 153608 | tf_op jit(solution)/shard_map/ppermute | solution.py:361
Sparse Core Ops, SparseCore 0:
  23.5 96.0 all-gather.3
  131.9 53.4 reduce-scatter.1

commit v5 on v4

--- a/solution.py
+++ b/solution.py
@@ -361,7 +361,7 @@
     weight_gradient = lax.ppermute(summed, ("z", "y"), swap)
 
     head_gradient = backward(head_inputs, probs, att, out_grad)
-    return head_gradient, weight_gradient
+    return lax.optimization_barrier((head_gradient, weight_gradient))
 
 
 def solution(mesh):

time: 213 us -> 205 us (0.962)
  the two profiles are of different devices: /device:TPU:34 before, /device:TPU:1 now
where the time goes in v5:
time: 205 us
  waiting for transfers between devices  62.3 us (30%)
  starting transfers between devices  49.2 us (24%)
  Pallas kernels  40.1 us (20%)
  blocking collectives  31.5 us (15%)
  between operations  14.3 us (7%)
  local copies, waits for them, and re-layouts  4.9 us (2%)
  other arithmetic  2.52 us (1%)
    all_to_all x1, blocking collectives, per_device(): spread = lax.all_to_all(both, ('z', 'x'), 0, 0, tiled=True)  31.5 us
    all_gather x1, waiting for transfers between devices, per_device(): weight = assemble(lax.all_gather(weight, SHARDS, axis=0))  27.2 us
    ppermute x4, waiting for transfers between devices, per_device(): back.append(lax.ppermute(back[-1], 'y', ring(8, 1)))  26.5 us
    all_to_all x1, starting transfers between devices, per_device(): arrived = lax.all_to_all(outgoing, SHARDS, 0, 0, tiled=True)  23.3 us
    ppermute x3, starting transfers between devices, per_device(): ahead.append(lax.ppermute(ahead[-1], 'y', ring(8, -1)))  12.3 us
    pallas_call x1, Pallas kernels, weight_parts(): pl.pallas_call(weight_kernel, out_shape=(jax.ShapeDtypeStruct((32, GSEND,...  9.57 us
    ppermute x4, starting transfers between devices, per_device(): back.append(lax.ppermute(back[-1], 'y', ring(8, 1)))  9.19 us
    pallas_call x1, Pallas kernels, receive(): pl.pallas_call(receive_kernel, grid=(2,), out_shape=(jax.ShapeDtypeStruct...  9.09 us
  transfers between devices with their start and end apart: 13, of which 6 were waited for; matrix products, arithmetic and copies ran while one was open for 1% of the time, Pallas kernels for 15%

profile of v5, /device:TPU:1, one launch (start us, length us, event | category | flops | bytes accessed | tf_op | source)
XLA Modules:
  0.0 204.7 jit_solution(8311914225294618683)
XLA Ops:
  7.2 1.4 collective-permute-start
  8.6 5.1 %pack_pieces.1 = bf16[64,16,1664]{2,1,0:T(8,128)(2,1)} custom-call(s32[1,32]{1,0:T(1,128)} %label_ref.1, bf16[4,400,512]{2,1,0:T(8,128)(2,1)} %bitcast.6), custom_call_target="tpu_custom_call" | custom-call | tf_op jit(solution)/shard_map/pack_pieces/pallas_call | solution.py:78
  13.7 0.6 copy-done.10
  14.3 23.3 %all-to-all-start = ((bf16[64,16,1664]{2,1,0:T(8,128)(2,1)}), bf16[64,16,1664]{2,1,0:T(8,128)(2,1)}, u32[]{:S(2)}, u32[]{:S(2)}) async-start(bf16[64,16,1664]{2,1,0:T(8,128)(2,1)} %pack_pieces.1), calls=%async_computation | async-start | bytes 6815744 | tf_op jit(solution)/shard_map/all_to_all | solution.py:342
  37.7 7.8 %attend.1 = (bf16[2,1040,1152]{2,1,0:T(8,128)(2,1)}, bf16[1152,256]{1,0:T(8,128)(2,1)S(1)}, bf16[1024,256]{1,0:T(8,128)(2,1)S(1)}) custom-call(bf16[1,3,1025,256]{3,2,1,0:T(8,128)(2,1)S(1)} %copy-done.1), custom_call_target="tpu_custom_call" | custom-call | flops 2000000000 | bytes 8000000 | tf_op jit(solution)/shard_map/attend/pallas_call | solution.py:210
  45.6 0.8 copy-done.2
  46.4 3.2 %collective-permute-start.1 = (bf16[1024,256]{1,0:T(8,128)(2,1)S(1)}, bf16[1024,256]{1,0:T(8,128)(2,1)S(1)}, u32[]{:S(2)}, u32[]{:S(2)}) collective-permute-start(bf16[1024,256]{1,0:T(8,128)(2,1)S(1)} %get-tuple-element.30.refs_0_), channel_id=1, source_target_pairs={{0,1},{1,2},{2,3},{3,4},{4,5},{5,6},{6,7},{7,0},{8,9},{9,10},{10,1... | collective-permute-start | bytes 1572872 | tf_op jit(solution)/shard_map/ppermute | solution.py:347
  49.6 3.3 %collective-permute-start.5 = (bf16[1024,256]{1,0:T(8,128)(2,1)S(1)}, bf16[1024,256]{1,0:T(8,128)(2,1)S(1)}, u32[]{:S(2)}, u32[]{:S(2)}) collective-permute-start(bf16[1024,256]{1,0:T(8,128)(2,1)S(1)} %get-tuple-element.30.refs_0_), channel_id=1, source_target_pairs={{0,7},{1,0},{2,1},{3,2},{4,3},{5,4},{6,5},{7,6},{8,15},{9,8},{10,9... | collective-permute-start | bytes 1572872 | tf_op jit(solution)/shard_map/ppermute | solution.py:350
  52.9 9.7 %collective-permute-done.1.refs_1_ = bf16[1024,256]{1,0:T(8,128)(2,1)S(1)} collective-permute-done((bf16[1024,256]{1,0:T(8,128)(2,1)S(1)}, bf16[1024,256]{1,0:T(8,128)(2,1)S(1)}, u32[]{:S(2)}, u32[]{:S(2)}) %collective-permute-start.1) | collective-permute-done | bytes 524320 | tf_op jit(solution)/shard_map/ppermute | solution.py:347
  62.5 2.0 collective-permute-start.2
  64.6 4.5 %collective-permute-start.6 = (bf16[1024,256]{1,0:T(8,128)(2,1)S(1)}, bf16[1024,256]{1,0:T(8,128)(2,1)S(1)}, u32[]{:S(2)}, u32[]{:S(2)}) collective-permute-start(bf16[1024,256]{1,0:T(8,128)(2,1)S(1)} %collective-permute-done.5.refs_7_), channel_id=1, source_target_pairs={{0,7},{1,0},{2,1},{3,2},{4,3},{5,4},{6,5},{7,6},{8,15},{9,8},{10,9... | collective-permute-start | bytes 1572872 | tf_op jit(solution)/shard_map/ppermute | solution.py:350
  69.1 8.8 %collective-permute-done.2.refs_2_ = bf16[1024,256]{1,0:T(8,128)(2,1)S(1)} collective-permute-done((bf16[1024,256]{1,0:T(8,128)(2,1)S(1)}, bf16[1024,256]{1,0:T(8,128)(2,1)S(1)}, u32[]{:S(2)}, u32[]{:S(2)}) %collective-permute-start.2) | collective-permute-done | bytes 524320 | tf_op jit(solution)/shard_map/ppermute | solution.py:347
  77.9 1.9 collective-permute-start.3
  79.8 4.6 %collective-permute-start.7 = (bf16[1024,256]{1,0:T(8,128)(2,1)S(1)}, bf16[1024,256]{1,0:T(8,128)(2,1)}, u32[]{:S(2)}, u32[]{:S(2)}) collective-permute-start(bf16[1024,256]{1,0:T(8,128)(2,1)S(1)} %collective-permute-done.6.refs_6_), channel_id=1, source_target_pairs={{0,7},{1,0},{2,1},{3,2},{4,3},{5,4},{6,5},{7,6},{8,15},{9,8},{10,9... | collective-permute-start | bytes 1572872 | tf_op jit(solution)/shard_map/ppermute | solution.py:350
  84.4 8.0 %collective-permute-done.3.refs_3_ = bf16[1024,256]{1,0:T(8,128)(2,1)S(1)} collective-permute-done((bf16[1024,256]{1,0:T(8,128)(2,1)S(1)}, bf16[1024,256]{1,0:T(8,128)(2,1)S(1)}, u32[]{:S(2)}, u32[]{:S(2)}) %collective-permute-start.3) | collective-permute-done | bytes 524320 | tf_op jit(solution)/shard_map/ppermute | solution.py:347
  92.4 2.1 %collective-permute-start.4 = (bf16[1024,256]{1,0:T(8,128)(2,1)S(1)}, bf16[1024,256]{1,0:T(8,128)(2,1)}, u32[]{:S(2)}, u32[]{:S(2)}) collective-permute-start(bf16[1024,256]{1,0:T(8,128)(2,1)S(1)} %collective-permute-done.3.refs_3_), channel_id=1, source_target_pairs={{0,1},{1,2},{2,3},{3,4},{4,5},{5,6},{6,7},{7,0},{8,9},{9,10},{10,1... | collective-permute-start | bytes 1572872 | tf_op jit(solution)/shard_map/ppermute | solution.py:347
  94.5 27.2 %all-gather.4.cloned.1.call-done.in_ref = bf16[64,50,256]{2,1,0:T(8,128)(2,1)} async-done(((bf16[1,50,256]{2,1,0:T(8,128)(2,1)}), bf16[64,50,256]{2,1,0:T(8,128)(2,1)}) %all-gather.4.cloned.1.call-update) | async-done | bytes 1638416 | tf_op jit(solution)/shard_map/all_gather | solution.py:341
  121.7 1.5 copy-done.4
  123.2 0.2 assemble_weight.1.weight_ref
  123.4 1.3 copy-done
  124.8 9.1 %receive_pieces.1 = (bf16[1024,512]{1,0:T(8,128)(2,1)}, bf16[8,1024,256]{2,1,0:T(8,128)(2,1)}) custom-call(bf16[1024,1664]{1,0:T(8,128)(2,1)} %bitcast.1.in_ref, bf16[8,512,256]{2,1,0:T(8,128)(2,1)} %copy-done), custom_call_target="tpu_custom_call" | custom-call | tf_op jit(solution)/shard_map/receive_pieces/pallas_call | solution.py:153
  133.9 0.6 pad_add_fusion.place_ref
  134.5 9.6 %weight_parts.1 = (f32[32,56,256]{2,1,0:T(8,128)}, bf16[32,56,256]{2,1,0:T(8,128)(2,1)}) custom-call(s32[2]{0:T(128)} %pad_add_fusion.place_ref, bf16[1024,512]{1,0:T(8,128)(2,1)} %get-tuple-element.29.r_ref, bf16[1024,256]{1,0:T(8,128)(2,1)} %copy-done.3, bf16[1024,256]{1,0:T(8,128)(2,1)} %copy-done.5, bf16[1024,256]{1,0:T(8,128)(2,1)} %copy-done.7, ...), custom_call_target="tpu_custom_call" | custom-call | tf_op jit(solution)/shard_map/weight_parts/pallas_call | solution.py:311
  144.1 2.1 %collective-permute-start.8 = (bf16[32,56,256]{2,1,0:T(8,128)(2,1)}, bf16[32,56,256]{2,1,0:T(8,128)(2,1)S(1)}, u32[]{:S(2)}, u32[]{:S(2)}) collective-permute-start(bf16[32,56,256]{2,1,0:T(8,128)(2,1)} %get-tuple-element.39), channel_id=1, source_target_pairs={{0,8},{8,0},{1,9},{9,1},{2,10},{10,2},{3,11},{11,3},{4,12},{12,4},... | collective-permute-start | bytes 2752520 | tf_op jit(solution)/shard_map/ppermute | solution.py:357
  146.2 2.4 %collective-permute-done.8 = bf16[32,56,256]{2,1,0:T(8,128)(2,1)S(1)} collective-permute-done((bf16[32,56,256]{2,1,0:T(8,128)(2,1)}, bf16[32,56,256]{2,1,0:T(8,128)(2,1)S(1)}, u32[]{:S(2)}, u32[]{:S(2)}) %collective-permute-start.8) | collective-permute-done | bytes 917536 | tf_op jit(solution)/shard_map/ppermute | solution.py:357
  148.7 1.8 add_convert_fusion
  150.4 31.5 %all_to_all.10 = bf16[32,56,256]{2,1,0:T(8,128)(2,1)S(1)} all-to-all(bf16[32,56,256]{2,1,0:T(8,128)(2,1)S(1)} %add_convert_fusion), channel_id=1, replica_groups=mesh['z'=8,'x'=4,'c'=2,'y'=8] {'z','x'}, dimensions={0} | all-to-all | bytes 1835008 | tf_op jit(solution)/shard_map/all_to_all | solution.py:359
  181.9 0.1 convert_reduce_fusion
  182.0 0.7 collective-permute-start.9
  182.7 6.1 %reduce-scatter.2.cloned.1.call-done = bf16[1,1024,256]{2,1,0:T(8,128)(2,1)} async-done(((bf16[8,1024,256]{2,1,0:T(8,128)(2,1)}), bf16[1,1024,256]{2,1,0:T(8,128)(2,1)}) %reduce-scatter.2.cloned.1.call-update) | async-done | bytes 524304 | tf_op jit(solution)/shard_map/reduce_scatter | solution.py:354
  188.8 8.4 %attend_backward.1 = bf16[1,3,1025,256]{3,2,1,0:T(8,128)(2,1)} custom-call(bf16[1,3,1025,256]{3,2,1,0:T(8,128)(2,1)} %x_ref.1, bf16[2,1040,1152]{2,1,0:T(8,128)(2,1)} %get-tuple-element.22.p_ref, bf16[1152,256]{1,0:T(8,128)(2,1)} %copy-done.2, bf16[1024,256]{1,0:T(8,128)(2,1)} %bitcast.7), custom_call_target="tpu_custom_call" | custom-call | tf_op jit(solution)/shard_map/attend_backward/pallas_call | solution.py:269
  197.2 0.6 copy.7
  (30 shorter events, 0.2 us)
Async XLA Ops:
  7.2 114.5 %all-gather.4.cloned.1.call-start = ((), (), s32[]{:S(2)}) async-start(), calls=%async_computation.4 | async-start | bytes 1863680 | tf_op jit(solution)/shard_map/all_gather | solution.py:341
  7.2 6.5 %collective-permute-start = (bf16[50,256]{1,0:T(8,128)(2,1)}, bf16[50,256]{1,0:T(8,128)(2,1)S(1)}, u32[]{:S(2)}, u32[]{:S(2)}) collective-permute-start(bf16[50,256]{1,0:T(8,128)(2,1)} %param.5), channel_id=1, source_target_pairs={{0,0},{1,64},{2,128},{3,192},{4,256},{5,320},{6,384},{7,448},{64,1... | collective-permute-start | bytes 76808 | tf_op jit(solution)/shard_map/ppermute | solution.py:337
  13.7 0.6 copy-start.10
  14.3 23.4 %copy-start.1 = (bf16[1,3,1025,256]{3,2,1,0:T(8,128)(2,1)S(1)}, bf16[1,3,1025,256]{3,2,1,0:T(8,128)(2,1)}, u32[]{:S(2)}) copy-start(bf16[1,3,1025,256]{3,2,1,0:T(8,128)(2,1)} %x_ref.1) | copy-start | bytes 4723204
  14.3 110.5 %all-to-all-start = ((bf16[64,16,1664]{2,1,0:T(8,128)(2,1)}), bf16[64,16,1664]{2,1,0:T(8,128)(2,1)}, u32[]{:S(2)}, u32[]{:S(2)}) async-start(bf16[64,16,1664]{2,1,0:T(8,128)(2,1)} %pack_pieces.1), calls=%async_computation | async-start | bytes 6815744 | tf_op jit(solution)/shard_map/all_to_all | solution.py:342
  37.7 151.2 %reduce-scatter.2.cloned.1.call-start = ((), (), s32[]{:S(2)}) async-start(), calls=%async_computation.3 | async-start | bytes 4718592 | tf_op jit(solution)/shard_map/reduce_scatter | solution.py:354
  45.6 0.8 copy-start.2
  46.4 77.0 %copy-start.3 = (bf16[1024,256]{1,0:T(8,128)(2,1)}, bf16[1024,256]{1,0:T(8,128)(2,1)S(1)}, u32[]{:S(2)}) copy-start(bf16[1024,256]{1,0:T(8,128)(2,1)S(1)} %get-tuple-element.30.refs_0_) | copy-start | bytes 1572868
  46.4 16.2 %collective-permute-start.1 = (bf16[1024,256]{1,0:T(8,128)(2,1)S(1)}, bf16[1024,256]{1,0:T(8,128)(2,1)S(1)}, u32[]{:S(2)}, u32[]{:S(2)}) collective-permute-start(bf16[1024,256]{1,0:T(8,128)(2,1)S(1)} %get-tuple-element.30.refs_0_), channel_id=1, source_target_pairs={{0,1},{1,2},{2,3},{3,4},{4,5},{5,6},{6,7},{7,0},{8,9},{9,10},{10,1... | collective-permute-start | bytes 1572872 | tf_op jit(solution)/shard_map/ppermute | solution.py:347
  49.6 15.0 %collective-permute-start.5 = (bf16[1024,256]{1,0:T(8,128)(2,1)S(1)}, bf16[1024,256]{1,0:T(8,128)(2,1)S(1)}, u32[]{:S(2)}, u32[]{:S(2)}) collective-permute-start(bf16[1024,256]{1,0:T(8,128)(2,1)S(1)} %get-tuple-element.30.refs_0_), channel_id=1, source_target_pairs={{0,7},{1,0},{2,1},{3,2},{4,3},{5,4},{6,5},{7,6},{8,15},{9,8},{10,9... | collective-permute-start | bytes 1572872 | tf_op jit(solution)/shard_map/ppermute | solution.py:350
  62.5 60.8 %copy-start.5 = (bf16[1024,256]{1,0:T(8,128)(2,1)}, bf16[1024,256]{1,0:T(8,128)(2,1)S(1)}, u32[]{:S(2)}) copy-start(bf16[1024,256]{1,0:T(8,128)(2,1)S(1)} %collective-permute-done.1.refs_1_) | copy-start | bytes 1572868
  62.5 15.4 %collective-permute-start.2 = (bf16[1024,256]{1,0:T(8,128)(2,1)S(1)}, bf16[1024,256]{1,0:T(8,128)(2,1)S(1)}, u32[]{:S(2)}, u32[]{:S(2)}) collective-permute-start(bf16[1024,256]{1,0:T(8,128)(2,1)S(1)} %collective-permute-done.1.refs_1_), channel_id=1, source_target_pairs={{0,1},{1,2},{2,3},{3,4},{4,5},{5,6},{6,7},{7,0},{8,9},{9,10},{10,1... | collective-permute-start | bytes 1572872 | tf_op jit(solution)/shard_map/ppermute | solution.py:347
  64.6 58.8 %copy-start.6 = (bf16[1024,256]{1,0:T(8,128)(2,1)}, bf16[1024,256]{1,0:T(8,128)(2,1)S(1)}, u32[]{:S(2)}) copy-start(bf16[1024,256]{1,0:T(8,128)(2,1)S(1)} %collective-permute-done.5.refs_7_) | copy-start | bytes 1572868
  64.6 15.3 %collective-permute-start.6 = (bf16[1024,256]{1,0:T(8,128)(2,1)S(1)}, bf16[1024,256]{1,0:T(8,128)(2,1)S(1)}, u32[]{:S(2)}, u32[]{:S(2)}) collective-permute-start(bf16[1024,256]{1,0:T(8,128)(2,1)S(1)} %collective-permute-done.5.refs_7_), channel_id=1, source_target_pairs={{0,7},{1,0},{2,1},{3,2},{4,3},{5,4},{6,5},{7,6},{8,15},{9,8},{10,9... | collective-permute-start | bytes 1572872 | tf_op jit(solution)/shard_map/ppermute | solution.py:350
  77.9 45.5 %copy-start.7 = (bf16[1024,256]{1,0:T(8,128)(2,1)}, bf16[1024,256]{1,0:T(8,128)(2,1)S(1)}, u32[]{:S(2)}) copy-start(bf16[1024,256]{1,0:T(8,128)(2,1)S(1)} %collective-permute-done.2.refs_2_) | copy-start | bytes 1572868
  77.9 14.5 %collective-permute-start.3 = (bf16[1024,256]{1,0:T(8,128)(2,1)S(1)}, bf16[1024,256]{1,0:T(8,128)(2,1)S(1)}, u32[]{:S(2)}, u32[]{:S(2)}) collective-permute-start(bf16[1024,256]{1,0:T(8,128)(2,1)S(1)} %collective-permute-done.2.refs_2_), channel_id=1, source_target_pairs={{0,1},{1,2},{2,3},{3,4},{4,5},{5,6},{6,7},{7,0},{8,9},{9,10},{10,1... | collective-permute-start | bytes 1572872 | tf_op jit(solution)/shard_map/ppermute | solution.py:347
  79.8 43.6 %copy-start.8 = (bf16[1024,256]{1,0:T(8,128)(2,1)}, bf16[1024,256]{1,0:T(8,128)(2,1)S(1)}, u32[]{:S(2)}) copy-start(bf16[1024,256]{1,0:T(8,128)(2,1)S(1)} %collective-permute-done.6.refs_6_) | copy-start | bytes 1572868
  79.8 44.9 %collective-permute-start.7 = (bf16[1024,256]{1,0:T(8,128)(2,1)S(1)}, bf16[1024,256]{1,0:T(8,128)(2,1)}, u32[]{:S(2)}, u32[]{:S(2)}) collective-permute-start(bf16[1024,256]{1,0:T(8,128)(2,1)S(1)} %collective-permute-done.6.refs_6_), channel_id=1, source_target_pairs={{0,7},{1,0},{2,1},{3,2},{4,3},{5,4},{6,5},{7,6},{8,15},{9,8},{10,9... | collective-permute-start | bytes 1572872 | tf_op jit(solution)/shard_map/ppermute | solution.py:350
  92.4 31.0 %copy-start.9 = (bf16[1024,256]{1,0:T(8,128)(2,1)}, bf16[1024,256]{1,0:T(8,128)(2,1)S(1)}, u32[]{:S(2)}) copy-start(bf16[1024,256]{1,0:T(8,128)(2,1)S(1)} %collective-permute-done.3.refs_3_) | copy-start | bytes 1572868
  92.4 32.3 %collective-permute-start.4 = (bf16[1024,256]{1,0:T(8,128)(2,1)S(1)}, bf16[1024,256]{1,0:T(8,128)(2,1)}, u32[]{:S(2)}, u32[]{:S(2)}) collective-permute-start(bf16[1024,256]{1,0:T(8,128)(2,1)S(1)} %collective-permute-done.3.refs_3_), channel_id=1, source_target_pairs={{0,1},{1,2},{2,3},{3,4},{4,5},{5,6},{6,7},{7,0},{8,9},{9,10},{10,1... | collective-permute-start | bytes 1572872 | tf_op jit(solution)/shard_map/ppermute | solution.py:347
  121.7 1.5 copy-start.4
  123.4 1.3 copy-start
  144.1 4.6 %collective-permute-start.8 = (bf16[32,56,256]{2,1,0:T(8,128)(2,1)}, bf16[32,56,256]{2,1,0:T(8,128)(2,1)S(1)}, u32[]{:S(2)}, u32[]{:S(2)}) collective-permute-start(bf16[32,56,256]{2,1,0:T(8,128)(2,1)} %get-tuple-element.39), channel_id=1, source_target_pairs={{0,8},{8,0},{1,9},{9,1},{2,10},{10,2},{3,11},{11,3},{4,12},{12,4},... | collective-permute-start | bytes 2752520 | tf_op jit(solution)/shard_map/ppermute | solution.py:357
  182.0 15.2 %collective-permute-start.9 = (f32[50,256]{1,0:T(8,128)S(1)}, f32[50,256]{1,0:T(8,128)S(1)}, u32[]{:S(2)}, u32[]{:S(2)}) collective-permute-start(f32[50,256]{1,0:T(8,128)S(1)} %slice_multiply_fusion), channel_id=1, source_target_pairs={{0,0},{1,64},{2,128},{3,192},{4,256},{5,320},{6,384},{7,448},{64,1... | collective-permute-start | bytes 153608 | tf_op jit(solution)/shard_map/ppermute | solution.py:361
Sparse Core Ops, SparseCore 0:
  14.4 107.2 all-gather.3
  134.0 54.7 reduce-scatter.1

commit v6 on v5

--- a/solution.py
+++ b/solution.py
@@ -104,7 +104,7 @@
         out_shape=jax.ShapeDtypeStruct((8, 8 * GPAD, 256), BF),
         in_specs=[vmem],
         out_specs=vmem,
-        compiler_params=params(24),
+        compiler_params=params(60),
         cost_estimate=pl.CostEstimate(flops=48 * 10**9, bytes_accessed=4 * 10**6, transcendentals=0),
         name="assemble_weight",
     )(arrived)

time: 205 us -> 207 us (level)
  local copies, waits for them, and re-layouts: 4.9 us -> 2.06 us
  Pallas kernels: 40.1 us -> 42.9 us
    unnamed x23 -> x19, local copies, waits for them, and re-layouts: 4.9 us -> 2.06 us
    pallas_call x1, Pallas kernels: 0.15 us -> 2.99 us  [assemble(): pl.pallas_call(assemble_kernel, out_shape=jax.ShapeDtypeStruct((8, 8 * GP...]
  transfers between devices with their start and end apart: 13 -> 13, of which waited for: 6 -> 6; matrix products, arithmetic and copies ran while one was open for 1% -> 1% of each run, Pallas kernels for 15% -> 17%
where the time goes in v6:
time: 207 us; the launch traced here: 205 us
  waiting for transfers between devices  61.7 us (30%)
  starting transfers between devices  49.2 us (24%)
  Pallas kernels  42.9 us (21%)
  blocking collectives  32.3 us (16%)
  between operations  14.2 us (7%)
  other arithmetic  2.46 us (1%)
    all_to_all x1, blocking collectives, per_device(): spread = lax.all_to_all(both, ('z', 'x'), 0, 0, tiled=True)  32.3 us
    all_gather x1, waiting for transfers between devices, per_device(): weight = assemble(lax.all_gather(weight, SHARDS, axis=0))  26.9 us
    ppermute x4, waiting for transfers between devices, per_device(): back.append(lax.ppermute(back[-1], 'y', ring(8, 1)))  26.5 us
    all_to_all x1, starting transfers between devices, per_device(): arrived = lax.all_to_all(outgoing, SHARDS, 0, 0, tiled=True)  23.3 us
    ppermute x3, starting transfers between devices, per_device(): ahead.append(lax.ppermute(ahead[-1], 'y', ring(8, -1)))  12.3 us
    pallas_call x1, Pallas kernels, weight_parts(): pl.pallas_call(weight_kernel, out_shape=(jax.ShapeDtypeStruct((32, GSEND,...  9.58 us
    ppermute x4, starting transfers between devices, per_device(): back.append(lax.ppermute(back[-1], 'y', ring(8, 1)))  9.19 us
    pallas_call x1, Pallas kernels, receive(): pl.pallas_call(receive_kernel, grid=(2,), out_shape=(jax.ShapeDtypeStruct...  9.08 us
  transfers between devices with their start and end apart: 13, of which 6 were waited for; matrix products, arithmetic and copies ran while one was open for 1% of the time, Pallas kernels for 17%

profile of v6, /device:TPU:1, one launch (start us, length us, event | category | flops | bytes accessed | tf_op | source)
XLA Modules:
  0.0 204.9 jit_solution(11519406854237654128)
XLA Ops:
  7.2 0.0 all-gather.4.cloned.1.call-start
  7.2 1.4 collective-permute-start
  8.6 5.0 %pack_pieces.1 = bf16[64,16,1664]{2,1,0:T(8,128)(2,1)} custom-call(s32[1,32]{1,0:T(1,128)} %label_ref.1, bf16[4,400,512]{2,1,0:T(8,128)(2,1)} %bitcast.6), custom_call_target="tpu_custom_call" | custom-call | tf_op jit(solution)/shard_map/pack_pieces/pallas_call | solution.py:78
  13.7 0.6 copy-done.8
  14.3 23.3 %all-to-all-start = ((bf16[64,16,1664]{2,1,0:T(8,128)(2,1)}), bf16[64,16,1664]{2,1,0:T(8,128)(2,1)}, u32[]{:S(2)}, u32[]{:S(2)}) async-start(bf16[64,16,1664]{2,1,0:T(8,128)(2,1)} %pack_pieces.1), calls=%async_computation | async-start | bytes 6815744 | tf_op jit(solution)/shard_map/all_to_all | solution.py:342
  37.7 0.0 reduce-scatter.2.cloned.1.call-start
  37.7 7.8 %attend.1 = (bf16[2,1040,1152]{2,1,0:T(8,128)(2,1)}, bf16[1152,256]{1,0:T(8,128)(2,1)S(1)}, bf16[1024,256]{1,0:T(8,128)(2,1)S(1)}) custom-call(bf16[1,3,1025,256]{3,2,1,0:T(8,128)(2,1)S(1)} %copy-done), custom_call_target="tpu_custom_call" | custom-call | flops 2000000000 | bytes 8000000 | tf_op jit(solution)/shard_map/attend/pallas_call | solution.py:210
  45.6 0.8 copy-done.1
  46.4 3.2 %collective-permute-start.1 = (bf16[1024,256]{1,0:T(8,128)(2,1)S(1)}, bf16[1024,256]{1,0:T(8,128)(2,1)S(1)}, u32[]{:S(2)}, u32[]{:S(2)}) collective-permute-start(bf16[1024,256]{1,0:T(8,128)(2,1)S(1)} %get-tuple-element.30.refs_0_), channel_id=1, source_target_pairs={{0,1},{1,2},{2,3},{3,4},{4,5},{5,6},{6,7},{7,0},{8,9},{9,10},{10,1... | collective-permute-start | bytes 1572872 | tf_op jit(solution)/shard_map/ppermute | solution.py:347
  49.6 3.3 %collective-permute-start.5 = (bf16[1024,256]{1,0:T(8,128)(2,1)S(1)}, bf16[1024,256]{1,0:T(8,128)(2,1)S(1)}, u32[]{:S(2)}, u32[]{:S(2)}) collective-permute-start(bf16[1024,256]{1,0:T(8,128)(2,1)S(1)} %get-tuple-element.30.refs_0_), channel_id=1, source_target_pairs={{0,7},{1,0},{2,1},{3,2},{4,3},{5,4},{6,5},{7,6},{8,15},{9,8},{10,9... | collective-permute-start | bytes 1572872 | tf_op jit(solution)/shard_map/ppermute | solution.py:350
  52.9 9.7 %collective-permute-done.1.refs_1_ = bf16[1024,256]{1,0:T(8,128)(2,1)S(1)} collective-permute-done((bf16[1024,256]{1,0:T(8,128)(2,1)S(1)}, bf16[1024,256]{1,0:T(8,128)(2,1)S(1)}, u32[]{:S(2)}, u32[]{:S(2)}) %collective-permute-start.1) | collective-permute-done | bytes 524320 | tf_op jit(solution)/shard_map/ppermute | solution.py:347
  62.5 2.0 collective-permute-start.2
  64.6 4.5 %collective-permute-start.6 = (bf16[1024,256]{1,0:T(8,128)(2,1)S(1)}, bf16[1024,256]{1,0:T(8,128)(2,1)S(1)}, u32[]{:S(2)}, u32[]{:S(2)}) collective-permute-start(bf16[1024,256]{1,0:T(8,128)(2,1)S(1)} %collective-permute-done.5.refs_7_), channel_id=1, source_target_pairs={{0,7},{1,0},{2,1},{3,2},{4,3},{5,4},{6,5},{7,6},{8,15},{9,8},{10,9... | collective-permute-start | bytes 1572872 | tf_op jit(solution)/shard_map/ppermute | solution.py:350
  69.0 8.8 %collective-permute-done.2.refs_2_ = bf16[1024,256]{1,0:T(8,128)(2,1)S(1)} collective-permute-done((bf16[1024,256]{1,0:T(8,128)(2,1)S(1)}, bf16[1024,256]{1,0:T(8,128)(2,1)S(1)}, u32[]{:S(2)}, u32[]{:S(2)}) %collective-permute-start.2) | collective-permute-done | bytes 524320 | tf_op jit(solution)/shard_map/ppermute | solution.py:347
  77.9 1.9 collective-permute-start.3
  79.8 4.6 %collective-permute-start.7 = (bf16[1024,256]{1,0:T(8,128)(2,1)S(1)}, bf16[1024,256]{1,0:T(8,128)(2,1)}, u32[]{:S(2)}, u32[]{:S(2)}) collective-permute-start(bf16[1024,256]{1,0:T(8,128)(2,1)S(1)} %collective-permute-done.6.refs_6_), channel_id=1, source_target_pairs={{0,7},{1,0},{2,1},{3,2},{4,3},{5,4},{6,5},{7,6},{8,15},{9,8},{10,9... | collective-permute-start | bytes 1572872 | tf_op jit(solution)/shard_map/ppermute | solution.py:350
  84.4 8.0 %collective-permute-done.3.refs_3_ = bf16[1024,256]{1,0:T(8,128)(2,1)S(1)} collective-permute-done((bf16[1024,256]{1,0:T(8,128)(2,1)S(1)}, bf16[1024,256]{1,0:T(8,128)(2,1)S(1)}, u32[]{:S(2)}, u32[]{:S(2)}) %collective-permute-start.3) | collective-permute-done | bytes 524320 | tf_op jit(solution)/shard_map/ppermute | solution.py:347
  92.4 2.1 %collective-permute-start.4 = (bf16[1024,256]{1,0:T(8,128)(2,1)S(1)}, bf16[1024,256]{1,0:T(8,128)(2,1)}, u32[]{:S(2)}, u32[]{:S(2)}) collective-permute-start(bf16[1024,256]{1,0:T(8,128)(2,1)S(1)} %collective-permute-done.3.refs_3_), channel_id=1, source_target_pairs={{0,1},{1,2},{2,3},{3,4},{4,5},{5,6},{6,7},{7,0},{8,9},{9,10},{10,1... | collective-permute-start | bytes 1572872 | tf_op jit(solution)/shard_map/ppermute | solution.py:347
  94.5 26.9 %all-gather.4.cloned.1.call-done.in_ref = bf16[64,50,256]{2,1,0:T(8,128)(2,1)} async-done(((bf16[1,50,256]{2,1,0:T(8,128)(2,1)}), bf16[64,50,256]{2,1,0:T(8,128)(2,1)}) %all-gather.4.cloned.1.call-update) | async-done | bytes 1638416 | tf_op jit(solution)/shard_map/all_gather | solution.py:341
  121.4 3.0 %assemble_weight.1.weight_ref = bf16[8,512,256]{2,1,0:T(8,128)(2,1)} custom-call(bf16[64,50,256]{2,1,0:T(8,128)(2,1)} %all-gather.4.cloned.1.call-done.in_ref), custom_call_target="tpu_custom_call" | custom-call | flops 48000000000 | bytes 4000000 | tf_op jit(solution)/shard_map/assemble_weight/pallas_call | solution.py:102
  124.5 9.1 %receive_pieces.1 = (bf16[1024,512]{1,0:T(8,128)(2,1)}, bf16[8,1024,256]{2,1,0:T(8,128)(2,1)}) custom-call(bf16[1024,1664]{1,0:T(8,128)(2,1)} %bitcast.1.in_ref, bf16[8,512,256]{2,1,0:T(8,128)(2,1)} %assemble_weight.1.weight_ref), custom_call_target="tpu_custom_call" | custom-call | tf_op jit(solution)/shard_map/receive_pieces/pallas_call | solution.py:153
  133.6 0.6 pad_add_fusion.place_ref
  134.1 9.6 %weight_parts.1 = (f32[32,56,256]{2,1,0:T(8,128)}, bf16[32,56,256]{2,1,0:T(8,128)(2,1)}) custom-call(s32[2]{0:T(128)} %pad_add_fusion.place_ref, bf16[1024,512]{1,0:T(8,128)(2,1)} %get-tuple-element.29.r_ref, bf16[1024,256]{1,0:T(8,128)(2,1)} %copy-done.2, bf16[1024,256]{1,0:T(8,128)(2,1)} %copy-done.3, bf16[1024,256]{1,0:T(8,128)(2,1)} %copy-done.5, ...), custom_call_target="tpu_custom_call" | custom-call | tf_op jit(solution)/shard_map/weight_parts/pallas_call | solution.py:311
  143.7 2.2 %collective-permute-start.8 = (bf16[32,56,256]{2,1,0:T(8,128)(2,1)}, bf16[32,56,256]{2,1,0:T(8,128)(2,1)S(1)}, u32[]{:S(2)}, u32[]{:S(2)}) collective-permute-start(bf16[32,56,256]{2,1,0:T(8,128)(2,1)} %get-tuple-element.39), channel_id=1, source_target_pairs={{0,8},{8,0},{1,9},{9,1},{2,10},{10,2},{3,11},{11,3},{4,12},{12,4},... | collective-permute-start | bytes 2752520 | tf_op jit(solution)/shard_map/ppermute | solution.py:357
  145.9 2.4 %collective-permute-done.8 = bf16[32,56,256]{2,1,0:T(8,128)(2,1)S(1)} collective-permute-done((bf16[32,56,256]{2,1,0:T(8,128)(2,1)}, bf16[32,56,256]{2,1,0:T(8,128)(2,1)S(1)}, u32[]{:S(2)}, u32[]{:S(2)}) %collective-permute-start.8) | collective-permute-done | bytes 917536 | tf_op jit(solution)/shard_map/ppermute | solution.py:357
  148.3 1.8 add_convert_fusion
  150.0 32.3 %all_to_all.10 = bf16[32,56,256]{2,1,0:T(8,128)(2,1)S(1)} all-to-all(bf16[32,56,256]{2,1,0:T(8,128)(2,1)S(1)} %add_convert_fusion), channel_id=1, replica_groups=mesh['z'=8,'x'=4,'c'=2,'y'=8] {'z','x'}, dimensions={0} | all-to-all | bytes 1835008 | tf_op jit(solution)/shard_map/all_to_all | solution.py:359
  182.3 0.1 convert_reduce_fusion
  182.5 0.7 collective-permute-start.9
  183.2 5.8 %reduce-scatter.2.cloned.1.call-done = bf16[1,1024,256]{2,1,0:T(8,128)(2,1)} async-done(((bf16[8,1024,256]{2,1,0:T(8,128)(2,1)}), bf16[1,1024,256]{2,1,0:T(8,128)(2,1)}) %reduce-scatter.2.cloned.1.call-update) | async-done | bytes 524304 | tf_op jit(solution)/shard_map/reduce_scatter | solution.py:354
  189.0 8.4 %attend_backward.1 = bf16[1,3,1025,256]{3,2,1,0:T(8,128)(2,1)} custom-call(bf16[1,3,1025,256]{3,2,1,0:T(8,128)(2,1)} %x_ref.1, bf16[2,1040,1152]{2,1,0:T(8,128)(2,1)} %get-tuple-element.22.p_ref, bf16[1152,256]{1,0:T(8,128)(2,1)} %copy-done.1, bf16[1024,256]{1,0:T(8,128)(2,1)} %bitcast.7), custom_call_target="tpu_custom_call" | custom-call | tf_op jit(solution)/shard_map/attend_backward/pallas_call | solution.py:269
  197.4 0.6 copy.7
  (26 shorter events, 0.1 us)
Async XLA Ops:
  7.2 114.2 %all-gather.4.cloned.1.call-start = ((), (), s32[]{:S(2)}) async-start(), calls=%async_computation.4 | async-start | bytes 1863680 | tf_op jit(solution)/shard_map/all_gather | solution.py:341
  7.2 6.5 %collective-permute-start = (bf16[50,256]{1,0:T(8,128)(2,1)}, bf16[50,256]{1,0:T(8,128)(2,1)S(1)}, u32[]{:S(2)}, u32[]{:S(2)}) collective-permute-start(bf16[50,256]{1,0:T(8,128)(2,1)} %param.5), channel_id=1, source_target_pairs={{0,0},{1,64},{2,128},{3,192},{4,256},{5,320},{6,384},{7,448},{64,1... | collective-permute-start | bytes 76808 | tf_op jit(solution)/shard_map/ppermute | solution.py:337
  13.7 0.6 copy-start.8
  14.3 23.4 %copy-start = (bf16[1,3,1025,256]{3,2,1,0:T(8,128)(2,1)S(1)}, bf16[1,3,1025,256]{3,2,1,0:T(8,128)(2,1)}, u32[]{:S(2)}) copy-start(bf16[1,3,1025,256]{3,2,1,0:T(8,128)(2,1)} %x_ref.1) | copy-start | bytes 4723204
  14.3 110.1 %all-to-all-start = ((bf16[64,16,1664]{2,1,0:T(8,128)(2,1)}), bf16[64,16,1664]{2,1,0:T(8,128)(2,1)}, u32[]{:S(2)}, u32[]{:S(2)}) async-start(bf16[64,16,1664]{2,1,0:T(8,128)(2,1)} %pack_pieces.1), calls=%async_computation | async-start | bytes 6815744 | tf_op jit(solution)/shard_map/all_to_all | solution.py:342
  37.7 151.3 %reduce-scatter.2.cloned.1.call-start = ((), (), s32[]{:S(2)}) async-start(), calls=%async_computation.3 | async-start | bytes 4718592 | tf_op jit(solution)/shard_map/reduce_scatter | solution.py:354
  45.6 0.8 copy-start.1
  46.4 78.0 %copy-start.2 = (bf16[1024,256]{1,0:T(8,128)(2,1)}, bf16[1024,256]{1,0:T(8,128)(2,1)S(1)}, u32[]{:S(2)}) copy-start(bf16[1024,256]{1,0:T(8,128)(2,1)S(1)} %get-tuple-element.30.refs_0_) | copy-start | bytes 1572868
  46.4 16.2 %collective-permute-start.1 = (bf16[1024,256]{1,0:T(8,128)(2,1)S(1)}, bf16[1024,256]{1,0:T(8,128)(2,1)S(1)}, u32[]{:S(2)}, u32[]{:S(2)}) collective-permute-start(bf16[1024,256]{1,0:T(8,128)(2,1)S(1)} %get-tuple-element.30.refs_0_), channel_id=1, source_target_pairs={{0,1},{1,2},{2,3},{3,4},{4,5},{5,6},{6,7},{7,0},{8,9},{9,10},{10,1... | collective-permute-start | bytes 1572872 | tf_op jit(solution)/shard_map/ppermute | solution.py:347
  49.6 15.0 %collective-permute-start.5 = (bf16[1024,256]{1,0:T(8,128)(2,1)S(1)}, bf16[1024,256]{1,0:T(8,128)(2,1)S(1)}, u32[]{:S(2)}, u32[]{:S(2)}) collective-permute-start(bf16[1024,256]{1,0:T(8,128)(2,1)S(1)} %get-tuple-element.30.refs_0_), channel_id=1, source_target_pairs={{0,7},{1,0},{2,1},{3,2},{4,3},{5,4},{6,5},{7,6},{8,15},{9,8},{10,9... | collective-permute-start | bytes 1572872 | tf_op jit(solution)/shard_map/ppermute | solution.py:350
  62.5 61.9 %copy-start.3 = (bf16[1024,256]{1,0:T(8,128)(2,1)}, bf16[1024,256]{1,0:T(8,128)(2,1)S(1)}, u32[]{:S(2)}) copy-start(bf16[1024,256]{1,0:T(8,128)(2,1)S(1)} %collective-permute-done.1.refs_1_) | copy-start | bytes 1572868
  62.5 15.4 %collective-permute-start.2 = (bf16[1024,256]{1,0:T(8,128)(2,1)S(1)}, bf16[1024,256]{1,0:T(8,128)(2,1)S(1)}, u32[]{:S(2)}, u32[]{:S(2)}) collective-permute-start(bf16[1024,256]{1,0:T(8,128)(2,1)S(1)} %collective-permute-done.1.refs_1_), channel_id=1, source_target_pairs={{0,1},{1,2},{2,3},{3,4},{4,5},{5,6},{6,7},{7,0},{8,9},{9,10},{10,1... | collective-permute-start | bytes 1572872 | tf_op jit(solution)/shard_map/ppermute | solution.py:347
  64.5 59.8 %copy-start.4 = (bf16[1024,256]{1,0:T(8,128)(2,1)}, bf16[1024,256]{1,0:T(8,128)(2,1)S(1)}, u32[]{:S(2)}) copy-start(bf16[1024,256]{1,0:T(8,128)(2,1)S(1)} %collective-permute-done.5.refs_7_) | copy-start | bytes 1572868
  64.6 15.3 %collective-permute-start.6 = (bf16[1024,256]{1,0:T(8,128)(2,1)S(1)}, bf16[1024,256]{1,0:T(8,128)(2,1)S(1)}, u32[]{:S(2)}, u32[]{:S(2)}) collective-permute-start(bf16[1024,256]{1,0:T(8,128)(2,1)S(1)} %collective-permute-done.5.refs_7_), channel_id=1, source_target_pairs={{0,7},{1,0},{2,1},{3,2},{4,3},{5,4},{6,5},{7,6},{8,15},{9,8},{10,9... | collective-permute-start | bytes 1572872 | tf_op jit(solution)/shard_map/ppermute | solution.py:350
  77.9 46.5 %copy-start.5 = (bf16[1024,256]{1,0:T(8,128)(2,1)}, bf16[1024,256]{1,0:T(8,128)(2,1)S(1)}, u32[]{:S(2)}) copy-start(bf16[1024,256]{1,0:T(8,128)(2,1)S(1)} %collective-permute-done.2.refs_2_) | copy-start | bytes 1572868
  77.9 14.5 %collective-permute-start.3 = (bf16[1024,256]{1,0:T(8,128)(2,1)S(1)}, bf16[1024,256]{1,0:T(8,128)(2,1)S(1)}, u32[]{:S(2)}, u32[]{:S(2)}) collective-permute-start(bf16[1024,256]{1,0:T(8,128)(2,1)S(1)} %collective-permute-done.2.refs_2_), channel_id=1, source_target_pairs={{0,1},{1,2},{2,3},{3,4},{4,5},{5,6},{6,7},{7,0},{8,9},{9,10},{10,1... | collective-permute-start | bytes 1572872 | tf_op jit(solution)/shard_map/ppermute | solution.py:347
  79.8 44.6 %copy-start.6 = (bf16[1024,256]{1,0:T(8,128)(2,1)}, bf16[1024,256]{1,0:T(8,128)(2,1)S(1)}, u32[]{:S(2)}) copy-start(bf16[1024,256]{1,0:T(8,128)(2,1)S(1)} %collective-permute-done.6.refs_6_) | copy-start | bytes 1572868
  79.8 44.6 %collective-permute-start.7 = (bf16[1024,256]{1,0:T(8,128)(2,1)S(1)}, bf16[1024,256]{1,0:T(8,128)(2,1)}, u32[]{:S(2)}, u32[]{:S(2)}) collective-permute-start(bf16[1024,256]{1,0:T(8,128)(2,1)S(1)} %collective-permute-done.6.refs_6_), channel_id=1, source_target_pairs={{0,7},{1,0},{2,1},{3,2},{4,3},{5,4},{6,5},{7,6},{8,15},{9,8},{10,9... | collective-permute-start | bytes 1572872 | tf_op jit(solution)/shard_map/ppermute | solution.py:350
  92.4 32.0 %copy-start.7 = (bf16[1024,256]{1,0:T(8,128)(2,1)}, bf16[1024,256]{1,0:T(8,128)(2,1)S(1)}, u32[]{:S(2)}) copy-start(bf16[1024,256]{1,0:T(8,128)(2,1)S(1)} %collective-permute-done.3.refs_3_) | copy-start | bytes 1572868
  92.4 32.0 %collective-permute-start.4 = (bf16[1024,256]{1,0:T(8,128)(2,1)S(1)}, bf16[1024,256]{1,0:T(8,128)(2,1)}, u32[]{:S(2)}, u32[]{:S(2)}) collective-permute-start(bf16[1024,256]{1,0:T(8,128)(2,1)S(1)} %collective-permute-done.3.refs_3_), channel_id=1, source_target_pairs={{0,1},{1,2},{2,3},{3,4},{4,5},{5,6},{6,7},{7,0},{8,9},{9,10},{10,1... | collective-permute-start | bytes 1572872 | tf_op jit(solution)/shard_map/ppermute | solution.py:347
  143.7 4.6 %collective-permute-start.8 = (bf16[32,56,256]{2,1,0:T(8,128)(2,1)}, bf16[32,56,256]{2,1,0:T(8,128)(2,1)S(1)}, u32[]{:S(2)}, u32[]{:S(2)}) collective-permute-start(bf16[32,56,256]{2,1,0:T(8,128)(2,1)} %get-tuple-element.39), channel_id=1, source_target_pairs={{0,8},{8,0},{1,9},{9,1},{2,10},{10,2},{3,11},{11,3},{4,12},{12,4},... | collective-permute-start | bytes 2752520 | tf_op jit(solution)/shard_map/ppermute | solution.py:357
  182.5 14.9 %collective-permute-start.9 = (f32[50,256]{1,0:T(8,128)S(1)}, f32[50,256]{1,0:T(8,128)S(1)}, u32[]{:S(2)}, u32[]{:S(2)}) collective-permute-start(f32[50,256]{1,0:T(8,128)S(1)} %slice_multiply_fusion), channel_id=1, source_target_pairs={{0,0},{1,64},{2,128},{3,192},{4,256},{5,320},{6,384},{7,448},{64,1... | collective-permute-start | bytes 153608 | tf_op jit(solution)/shard_map/ppermute | solution.py:361
Sparse Core Ops, SparseCore 0:
  14.4 106.9 all-gather.3
  133.7 55.2 reduce-scatter.1
